TPU v7x, 32 devices: a whole 2x2x4 slice. The times are simulated.
32 devices in a mesh: groups: 1, ep: 16 (over z, y, x), etp: 2 (over core).
Axes of the slice: x: 2, y: 2, z: 4, core: 2. Of those that a mesh axis runs over, the one named last changes fastest.
Arguments:
- tokens: bfloat16 [2048, 4096], P(('groups', 'ep', 'etp')), may hold values from -6 to 6
- expert_ids: int32 [2048, 8], P(('groups', 'ep', 'etp')), may hold values from 0 to 15, all different within a row; in each aligned block of 64 rows (0 to 63, 64 to 127, ...) at most 40 rows name the same one
- route_weights: float32 [2048, 8], P(('groups', 'ep', 'etp')), may hold values from 0.1 to 1
- gate_proj: bfloat16 [16, 4096, 768], P('ep', None, 'etp'), may hold values from -0.09375 to 0.09375
- up_proj: bfloat16 [16, 4096, 768], P('ep', None, 'etp'), may hold values from -0.09375 to 0.09375
- down_proj: bfloat16 [16, 768, 4096], P('ep', 'etp'), may hold values from -0.21875 to 0.21875
Outputs:
- mixed: bfloat16 [2048, 4096], P(('groups', 'ep', 'etp'))
Inputs may be any that keep to these rules, and one draw needn't show every extreme that they name: `expert_ids`: each row names 8 different experts. Within the 64 rows of one device no expert is named by more than 40 rows, and on some device some expert is named by exactly 40 rows.
All inputs are finite; a program needn't handle non-finite values.
Results may differ from a plain program's by a relative error of at most 0.0058.
Values may be sent and summed in bfloat16 or wider, within the bound.
No kernel may reach another device: no remote copies, remote signals or barrier semaphores. Data moves between devices by JAX's collectives and lax.ppermute only.
A program may use at most 128 MiB of HBM per device.

v0:
```python
import jax
import jax.numpy as jnp
from jax import lax
from jax.sharding import PartitionSpec as P


def on_device(tokens, expert_ids, route_weights, gate_proj, up_proj, down_proj):
    tok_rows, width = tokens.shape
    top_count = expert_ids.shape[1]
    experts = lax.axis_size("ep") * gate_proj.shape[0]
    capacity = max(2, min(tok_rows, tok_rows * top_count * 5 // (4 * experts)))
    flat_ids = expert_ids.reshape(-1)
    onehot = (flat_ids[:, None] == jnp.arange(experts, dtype=jnp.int32)[None, :]).astype(jnp.int32)
    ranks = jnp.cumsum(onehot, axis=0) - onehot
    slots = jnp.sum(ranks * onehot, axis=1)
    target = flat_ids * capacity + slots
    owner = jnp.arange(tok_rows * top_count, dtype=jnp.int32) // top_count
    outgoing = jnp.zeros((experts * capacity, width), jnp.bfloat16).at[target].set(tokens[owner])
    outgoing = outgoing.reshape(experts, capacity, width)
    w_gate = gate_proj[0]
    w_up = up_proj[0]
    w_down = down_proj[0]
    received = lax.all_to_all(outgoing, "ep", split_axis=0, concat_axis=0, tiled=True)
    senders, taken, _ = received.shape
    rows = received.reshape(senders * taken, width)
    piece = lax.all_gather(rows, "etp", axis=0, tiled=True)
    gate = jnp.dot(piece, w_gate, preferred_element_type=jnp.float32)
    upper = jnp.dot(piece, w_up, preferred_element_type=jnp.float32)
    hidden = (jax.nn.silu(gate) * upper).astype(jnp.bfloat16)
    result = lax.psum_scatter(
        jnp.dot(hidden, w_down, preferred_element_type=jnp.float32),
        "etp",
        scatter_dimension=0,
        tiled=True,
    )
    back = result.astype(jnp.bfloat16).reshape(senders, taken, width)
    returned = lax.all_to_all(back, "ep", split_axis=0, concat_axis=0, tiled=True)
    picked = returned.reshape(experts * capacity, width)[target]
    picked = picked.reshape(tok_rows, top_count, width).astype(jnp.float32)
    mixed = jnp.sum(route_weights[:, :, None] * picked, axis=1)
    return mixed.astype(jnp.bfloat16)


def solution(mesh):
    in_specs = (
        P(("groups", "ep", "etp"), None),
        P(("groups", "ep", "etp"), None),
        P(("groups", "ep", "etp"), None),
        P("ep", None, "etp"),
        P("ep", None, "etp"),
        P("ep", "etp", None),
    )
    out_specs = P(("groups", "ep", "etp"), None)
    return jax.shard_map(
        on_device, mesh=mesh, in_specs=in_specs, out_specs=out_specs, check_vma=False
    )
```

profile of v0, /device:TPU:14, one launch (start us, length us, event | category | flops | bytes accessed | tf_op | source)
XLA Modules:
  0.0 395.5 jit_solution(609076464001162175)
XLA Ops:
  6.5 0.0 copy-start
  6.5 0.0 all-gather.2.cloned.1.call-start
  6.5 0.9 copy.10
  7.5 0.1 eq.29
  7.6 0.1 eq.25
  7.6 0.7 broadcast_multiply_fusion
  8.4 1.2 reduce-window.6
  9.5 0.2 slice_reduce_fusion
  9.8 0.1 copy.9
  9.9 0.1 mul.37
  10.0 0.1 fusion.22
  10.1 21.0 %scatter_custom_fusion = bf16[640,4096]{1,0:T(8,128)(2,1)} fusion(s32[512]{0:T(512)S(1)} %bitcast.47, bf16[64,4096]{1,0:T(8,128)(2,1)} %param.6, s32[1024]{0:T(1024)S(1)} %pad_clamp_fusion.1, bf16[]{:T(256)} %constant.26.clone.1), kind=kCustom, calls=%fused_computation.5 | custom fusion | bytes 5243392 | tf_op jit(solution)/shard_map/scatter | solution.py:18
  31.0 121.4 %all_to_all.10 = bf16[16,40,4096]{2,1,0:T(8,128)(2,1)} all-to-all(bf16[16,40,4096]{2,1,0:T(8,128)(2,1)} %bitcast.45), channel_id=1, replica_groups=mesh['groups'=1,'ep'=16,'etp'=2] {'ep'}, dimensions={0} | all-to-all | bytes 10485760 | tf_op jit(solution)/shard_map/all_to_all | solution.py:23
  152.4 0.0 all-gather.2.cloned.1.call-update
  152.5 0.0 reduce-scatter.2.cloned.1.call-start
  152.5 23.2 %all-gather.2.cloned.1.call-done = bf16[1280,4096]{1,0:T(8,128)(2,1)} async-done(((bf16[640,4096]{1,0:T(8,128)(2,1)}), bf16[1280,4096]{1,0:T(8,128)(2,1)}) %all-gather.2.cloned.1.call-update) | async-done | bytes 10485776 | tf_op jit(solution)/shard_map/all_gather | solution.py:26
  175.7 10.2 %fusion.6 = f32[1280,384]{1,0:T(8,128)} fusion(bf16[1280,4096]{1,0:T(8,128)(2,1)} %all-gather.2.cloned.1.call-done, bf16[1,4096,384]{2,1,0:T(8,128)(2,1)} %param.9), kind=kOutput, calls=%fused_computation.11 | convolution fusion | flops 4026531840 | bytes 15597568 | tf_op jit(solution)/shard_map/dot_general | solution.py:27
  185.9 0.0 copy-done
  185.9 18.8 %fusion.3 = f32[1280,4096]{1,0:T(8,128)} fusion(bf16[1,384,4096]{2,1,0:T(8,128)(2,1)S(1)} %copy-done, bf16[1280,4096]{1,0:T(8,128)(2,1)} %all-gather.2.cloned.1.call-done, bf16[1,4096,384]{2,1,0:T(8,128)(2,1)} %param.10, f32[1280,384]{1,0:T(8,128)} %fusion.6), kind=kOutput, calls=%fused_computation.8 | convolution fusion | flops 8056012800 | bytes 39714816 | tf_op jit(solution)/shard_map/dot_general | solution.py:31
  204.7 0.0 reduce-scatter.2.cloned.1.call-update
  204.7 32.1 %reduce-scatter.2.cloned.1.call-done = f32[640,4096]{1,0:T(8,128)} async-done(((f32[1280,4096]{1,0:T(8,128)}), f32[640,4096]{1,0:T(8,128)}) %reduce-scatter.2.cloned.1.call-update) | async-done | bytes 10485776 | tf_op jit(solution)/shard_map/reduce_scatter | solution.py:30
  236.8 7.1 %convert_element_type.25 = bf16[640,4096]{1,0:T(8,128)(2,1)} convert(f32[640,4096]{1,0:T(8,128)} %reduce-scatter.2.cloned.1.call-done) | non-fusion elementwise | flops 2621440 | bytes 15728640 | tf_op jit(solution)/shard_map/convert_element_type | solution.py:36
  243.9 0.0 copy-start.2
  243.9 7.1 %all-to-all-start.1 = ((bf16[16,40,4096]{2,1,0:T(8,128)(2,1)}), bf16[16,40,4096]{2,1,0:T(8,128)(2,1)}, u32[]{:S(2)}, u32[]{:S(2)}) async-start(bf16[16,40,4096]{2,1,0:T(8,128)(2,1)} %bitcast.46), calls=%async_computation.2 | async-start | bytes 10485760 | tf_op jit(solution)/shard_map/all_to_all | solution.py:37
  251.0 0.0 copy-done.2
  251.0 0.1 copy.8
  251.1 119.2 %all-to-all-done.1 = bf16[16,40,4096]{2,1,0:T(8,128)(2,1)} async-done(((bf16[16,40,4096]{2,1,0:T(8,128)(2,1)}), bf16[16,40,4096]{2,1,0:T(8,128)(2,1)}, u32[]{:S(2)}, u32[]{:S(2)}) %all-to-all-start.1) | async-done | bytes 5242912 | tf_op jit(solution)/shard_map/all_to_all | solution.py:37
  370.3 0.0 copy-start.1
  370.3 12.0 %gather_fusion = bf16[512,4096]{1,0:T(8,128)(2,1)} fusion(bf16[640,4096]{1,0:T(8,128)(2,1)} %bitcast.10, s32[1024]{0:T(1024)S(1)} %pad_clamp_fusion), kind=kCustom, calls=%fused_computation.1 | custom fusion | bytes 8390656 | tf_op jit(solution)/shard_map/gather | solution.py:38
  382.2 6.5 %fusion = bf16[64,4096]{1,0:T(8,128)(2,1)} fusion(bf16[512,4096]{1,0:T(8,128)(2,1)} %gather_fusion, f32[64,8]{1,0:T(8,128)S(1)} %copy.8), kind=kLoop, calls=%fused_computation.4 | loop fusion | flops 6029312 | bytes 4720640 | tf_op jit(solution)/shard_map/reduce_sum | solution.py:40
  388.7 0.0 copy-done.1
  (7 shorter events, 0.1 us)
Async XLA Ops:
  6.5 179.3 %copy-start = (bf16[1,384,4096]{2,1,0:T(8,128)(2,1)S(1)}, bf16[1,384,4096]{2,1,0:T(8,128)(2,1)}, u32[]{:S(2)}) copy-start(bf16[1,384,4096]{2,1,0:T(8,128)(2,1)} %param.11) | copy-start | bytes 9437188
  6.5 169.2 %all-gather.2.cloned.1.call-start = ((), (), s32[]{:S(2)}) async-start(), calls=%async_computation.3 | async-start | bytes 15728640 | tf_op jit(solution)/shard_map/all_gather | solution.py:26
  152.5 84.3 %reduce-scatter.2.cloned.1.call-start = ((), (), s32[]{:S(2)}) async-start(), calls=%async_computation.4 | async-start | bytes 31457280 | tf_op jit(solution)/shard_map/reduce_scatter | solution.py:30
  243.9 7.1 %copy-start.2 = (f32[64,8]{0,1:T(8,128)S(1)}, f32[64,8]{0,1:T(8,128)}, u32[]{:S(2)}) copy-start(f32[64,8]{0,1:T(8,128)} %param.8) | copy-start | bytes 6148
  243.9 126.4 %all-to-all-start.1 = ((bf16[16,40,4096]{2,1,0:T(8,128)(2,1)}), bf16[16,40,4096]{2,1,0:T(8,128)(2,1)}, u32[]{:S(2)}, u32[]{:S(2)}) async-start(bf16[16,40,4096]{2,1,0:T(8,128)(2,1)} %bitcast.46), calls=%async_computation.2 | async-start | bytes 10485760 | tf_op jit(solution)/shard_map/all_to_all | solution.py:37
  370.3 18.4 %copy-start.1 = (bf16[1,384,4096]{2,1,0:T(8,128)(2,1)S(1)}, bf16[1,384,4096]{2,1,0:T(8,128)(2,1)}, u32[]{:S(2)}) copy-start(bf16[1,384,4096]{2,1,0:T(8,128)(2,1)} %param.11) | copy-start | bytes 9437188
Sparse Core Ops, SparseCore 0:
  152.6 23.0 all-gather.1
  204.8 31.9 reduce-scatter.1
where the time goes:
time: 396 us
  waiting for transfers between devices  174 us (44%)
  blocking collectives  121 us (31%)
  local copies, waits for them, and re-layouts  34.5 us (9%)
  matrix products  29 us (7%)
  other arithmetic  15.6 us (4%)
  between operations  13.4 us (3%)
  starting transfers between devices  7.13 us (2%)
    all_to_all x1, blocking collectives, on_device(): lax.all_to_all(outgoing, 'ep', split_axis=0, concat_axis=0, tiled=True)  121 us
    all_to_all x1, waiting for transfers between devices, on_device(): lax.all_to_all(back, 'ep', split_axis=0, concat_axis=0, tiled=True)  119 us
    reduce_scatter x1, waiting for transfers between devices, on_device(): lax.psum_scatter(jnp.dot(hidden, w_down, preferred_element_type=jnp.float...  32.1 us
    all_gather x1, waiting for transfers between devices, on_device(): piece = lax.all_gather(rows, 'etp', axis=0, tiled=True)  23.2 us
    scatter x1, local copies, waits for them, and re-layouts, on_device(): jnp.zeros((experts * capacity, width), jnp.bfloat16).at[target]  21 us
    dot_general x1, matrix products, on_device(): jnp.dot(hidden, w_down, preferred_element_type=jnp.float32)  18.8 us
    gather x1, local copies, waits for them, and re-layouts, on_device(): picked = returned.reshape(experts * capacity, width)[target]  12 us
    dot_general x1, matrix products, on_device(): gate = jnp.dot(piece, w_gate, preferred_element_type=jnp.float32)  10.2 us
  transfers between devices with their start and end apart: 3, of which 3 were waited for; matrix products, arithmetic and copies ran while one was open for 0% of the time, Pallas kernels for 0%

commit v1 on v0

v1 whole, which is shorter than its diff:
```python
import jax
import jax.numpy as jnp
from jax import lax
from jax.sharding import PartitionSpec as P

BF = jnp.bfloat16
F32 = jnp.float32


def on_device(tokens, expert_ids, route_weights, gate_proj, up_proj, down_proj):
    rows, width = tokens.shape
    n_ep = lax.axis_size("ep")
    ring = n_ep // 4
    me = lax.axis_index("ep")
    core = lax.axis_index("etp")
    axes = ("ep", "etp")

    def swap(x):
        return lax.ppermute(x, "etp", [(0, 1), (1, 0)])

    pairs_a = [(2 * i + c, 2 * (i ^ (1, 2)[c]) + c) for i in range(n_ep) for c in range(2)]
    pairs_b = [(2 * i + c, 2 * (i ^ (2, 1)[c]) + c) for i in range(n_ep) for c in range(2)]
    pairs_z = [(i, (i + 4) % n_ep) for i in range(n_ep)]

    def hop_a(x):
        return lax.ppermute(x, axes, pairs_a)

    def hop_b(x):
        return lax.ppermute(x, axes, pairs_b)

    def hop_z(x):
        return lax.ppermute(x, "ep", pairs_z)

    experts = jnp.arange(n_ep, dtype=jnp.int32)
    named = expert_ids[:, :, None] == experts[None, None, :]
    dense = jnp.sum(jnp.where(named, route_weights[:, :, None], 0.0), axis=1)
    everyone = lax.all_gather(dense, "ep", axis=0)
    mine = lax.dynamic_index_in_dim(everyone, me, axis=2, keepdims=False)
    flip_a = jnp.where(core == 0, 1, 2)
    flip_b = 3 - flip_a
    plane = me % 4
    level = me // 4

    groups = []
    block = tokens
    for k in range(ring):
        if k:
            block = hop_z(block)
        a = hop_a(block)
        groups.append((block, a, hop_b(block), hop_b(a)))
    w_gate = jnp.concatenate([gate_proj[0], swap(gate_proj[0])], axis=1)
    w_up = jnp.concatenate([up_proj[0], swap(up_proj[0])], axis=1)
    w_down = jnp.concatenate([down_proj[0], swap(down_proj[0])], axis=0)

    def partial_of(k):
        x = jnp.concatenate(groups[k], axis=0)
        base = ((level - k) % ring) * 4
        source = jnp.stack([base + plane, base + (plane ^ flip_a), base + (plane ^ flip_b), base + (plane ^ 3)])
        scale = mine[source].reshape(4 * rows, 1)
        gate = jnp.dot(x, w_gate, preferred_element_type=F32)
        upper = jnp.dot(x, w_up, preferred_element_type=F32)
        hidden = (jax.nn.silu(gate) * upper).astype(BF)
        result = jnp.dot(hidden, w_down, preferred_element_type=F32)
        return (result * scale).astype(BF).reshape(4, rows, width)

    def add(*terms):
        total = terms[0].astype(F32)
        for term in terms[1:]:
            total = total + term.astype(F32)
        return total.astype(BF)

    carry = None
    for k in list(range(1, ring)) + [0]:
        p = partial_of(k)
        got_b2 = hop_b(p[3])
        got_b1 = hop_b(p[2])
        got_a = hop_a(add(p[1], got_b2))
        terms = [p[0], got_b1, got_a]
        if carry is not None:
            terms.append(hop_z(carry))
        carry = add(*terms)
    return carry


def solution(mesh):
    in_specs = (
        P(("groups", "ep", "etp"), None),
        P(("groups", "ep", "etp"), None),
        P(("groups", "ep", "etp"), None),
        P("ep", None, "etp"),
        P("ep", None, "etp"),
        P("ep", "etp", None),
    )
    out_specs = P(("groups", "ep", "etp"), None)
    return jax.shard_map(
        on_device, mesh=mesh, in_specs=in_specs, out_specs=out_specs, check_vma=False
    )
```

time: 396 us -> 270 us (0.68)
  blocking collectives: 121 us -> 35.5 us
  waiting for transfers between devices: 174 us -> 110 us
  matrix products: 29 us -> 63.2 us
  starting transfers between devices: 7.13 us -> 38.1 us
  local copies, waits for them, and re-layouts: 34.5 us -> 12.2 us
  between operations: 13.4 us -> 0.39 us
  other arithmetic: 15.6 us -> 7.11 us
    all_to_all x1 -> x0, blocking collectives: 121 us -> none  [on_device(): lax.all_to_all(outgoing, 'ep', split_axis=0, concat_axis=0, tiled=True)]
    all_to_all x1 -> x0, waiting for transfers between devices: 119 us -> none  [on_device(): lax.all_to_all(back, 'ep', split_axis=0, concat_axis=0, tiled=True)]
    ppermute x0 -> x33, waiting for transfers between devices: none -> 110 us  [the longest x6 49.4 us: hop_z(): return lax.ppermute(x, 'ep', pairs_z)]
    ppermute x0 -> x33, starting transfers between devices: none -> 38.1 us  [the longest x16 24.4 us: hop_b(): return lax.ppermute(x, axes, pairs_b)]
    all_gather x0 -> x1, blocking collectives: none -> 35.5 us  [on_device(): everyone = lax.all_gather(dense, 'ep', axis=0)]
    dot_general x2 -> x8, matrix products: 29 us -> 63.2 us  [the longest x4 40.1 us: partial_of(): result = jnp.dot(hidden, w_down, preferred_element_type=F32)]
    reduce_scatter x1 -> x0, waiting for transfers between devices: 32.1 us -> none  [on_device(): lax.psum_scatter(jnp.dot(hidden, w_down, preferred_element_type=jnp.float...]
    all_gather x1 -> x0, waiting for transfers between devices: 23.2 us -> none  [on_device(): piece = lax.all_gather(rows, 'etp', axis=0, tiled=True)]
  transfers between devices with their start and end apart: 3 -> 33, of which waited for: 3 -> 15; matrix products, arithmetic and copies ran while one was open for 0% -> 26% of each run, Pallas kernels for 0% -> 0%
where the time goes in v1:
time: 270 us; the launch traced here: 266 us
  waiting for transfers between devices  110 us (41%)
  matrix products  63.2 us (23%)
  starting transfers between devices  38.1 us (14%)
  blocking collectives  35.5 us (13%)
  local copies, waits for them, and re-layouts  12.2 us (5%)
  other arithmetic  7.11 us (3%)
    ppermute x6, waiting for transfers between devices, hop_z(): return lax.ppermute(x, 'ep', pairs_z)  49.4 us
    dot_general x4, matrix products, partial_of(): result = jnp.dot(hidden, w_down, preferred_element_type=F32)  40.1 us
    all_gather x1, blocking collectives, on_device(): everyone = lax.all_gather(dense, 'ep', axis=0)  35.5 us
    ppermute x8, waiting for transfers between devices, hop_a(): return lax.ppermute(x, axes, pairs_a)  33.9 us
    ppermute x16, waiting for transfers between devices, hop_b(): return lax.ppermute(x, axes, pairs_b)  26.2 us
    ppermute x16, starting transfers between devices, hop_b(): return lax.ppermute(x, axes, pairs_b)  24.4 us
    dot_general x4, matrix products, partial_of(): gate = jnp.dot(x, w_gate, preferred_element_type=F32)  23.1 us
    ppermute x8, starting transfers between devices, hop_a(): return lax.ppermute(x, axes, pairs_a)  9.99 us
  transfers between devices with their start and end apart: 33, of which 15 were waited for; matrix products, arithmetic and copies ran while one was open for 26% of the time, Pallas kernels for 0%

profile of v1, /device:TPU:14, one launch (start us, length us, event | category | flops | bytes accessed | tf_op | source)
XLA Modules:
  0.0 266.0 jit_solution(7098554510306558402)
XLA Ops:
  3.9 35.5 %all-gather.1 = f32[16,64,16]{1,2,0:T(8,128)S(1)} all-gather(f32[1,64,16]{1,2,0:T(8,128)S(1)} %bitcast.41), channel_id=2, replica_groups=mesh['groups'=1,'ep'=16,'etp'=2] {'ep'}, dimensions={0}, use_global_device_ids=true | all-gather | bytes 69632 | tf_op jit(solution)/shard_map/all_gather | solution.py:37
  40.9 1.9 constant_dynamic-update-slice_fusion.3
  48.0 12.8 %collective-permute-done.10 = bf16[64,4096]{1,0:T(8,128)(2,1)S(1)} collective-permute-done((bf16[64,4096]{1,0:T(8,128)(2,1)S(1)}, bf16[64,4096]{1,0:T(8,128)(2,1)S(1)}, u32[]{:S(2)}, u32[]{:S(2)}) %collective-permute-start.10) | collective-permute-done | bytes 524320 | tf_op jit(solution)/shard_map/ppermute | solution.py:32
  60.9 4.2 %collective-permute-start.25 = (bf16[64,4096]{1,0:T(8,128)(2,1)S(1)}, bf16[64,4096]{1,0:T(8,128)(2,1)S(1)}, u32[]{:S(2)}, u32[]{:S(2)}) collective-permute-start(bf16[64,4096]{1,0:T(8,128)(2,1)S(1)} %collective-permute-done.9), channel_id=1, source_target_pairs={{0,4},{1,3},{2,6},{3,1},{4,0},{5,7},{6,2},{7,5},{8,12},{9,11},{10,... | collective-permute-start | bytes 1572872 | tf_op jit(solution)/shard_map/ppermute | solution.py:29
  65.2 7.0 %collective-permute-done.25 = bf16[64,4096]{1,0:T(8,128)(2,1)S(1)} collective-permute-done((bf16[64,4096]{1,0:T(8,128)(2,1)S(1)}, bf16[64,4096]{1,0:T(8,128)(2,1)S(1)}, u32[]{:S(2)}, u32[]{:S(2)}) %collective-permute-start.25) | collective-permute-done | bytes 524320 | tf_op jit(solution)/shard_map/ppermute | solution.py:29
  72.2 5.6 %collective-permute-done.2 = bf16[64,4096]{1,0:T(8,128)(2,1)S(1)} collective-permute-done((bf16[64,4096]{1,0:T(8,128)(2,1)S(1)}, bf16[64,4096]{1,0:T(8,128)(2,1)S(1)}, u32[]{:S(2)}, u32[]{:S(2)}) %collective-permute-start.2) | collective-permute-done | bytes 524320 | tf_op jit(solution)/shard_map/ppermute | solution.py:29
  77.8 2.0 collective-permute-start.26
  80.7 4.2 %collective-permute-done.11 = bf16[64,4096]{1,0:T(8,128)(2,1)S(1)} collective-permute-done((bf16[64,4096]{1,0:T(8,128)(2,1)S(1)}, bf16[64,4096]{1,0:T(8,128)(2,1)S(1)}, u32[]{:S(2)}, u32[]{:S(2)}) %collective-permute-start.11) | collective-permute-done | bytes 524320 | tf_op jit(solution)/shard_map/ppermute | solution.py:32
  87.0 3.9 %collective-permute-start.19 = (bf16[64,4096]{1,0:T(8,128)(2,1)S(1)}, bf16[64,4096]{1,0:T(8,128)(2,1)S(1)}, u32[]{:S(2)}, u32[]{:S(2)}) collective-permute-start(bf16[64,4096]{1,0:T(8,128)(2,1)S(1)} %collective-permute-done.10), channel_id=1, source_target_pairs={{0,4},{1,3},{2,6},{3,1},{4,0},{5,7},{6,2},{7,5},{8,12},{9,11},{10,... | collective-permute-start | bytes 1572872 | tf_op jit(solution)/shard_map/ppermute | solution.py:29
  91.0 7.1 %collective-permute-done.18 = bf16[64,4096]{1,0:T(8,128)(2,1)S(1)} collective-permute-done((bf16[64,4096]{1,0:T(8,128)(2,1)S(1)}, bf16[64,4096]{1,0:T(8,128)(2,1)S(1)}, u32[]{:S(2)}, u32[]{:S(2)}) %collective-permute-start.18) | collective-permute-done | bytes 524320 | tf_op jit(solution)/shard_map/ppermute | solution.py:26
  98.0 2.1 collective-permute-start.12
  101.0 2.3 collective-permute-start.20
  103.3 9.0 %collective-permute-done.12 = bf16[64,4096]{1,0:T(8,128)(2,1)S(1)} collective-permute-done((bf16[64,4096]{1,0:T(8,128)(2,1)S(1)}, bf16[64,4096]{1,0:T(8,128)(2,1)S(1)}, u32[]{:S(2)}, u32[]{:S(2)}) %collective-permute-start.12) | collective-permute-done | bytes 524320 | tf_op jit(solution)/shard_map/ppermute | solution.py:26
  112.3 3.5 %collective-permute-start.13 = (bf16[64,4096]{1,0:T(8,128)(2,1)S(1)}, bf16[64,4096]{1,0:T(8,128)(2,1)S(1)}, u32[]{:S(2)}, u32[]{:S(2)}) collective-permute-start(bf16[64,4096]{1,0:T(8,128)(2,1)S(1)} %collective-permute-done.11), channel_id=1, source_target_pairs={{0,4},{1,3},{2,6},{3,1},{4,0},{5,7},{6,2},{7,5},{8,12},{9,11},{10,... | collective-permute-start | bytes 1572872 | tf_op jit(solution)/shard_map/ppermute | solution.py:29
  115.9 7.0 %collective-permute-done.13 = bf16[64,4096]{1,0:T(8,128)(2,1)S(1)} collective-permute-done((bf16[64,4096]{1,0:T(8,128)(2,1)S(1)}, bf16[64,4096]{1,0:T(8,128)(2,1)S(1)}, u32[]{:S(2)}, u32[]{:S(2)}) %collective-permute-start.13) | collective-permute-done | bytes 524320 | tf_op jit(solution)/shard_map/ppermute | solution.py:29
  123.0 5.6 %collective-permute-done.14 = bf16[64,4096]{1,0:T(8,128)(2,1)S(1)} collective-permute-done((bf16[64,4096]{1,0:T(8,128)(2,1)S(1)}, bf16[64,4096]{1,0:T(8,128)(2,1)S(1)}, u32[]{:S(2)}, u32[]{:S(2)}) %collective-permute-start.14) | collective-permute-done | bytes 524320 | tf_op jit(solution)/shard_map/ppermute | solution.py:29
  129.9 4.6 %fusion.20 = f32[256,768]{1,0:T(8,128)} fusion(bf16[256,4096]{1,0:T(8,128)(2,1)S(1)} %constant_dynamic-update-slice_fusion.12, bf16[4096,384]{1,0:T(8,128)(2,1)} %collective-permute-done.3, bf16[4096,384]{1,0:T(8,128)(2,1)S(1)} %bitcast.46), kind=kOutput, calls=%fused_computation.70 | convolution fusion | flops 1623195648 | bytes 9175040 | tf_op jit(solution)/shard_map/dot_general | solution.py:60
  134.5 10.0 %fusion.3 = bf16[256,4096]{1,0:T(8,128)(2,1)S(1)} fusion(f32[256]{0:T(256)S(1)} %mul.98, f32[256,768]{1,0:T(8,128)} %fusion.20, bf16[384,4096]{1,0:T(8,128)(2,1)} %collective-permute-done.5, bf16[384,4096]{1,0:T(8,128)(2,1)} %bitcast.48, bf16[256,4096]{1,0:T(8,128)(2,1)} %copy-done.7, bf16[4096,384]{1,0:T(8,128)(2,1)} %collective-permute-done.4, ...), kind=kOutput, calls=%fused_computation.14 | convolution fusion | flops 3249668096 | bytes 17564672 | tf_op jit(solution)/shard_map/dot_general | solution.py:63
  145.7 2.0 collective-permute-start.28
  147.7 6.1 %fusion.21 = f32[256,768]{1,0:T(8,128)} fusion(bf16[256,4096]{1,0:T(8,128)(2,1)} %copy-done.5, bf16[4096,384]{1,0:T(8,128)(2,1)} %collective-permute-done.3, bf16[4096,384]{1,0:T(8,128)(2,1)} %bitcast.43), kind=kOutput, calls=%fused_computation.71 | convolution fusion | flops 1623195648 | bytes 9175040 | tf_op jit(solution)/shard_map/dot_general | solution.py:60
  153.8 10.0 %fusion.2 = bf16[256,4096]{1,0:T(8,128)(2,1)S(1)} fusion(f32[256]{0:T(256)S(1)} %mul.92, f32[256,768]{1,0:T(8,128)} %fusion.21, bf16[384,4096]{1,0:T(8,128)(2,1)} %collective-permute-done.5, bf16[384,4096]{1,0:T(8,128)(2,1)} %bitcast.49, bf16[256,4096]{1,0:T(8,128)(2,1)} %copy-done.5, bf16[4096,384]{1,0:T(8,128)(2,1)} %collective-permute-done.4, ...), kind=kOutput, calls=%fused_computation.13 | convolution fusion | flops 3249668096 | bytes 17564672 | tf_op jit(solution)/shard_map/dot_general | solution.py:63
  165.0 2.0 collective-permute-start.22
  167.1 6.3 %fusion.22 = f32[256,768]{1,0:T(8,128)} fusion(bf16[256,4096]{1,0:T(8,128)(2,1)} %copy-done.6, bf16[4096,384]{1,0:T(8,128)(2,1)} %collective-permute-done.3, bf16[4096,384]{1,0:T(8,128)(2,1)} %bitcast.44), kind=kOutput, calls=%fused_computation.72 | convolution fusion | flops 1623195648 | bytes 9175040 | tf_op jit(solution)/shard_map/dot_general | solution.py:60
  173.4 10.0 %fusion.1 = bf16[256,4096]{1,0:T(8,128)(2,1)S(1)} fusion(f32[256]{0:T(256)S(1)} %mul.86, f32[256,768]{1,0:T(8,128)} %fusion.22, bf16[384,4096]{1,0:T(8,128)(2,1)} %collective-permute-done.5, bf16[384,4096]{1,0:T(8,128)(2,1)} %bitcast.50, bf16[256,4096]{1,0:T(8,128)(2,1)} %copy-done.6, bf16[4096,384]{1,0:T(8,128)(2,1)} %collective-permute-done.4, ...), kind=kOutput, calls=%fused_computation.12 | convolution fusion | flops 3249668096 | bytes 17564672 | tf_op jit(solution)/shard_map/dot_general | solution.py:63
  184.5 2.0 collective-permute-start.16
  186.5 6.1 %fusion.23 = f32[256,768]{1,0:T(8,128)} fusion(bf16[256,4096]{1,0:T(8,128)(2,1)} %constant_dynamic-update-slice_fusion, bf16[4096,384]{1,0:T(8,128)(2,1)} %collective-permute-done.3, bf16[4096,384]{1,0:T(8,128)(2,1)} %bitcast.45), kind=kOutput, calls=%fused_computation.73 | convolution fusion | flops 1623195648 | bytes 9175040 | tf_op jit(solution)/shard_map/dot_general | solution.py:60
  192.6 10.0 %fusion = bf16[256,4096]{1,0:T(8,128)(2,1)S(1)} fusion(f32[256]{0:T(256)S(1)} %mul.80, f32[256,768]{1,0:T(8,128)} %fusion.23, bf16[384,4096]{1,0:T(8,128)(2,1)} %collective-permute-done.5, bf16[384,4096]{1,0:T(8,128)(2,1)} %bitcast.51, bf16[256,4096]{1,0:T(8,128)(2,1)} %constant_dynamic-update-slice_fusion, bf16[4096,384]{1,0:T(8,128)(2,1)} %collective-permute-done.4, ...), kind=kOutput, calls=%fused_computation.11 | convolution fusion | flops 3249668096 | bytes 17564672 | tf_op jit(solution)/shard_map/dot_general | solution.py:63
  208.6 11.4 %collective-permute-done.29 = bf16[64,4096]{1,0:T(8,128)(2,1)S(1)} collective-permute-done((bf16[64,4096]{1,0:T(8,128)(2,1)S(1)}, bf16[64,4096]{1,0:T(8,128)(2,1)S(1)}, u32[]{:S(2)}, u32[]{:S(2)}) %collective-permute-start.29) | collective-permute-done | bytes 524320 | tf_op jit(solution)/shard_map/ppermute | solution.py:26
  222.8 6.4 %collective-permute-done.23 = bf16[64,4096]{1,0:T(8,128)(2,1)S(1)} collective-permute-done((bf16[64,4096]{1,0:T(8,128)(2,1)S(1)}, bf16[64,4096]{1,0:T(8,128)(2,1)S(1)}, u32[]{:S(2)}, u32[]{:S(2)}) %collective-permute-start.23) | collective-permute-done | bytes 524320 | tf_op jit(solution)/shard_map/ppermute | solution.py:26
  230.3 6.5 %collective-permute-done.30 = bf16[64,4096]{1,0:T(8,128)(2,1)S(1)} collective-permute-done((bf16[64,4096]{1,0:T(8,128)(2,1)S(1)}, bf16[64,4096]{1,0:T(8,128)(2,1)S(1)}, u32[]{:S(2)}, u32[]{:S(2)}) %collective-permute-start.30) | collective-permute-done | bytes 524320 | tf_op jit(solution)/shard_map/ppermute | solution.py:32
  238.8 14.7 %collective-permute-done.31 = bf16[64,4096]{1,0:T(8,128)(2,1)S(1)} collective-permute-done((bf16[64,4096]{1,0:T(8,128)(2,1)S(1)}, bf16[64,4096]{1,0:T(8,128)(2,1)S(1)}, u32[]{:S(2)}, u32[]{:S(2)}) %collective-permute-start.31) | collective-permute-done | bytes 524320 | tf_op jit(solution)/shard_map/ppermute | solution.py:32
  253.8 11.2 %collective-permute-done.32 = bf16[64,4096]{1,0:T(8,128)(2,1)S(1)} collective-permute-done((bf16[64,4096]{1,0:T(8,128)(2,1)S(1)}, bf16[64,4096]{1,0:T(8,128)(2,1)S(1)}, u32[]{:S(2)}, u32[]{:S(2)}) %collective-permute-start.32) | collective-permute-done | bytes 524320 | tf_op jit(solution)/shard_map/ppermute | solution.py:32
  (105 shorter events, 32.7 us)
Async XLA Ops:
  0.0 44.1 %collective-permute-start.9 = (bf16[64,4096]{1,0:T(8,128)(2,1)}, bf16[64,4096]{1,0:T(8,128)(2,1)S(1)}, u32[]{:S(2)}, u32[]{:S(2)}) collective-permute-start(bf16[64,4096]{1,0:T(8,128)(2,1)} %param.6), channel_id=1, source_target_pairs={{0,8},{2,10},{4,12},{6,14},{8,16},{10,18},{12,20},{14,22},{16,24},... | collective-permute-start | bytes 1572872 | tf_op jit(solution)/shard_map/ppermute | solution.py:32
  1.6 42.6 %collective-permute-start = (bf16[64,4096]{1,0:T(8,128)(2,1)}, bf16[64,4096]{1,0:T(8,128)(2,1)S(1)}, u32[]{:S(2)}, u32[]{:S(2)}) collective-permute-start(bf16[64,4096]{1,0:T(8,128)(2,1)} %param.6), channel_id=1, source_target_pairs={{0,2},{1,5},{2,0},{3,7},{4,6},{5,1},{6,4},{7,3},{8,10},{9,13},{10,... | collective-permute-start | bytes 1572872 | tf_op jit(solution)/shard_map/ppermute | solution.py:26
  2.1 43.8 %collective-permute-start.1 = (bf16[64,4096]{1,0:T(8,128)(2,1)}, bf16[64,4096]{1,0:T(8,128)(2,1)S(1)}, u32[]{:S(2)}, u32[]{:S(2)}) collective-permute-start(bf16[64,4096]{1,0:T(8,128)(2,1)} %param.6), channel_id=1, source_target_pairs={{0,4},{1,3},{2,6},{3,1},{4,0},{5,7},{6,2},{7,5},{8,12},{9,11},{10,... | collective-permute-start | bytes 1572872 | tf_op jit(solution)/shard_map/ppermute | solution.py:29
  2.6 127.3 %collective-permute-start.3 = (bf16[4096,384]{1,0:T(8,128)(2,1)}, bf16[4096,384]{1,0:T(8,128)(2,1)}, u32[]{:S(2)}, u32[]{:S(2)}) collective-permute-start(bf16[4096,384]{1,0:T(8,128)(2,1)} %bitcast.42), channel_id=1, source_target_pairs={{0,1},{1,0},{2,3},{3,2},{4,5},{5,4},{6,7},{7,6},{8,9},{9,8},{10,11... | collective-permute-start | bytes 9437192 | tf_op jit(solution)/shard_map/ppermute | solution.py:19
  2.6 131.9 %collective-permute-start.5 = (bf16[384,4096]{1,0:T(8,128)(2,1)}, bf16[384,4096]{1,0:T(8,128)(2,1)}, u32[]{:S(2)}, u32[]{:S(2)}) collective-permute-start(bf16[384,4096]{1,0:T(8,128)(2,1)} %bitcast.47), channel_id=1, source_target_pairs={{0,1},{1,0},{2,3},{3,2},{4,5},{5,4},{6,7},{7,6},{8,9},{9,8},{10,11... | collective-permute-start | bytes 9437192 | tf_op jit(solution)/shard_map/ppermute | solution.py:19
  44.1 90.4 %collective-permute-start.4 = (bf16[4096,384]{1,0:T(8,128)(2,1)}, bf16[4096,384]{1,0:T(8,128)(2,1)}, u32[]{:S(2)}, u32[]{:S(2)}) collective-permute-start(bf16[4096,384]{1,0:T(8,128)(2,1)} %bitcast.52), channel_id=1, source_target_pairs={{0,1},{1,0},{2,3},{3,2},{4,5},{5,4},{6,7},{7,6},{8,9},{9,8},{10,11... | collective-permute-start | bytes 9437192 | tf_op jit(solution)/shard_map/ppermute | solution.py:19
  44.2 16.7 %collective-permute-start.10 = (bf16[64,4096]{1,0:T(8,128)(2,1)S(1)}, bf16[64,4096]{1,0:T(8,128)(2,1)S(1)}, u32[]{:S(2)}, u32[]{:S(2)}) collective-permute-start(bf16[64,4096]{1,0:T(8,128)(2,1)S(1)} %collective-permute-done.9), channel_id=1, source_target_pairs={{0,8},{2,10},{4,12},{6,14},{8,16},{10,18},{12,20},{14,22},{16,24},... | collective-permute-start | bytes 1572872 | tf_op jit(solution)/shard_map/ppermute | solution.py:32
  45.9 19.2 %collective-permute-start.24 = (bf16[64,4096]{1,0:T(8,128)(2,1)S(1)}, bf16[64,4096]{1,0:T(8,128)(2,1)S(1)}, u32[]{:S(2)}, u32[]{:S(2)}) collective-permute-start(bf16[64,4096]{1,0:T(8,128)(2,1)S(1)} %collective-permute-done.9), channel_id=1, source_target_pairs={{0,2},{1,5},{2,0},{3,7},{4,6},{5,1},{6,4},{7,3},{8,10},{9,13},{10,... | collective-permute-start | bytes 1572872 | tf_op jit(solution)/shard_map/ppermute | solution.py:26
  60.9 11.3 %collective-permute-start.25 = (bf16[64,4096]{1,0:T(8,128)(2,1)S(1)}, bf16[64,4096]{1,0:T(8,128)(2,1)S(1)}, u32[]{:S(2)}, u32[]{:S(2)}) collective-permute-start(bf16[64,4096]{1,0:T(8,128)(2,1)S(1)} %collective-permute-done.9), channel_id=1, source_target_pairs={{0,4},{1,3},{2,6},{3,1},{4,0},{5,7},{6,2},{7,5},{8,12},{9,11},{10,... | collective-permute-start | bytes 1572872 | tf_op jit(solution)/shard_map/ppermute | solution.py:29
  65.1 12.7 %collective-permute-start.2 = (bf16[64,4096]{1,0:T(8,128)(2,1)S(1)}, bf16[64,4096]{1,0:T(8,128)(2,1)S(1)}, u32[]{:S(2)}, u32[]{:S(2)}) collective-permute-start(bf16[64,4096]{1,0:T(8,128)(2,1)S(1)} %collective-permute-done), channel_id=1, source_target_pairs={{0,4},{1,3},{2,6},{3,1},{4,0},{5,7},{6,2},{7,5},{8,12},{9,11},{10,... | collective-permute-start | bytes 1572872 | tf_op jit(solution)/shard_map/ppermute | solution.py:29
  72.2 12.7 %collective-permute-start.11 = (bf16[64,4096]{1,0:T(8,128)(2,1)S(1)}, bf16[64,4096]{1,0:T(8,128)(2,1)S(1)}, u32[]{:S(2)}, u32[]{:S(2)}) collective-permute-start(bf16[64,4096]{1,0:T(8,128)(2,1)S(1)} %collective-permute-done.10), channel_id=1, source_target_pairs={{0,8},{2,10},{4,12},{6,14},{8,16},{10,18},{12,20},{14,22},{16,24},... | collective-permute-start | bytes 1572872 | tf_op jit(solution)/shard_map/ppermute | solution.py:32
  77.8 9.2 %collective-permute-start.26 = (bf16[64,4096]{1,0:T(8,128)(2,1)S(1)}, bf16[64,4096]{1,0:T(8,128)(2,1)S(1)}, u32[]{:S(2)}, u32[]{:S(2)}) collective-permute-start(bf16[64,4096]{1,0:T(8,128)(2,1)S(1)} %collective-permute-done.24), channel_id=1, source_target_pairs={{0,4},{1,3},{2,6},{3,1},{4,0},{5,7},{6,2},{7,5},{8,12},{9,11},{10,... | collective-permute-start | bytes 1572872 | tf_op jit(solution)/shard_map/ppermute | solution.py:29
  84.9 13.1 %collective-permute-start.18 = (bf16[64,4096]{1,0:T(8,128)(2,1)S(1)}, bf16[64,4096]{1,0:T(8,128)(2,1)S(1)}, u32[]{:S(2)}, u32[]{:S(2)}) collective-permute-start(bf16[64,4096]{1,0:T(8,128)(2,1)S(1)} %collective-permute-done.10), channel_id=1, source_target_pairs={{0,2},{1,5},{2,0},{3,7},{4,6},{5,1},{6,4},{7,3},{8,10},{9,13},{10,... | collective-permute-start | bytes 1572872 | tf_op jit(solution)/shard_map/ppermute | solution.py:26
  87.0 14.0 %collective-permute-start.19 = (bf16[64,4096]{1,0:T(8,128)(2,1)S(1)}, bf16[64,4096]{1,0:T(8,128)(2,1)S(1)}, u32[]{:S(2)}, u32[]{:S(2)}) collective-permute-start(bf16[64,4096]{1,0:T(8,128)(2,1)S(1)} %collective-permute-done.10), channel_id=1, source_target_pairs={{0,4},{1,3},{2,6},{3,1},{4,0},{5,7},{6,2},{7,5},{8,12},{9,11},{10,... | collective-permute-start | bytes 1572872 | tf_op jit(solution)/shard_map/ppermute | solution.py:29
  98.0 14.3 %collective-permute-start.12 = (bf16[64,4096]{1,0:T(8,128)(2,1)S(1)}, bf16[64,4096]{1,0:T(8,128)(2,1)S(1)}, u32[]{:S(2)}, u32[]{:S(2)}) collective-permute-start(bf16[64,4096]{1,0:T(8,128)(2,1)S(1)} %collective-permute-done.11), channel_id=1, source_target_pairs={{0,2},{1,5},{2,0},{3,7},{4,6},{5,1},{6,4},{7,3},{8,10},{9,13},{10,... | collective-permute-start | bytes 1572872 | tf_op jit(solution)/shard_map/ppermute | solution.py:26
  101.0 14.8 %collective-permute-start.20 = (bf16[64,4096]{1,0:T(8,128)(2,1)S(1)}, bf16[64,4096]{1,0:T(8,128)(2,1)S(1)}, u32[]{:S(2)}, u32[]{:S(2)}) collective-permute-start(bf16[64,4096]{1,0:T(8,128)(2,1)S(1)} %collective-permute-done.18), channel_id=1, source_target_pairs={{0,4},{1,3},{2,6},{3,1},{4,0},{5,7},{6,2},{7,5},{8,12},{9,11},{10,... | collective-permute-start | bytes 1572872 | tf_op jit(solution)/shard_map/ppermute | solution.py:29
  112.3 10.6 %collective-permute-start.13 = (bf16[64,4096]{1,0:T(8,128)(2,1)S(1)}, bf16[64,4096]{1,0:T(8,128)(2,1)S(1)}, u32[]{:S(2)}, u32[]{:S(2)}) collective-permute-start(bf16[64,4096]{1,0:T(8,128)(2,1)S(1)} %collective-permute-done.11), channel_id=1, source_target_pairs={{0,4},{1,3},{2,6},{3,1},{4,0},{5,7},{6,2},{7,5},{8,12},{9,11},{10,... | collective-permute-start | bytes 1572872 | tf_op jit(solution)/shard_map/ppermute | solution.py:29
  115.8 12.7 %collective-permute-start.14 = (bf16[64,4096]{1,0:T(8,128)(2,1)S(1)}, bf16[64,4096]{1,0:T(8,128)(2,1)S(1)}, u32[]{:S(2)}, u32[]{:S(2)}) collective-permute-start(bf16[64,4096]{1,0:T(8,128)(2,1)S(1)} %collective-permute-done.12), channel_id=1, source_target_pairs={{0,4},{1,3},{2,6},{3,1},{4,0},{5,7},{6,2},{7,5},{8,12},{9,11},{10,... | collective-permute-start | bytes 1572872 | tf_op jit(solution)/shard_map/ppermute | solution.py:29
  145.7 57.1 %collective-permute-start.28 = (bf16[64,4096]{1,0:T(8,128)(2,1)}, bf16[64,4096]{1,0:T(8,128)(2,1)}, u32[]{:S(2)}, u32[]{:S(2)}) collective-permute-start(bf16[64,4096]{1,0:T(8,128)(2,1)} %get-tuple-element.12), channel_id=1, source_target_pairs={{0,4},{1,3},{2,6},{3,1},{4,0},{5,7},{6,2},{7,5},{8,12},{9,11},{10,... | collective-permute-start | bytes 1572872 | tf_op jit(solution)/shard_map/ppermute | solution.py:29
  147.7 59.7 %collective-permute-start.27 = (bf16[64,4096]{1,0:T(8,128)(2,1)}, bf16[64,4096]{1,0:T(8,128)(2,1)}, u32[]{:S(2)}, u32[]{:S(2)}) collective-permute-start(bf16[64,4096]{1,0:T(8,128)(2,1)} %get-tuple-element.11), channel_id=1, source_target_pairs={{0,4},{1,3},{2,6},{3,1},{4,0},{5,7},{6,2},{7,5},{8,12},{9,11},{10,... | collective-permute-start | bytes 1572872 | tf_op jit(solution)/shard_map/ppermute | solution.py:29
  165.0 40.1 %collective-permute-start.22 = (bf16[64,4096]{1,0:T(8,128)(2,1)}, bf16[64,4096]{1,0:T(8,128)(2,1)}, u32[]{:S(2)}, u32[]{:S(2)}) collective-permute-start(bf16[64,4096]{1,0:T(8,128)(2,1)} %get-tuple-element.10), channel_id=1, source_target_pairs={{0,4},{1,3},{2,6},{3,1},{4,0},{5,7},{6,2},{7,5},{8,12},{9,11},{10,... | collective-permute-start | bytes 1572872 | tf_op jit(solution)/shard_map/ppermute | solution.py:29
  167.0 55.7 %collective-permute-start.21 = (bf16[64,4096]{1,0:T(8,128)(2,1)}, bf16[64,4096]{1,0:T(8,128)(2,1)S(1)}, u32[]{:S(2)}, u32[]{:S(2)}) collective-permute-start(bf16[64,4096]{1,0:T(8,128)(2,1)} %get-tuple-element.9), channel_id=1, source_target_pairs={{0,4},{1,3},{2,6},{3,1},{4,0},{5,7},{6,2},{7,5},{8,12},{9,11},{10,... | collective-permute-start | bytes 1572872 | tf_op jit(solution)/shard_map/ppermute | solution.py:29
  184.5 37.9 %collective-permute-start.16 = (bf16[64,4096]{1,0:T(8,128)(2,1)}, bf16[64,4096]{1,0:T(8,128)(2,1)S(1)}, u32[]{:S(2)}, u32[]{:S(2)}) collective-permute-start(bf16[64,4096]{1,0:T(8,128)(2,1)} %get-tuple-element.8), channel_id=1, source_target_pairs={{0,4},{1,3},{2,6},{3,1},{4,0},{5,7},{6,2},{7,5},{8,12},{9,11},{10,... | collective-permute-start | bytes 1572872 | tf_op jit(solution)/shard_map/ppermute | solution.py:29
  202.8 36.0 %collective-permute-start.15 = (bf16[64,4096]{1,0:T(8,128)(2,1)}, bf16[64,4096]{1,0:T(8,128)(2,1)S(1)}, u32[]{:S(2)}, u32[]{:S(2)}) collective-permute-start(bf16[64,4096]{1,0:T(8,128)(2,1)} %get-tuple-element.7), channel_id=1, source_target_pairs={{0,4},{1,3},{2,6},{3,1},{4,0},{5,7},{6,2},{7,5},{8,12},{9,11},{10,... | collective-permute-start | bytes 1572872 | tf_op jit(solution)/shard_map/ppermute | solution.py:29
  205.1 14.9 %collective-permute-start.29 = (bf16[64,4096]{1,0:T(8,128)(2,1)S(1)}, bf16[64,4096]{1,0:T(8,128)(2,1)S(1)}, u32[]{:S(2)}, u32[]{:S(2)}) collective-permute-start(bf16[64,4096]{1,0:T(8,128)(2,1)S(1)} %add_convert_fusion.4), channel_id=1, source_target_pairs={{0,2},{1,5},{2,0},{3,7},{4,6},{5,1},{6,4},{7,3},{8,10},{9,13},{10,... | collective-permute-start | bytes 1572872 | tf_op jit(solution)/shard_map/ppermute | solution.py:26
  207.4 30.3 %collective-permute-start.7 = (bf16[64,4096]{1,0:T(8,128)(2,1)S(1)}, bf16[64,4096]{1,0:T(8,128)(2,1)S(1)}, u32[]{:S(2)}, u32[]{:S(2)}) collective-permute-start(bf16[64,4096]{1,0:T(8,128)(2,1)S(1)} %get-tuple-element.6), channel_id=1, source_target_pairs={{0,4},{1,3},{2,6},{3,1},{4,0},{5,7},{6,2},{7,5},{8,12},{9,11},{10,... | collective-permute-start | bytes 1572872 | tf_op jit(solution)/shard_map/ppermute | solution.py:29
  222.5 14.3 %collective-permute-start.30 = (bf16[64,4096]{1,0:T(8,128)(2,1)S(1)}, bf16[64,4096]{1,0:T(8,128)(2,1)S(1)}, u32[]{:S(2)}, u32[]{:S(2)}) collective-permute-start(bf16[64,4096]{1,0:T(8,128)(2,1)S(1)} %add_convert_fusion.3), channel_id=1, source_target_pairs={{0,8},{2,10},{4,12},{6,14},{8,16},{10,18},{12,20},{14,22},{16,24},... | collective-permute-start | bytes 1572872 | tf_op jit(solution)/shard_map/ppermute | solution.py:32
  222.7 31.1 %collective-permute-start.6 = (bf16[64,4096]{1,0:T(8,128)(2,1)S(1)}, bf16[64,4096]{1,0:T(8,128)(2,1)S(1)}, u32[]{:S(2)}, u32[]{:S(2)}) collective-permute-start(bf16[64,4096]{1,0:T(8,128)(2,1)S(1)} %get-tuple-element.5), channel_id=1, source_target_pairs={{0,4},{1,3},{2,6},{3,1},{4,0},{5,7},{6,2},{7,5},{8,12},{9,11},{10,... | collective-permute-start | bytes 1572872 | tf_op jit(solution)/shard_map/ppermute | solution.py:29
  229.2 9.6 %collective-permute-start.17 = (bf16[64,4096]{1,0:T(8,128)(2,1)S(1)}, bf16[64,4096]{1,0:T(8,128)(2,1)S(1)}, u32[]{:S(2)}, u32[]{:S(2)}) collective-permute-start(bf16[64,4096]{1,0:T(8,128)(2,1)S(1)} %add_convert_fusion.6), channel_id=1, source_target_pairs={{0,2},{1,5},{2,0},{3,7},{4,6},{5,1},{6,4},{7,3},{8,10},{9,13},{10,... | collective-permute-start | bytes 1572872 | tf_op jit(solution)/shard_map/ppermute | solution.py:26
  237.0 16.4 %collective-permute-start.31 = (bf16[64,4096]{1,0:T(8,128)(2,1)S(1)}, bf16[64,4096]{1,0:T(8,128)(2,1)S(1)}, u32[]{:S(2)}, u32[]{:S(2)}) collective-permute-start(bf16[64,4096]{1,0:T(8,128)(2,1)S(1)} %add_convert_fusion.2), channel_id=1, source_target_pairs={{0,8},{2,10},{4,12},{6,14},{8,16},{10,18},{12,20},{14,22},{16,24},... | collective-permute-start | bytes 1572872 | tf_op jit(solution)/shard_map/ppermute | solution.py:32
  237.8 16.0 %collective-permute-start.8 = (bf16[64,4096]{1,0:T(8,128)(2,1)S(1)}, bf16[64,4096]{1,0:T(8,128)(2,1)S(1)}, u32[]{:S(2)}, u32[]{:S(2)}) collective-permute-start(bf16[64,4096]{1,0:T(8,128)(2,1)S(1)} %add_convert_fusion.7), channel_id=1, source_target_pairs={{0,2},{1,5},{2,0},{3,7},{4,6},{5,1},{6,4},{7,3},{8,10},{9,13},{10,... | collective-permute-start | bytes 1572872 | tf_op jit(solution)/shard_map/ppermute | solution.py:26
  253.7 11.3 %collective-permute-start.32 = (bf16[64,4096]{1,0:T(8,128)(2,1)S(1)}, bf16[64,4096]{1,0:T(8,128)(2,1)S(1)}, u32[]{:S(2)}, u32[]{:S(2)}) collective-permute-start(bf16[64,4096]{1,0:T(8,128)(2,1)S(1)} %add_convert_fusion.1), channel_id=1, source_target_pairs={{0,8},{2,10},{4,12},{6,14},{8,16},{10,18},{12,20},{14,22},{16,24},... | collective-permute-start | bytes 1572872 | tf_op jit(solution)/shard_map/ppermute | solution.py:32
  (10 other events, 133.9 us)

commit v2 on v1

v2 whole, which is shorter than its diff:
```python
import functools

import jax
import jax.numpy as jnp
from jax import lax
from jax.experimental import pallas as pl
from jax.experimental.pallas import tpu as pltpu
from jax.sharding import PartitionSpec as P

BF = jnp.bfloat16
F32 = jnp.float32
META = 128


def named_by(meta, expert, top):
    ids = meta[:, :top].astype(F32)
    return (ids == expert.astype(F32)).astype(F32)


def weight_for(meta, expert, top):
    m = meta.astype(F32)
    parts = m[:, top : 2 * top] + m[:, 2 * top : 3 * top] + m[:, 3 * top : 4 * top]
    return jnp.sum(named_by(meta, expert, top) * parts, axis=1, keepdims=True)


def one_hot(meta, expert, top, first, slots):
    rows = meta.shape[0]
    named = jnp.sum(named_by(meta, expert, top), axis=1, keepdims=True)
    below = lax.broadcasted_iota(jnp.int32, (rows, rows), 0) > lax.broadcasted_iota(jnp.int32, (rows, rows), 1)
    wide = jnp.broadcast_to(named, (rows, slots)).astype(BF)
    rank = jnp.dot(below.astype(F32).astype(BF), wide, preferred_element_type=F32)
    slot = lax.broadcasted_iota(jnp.int32, (rows, slots), 1).astype(F32)
    hit = jnp.logical_and(rank + float(first) == slot, named > 0.5)
    return hit.astype(F32).astype(BF)


def select_kernel(top, cap, slots, expert_ref, z_ref, a_ref, zm_ref, am_ref, out_ref):
    expert = expert_ref[0]
    dims = (((0,), (0,)), ((), ()))
    pick_z = one_hot(zm_ref[...], expert, top, 0, slots)
    pick_a = one_hot(am_ref[...], expert, top, cap, slots)
    got = lax.dot_general(pick_z, z_ref[...], dims, preferred_element_type=F32)
    got = got + lax.dot_general(pick_a, a_ref[...], dims, preferred_element_type=F32)
    out_ref[...] = got.astype(BF)


def select(expert, z, a, top, cap, slots):
    rows, wide = z.shape
    last = wide // META - 1
    return pl.pallas_call(
        functools.partial(select_kernel, top, cap, slots),
        out_shape=jax.ShapeDtypeStruct((slots, wide), BF),
        grid=(1,),
        in_specs=[
            pl.BlockSpec(memory_space=pltpu.SMEM),
            pl.BlockSpec((rows, wide), lambda i: (0, 0)),
            pl.BlockSpec((rows, wide), lambda i: (0, 0)),
            pl.BlockSpec((rows, META), lambda i: (0, last)),
            pl.BlockSpec((rows, META), lambda i: (0, last)),
        ],
        out_specs=pl.BlockSpec((slots, wide), lambda i: (0, 0)),
        compiler_params=pltpu.CompilerParams(vmem_limit_bytes=16 << 20),
        cost_estimate=pl.CostEstimate(flops=4 * slots * rows * wide, bytes_accessed=6 * rows * wide, transcendentals=0),
    )(expert, z, a, z, a)


def expert_kernel(top, nk, ff, expert_ref, z_ref, a_ref, b_ref, zm_ref, am_ref, bm_ref, w0_ref, w1_ref, d0_ref, d1_ref,
                  pz_ref, pa_ref, pb_ref, acc0, acc1, hid):
    i = pl.program_id(0)
    rows = z_ref.shape[0]

    @pl.when(i == 0)
    def _():
        acc0[...] = jnp.zeros_like(acc0)
        acc1[...] = jnp.zeros_like(acc1)

    @pl.when(i < nk)
    def _():
        x = jnp.concatenate([z_ref[...], a_ref[...], b_ref[...]], axis=0)
        acc0[...] += jnp.dot(x, w0_ref[...], preferred_element_type=F32)
        acc1[...] += jnp.dot(x, w1_ref[...], preferred_element_type=F32)

    @pl.when(i == nk - 1)
    def _():
        for c, acc in enumerate((acc0, acc1)):
            gate = acc[:, :ff]
            hid[:, c * ff : (c + 1) * ff] = (gate / (1.0 + jnp.exp(-gate)) * acc[:, ff:]).astype(BF)

    @pl.when(i >= nk)
    def _():
        expert = expert_ref[0]
        out = jnp.dot(hid[:, :ff], d0_ref[...], preferred_element_type=F32)
        out = out + jnp.dot(hid[:, ff:], d1_ref[...], preferred_element_type=F32)
        pz_ref[...] = (out[:rows] * weight_for(zm_ref[...], expert, top)).astype(BF)
        pa_ref[...] = (out[rows : 2 * rows] * weight_for(am_ref[...], expert, top)).astype(BF)
        pb_ref[...] = (out[2 * rows :] * weight_for(bm_ref[...], expert, top)).astype(BF)


def run_expert(expert, z, a, b, w0, w1, d0, d1, top):
    rows, wide = z.shape
    slots = b.shape[0]
    width = wide - META
    ff = d0.shape[0]
    total = 2 * rows + slots
    last = wide // META - 1
    tile = 1024
    nk = width // tile
    col = lambda i: (0, jnp.minimum(i, nk - 1))
    meta = lambda i: (0, last)
    down = lambda i: (0, jnp.maximum(i - nk, 0))
    return pl.pallas_call(
        functools.partial(expert_kernel, top, nk, ff),
        out_shape=[
            jax.ShapeDtypeStruct((rows, width), BF),
            jax.ShapeDtypeStruct((rows, width), BF),
            jax.ShapeDtypeStruct((slots, width), BF),
        ],
        grid=(2 * nk,),
        in_specs=[
            pl.BlockSpec(memory_space=pltpu.SMEM),
            pl.BlockSpec((rows, tile), col),
            pl.BlockSpec((rows, tile), col),
            pl.BlockSpec((slots, tile), col),
            pl.BlockSpec((rows, META), meta),
            pl.BlockSpec((rows, META), meta),
            pl.BlockSpec((slots, META), meta),
            pl.BlockSpec((tile, 2 * ff), lambda i: (jnp.minimum(i, nk - 1), 0)),
            pl.BlockSpec((tile, 2 * ff), lambda i: (jnp.minimum(i, nk - 1), 0)),
            pl.BlockSpec((ff, tile), down),
            pl.BlockSpec((ff, tile), down),
        ],
        out_specs=[
            pl.BlockSpec((rows, tile), down),
            pl.BlockSpec((rows, tile), down),
            pl.BlockSpec((slots, tile), down),
        ],
        scratch_shapes=[
            pltpu.VMEM((total, 2 * ff), F32),
            pltpu.VMEM((total, 2 * ff), F32),
            pltpu.VMEM((total, 2 * ff), BF),
        ],
        compiler_params=pltpu.CompilerParams(vmem_limit_bytes=32 << 20),
        cost_estimate=pl.CostEstimate(
            flops=12 * total * width * ff, bytes_accessed=12 * ff * width + 4 * total * width, transcendentals=2 * total * ff
        ),
    )(expert, z, a, b, z, a, b, w0, w1, d0, d1)


def put_back_kernel(top, first, slots, n_more, expert_ref, own_ref, meta_ref, got_ref, *refs):
    out_ref = refs[n_more]
    place = one_hot(meta_ref[...], expert_ref[0], top, first, slots)
    total = own_ref[...].astype(F32) + jnp.dot(place, got_ref[...], preferred_element_type=F32)
    for more in refs[:n_more]:
        total = total + more[...].astype(F32)
    out_ref[...] = total.astype(BF)


def put_back(expert, own, block, got, more, top, first):
    rows, width = own.shape
    slots = got.shape[0]
    last = block.shape[1] // META - 1
    whole = lambda i: (0, 0)
    return pl.pallas_call(
        functools.partial(put_back_kernel, top, first, slots, len(more)),
        out_shape=jax.ShapeDtypeStruct((rows, width), BF),
        grid=(1,),
        in_specs=[
            pl.BlockSpec(memory_space=pltpu.SMEM),
            pl.BlockSpec((rows, width), whole),
            pl.BlockSpec((rows, META), lambda i: (0, last)),
            pl.BlockSpec((slots, width), whole),
        ]
        + [pl.BlockSpec((rows, width), whole) for _ in more],
        out_specs=pl.BlockSpec((rows, width), whole),
        compiler_params=pltpu.CompilerParams(vmem_limit_bytes=16 << 20),
        cost_estimate=pl.CostEstimate(
            flops=2 * slots * rows * width, bytes_accessed=(6 + 2 * len(more)) * rows * width, transcendentals=0
        ),
    )(expert, own, block, got, *more)


def on_device(tokens, expert_ids, route_weights, gate_proj, up_proj, down_proj):
    rows, width = tokens.shape
    top = expert_ids.shape[1]
    n_ep = lax.axis_size("ep")
    ring = n_ep // 4
    cap = max(2, min(rows, rows * top * 5 // (4 * n_ep)))
    slots = -(-2 * cap // 16) * 16
    me = lax.axis_index("ep")
    core = lax.axis_index("etp")
    axes = ("ep", "etp")

    pairs_a = [(2 * i + c, 2 * (i ^ (1, 2)[c]) + c) for i in range(n_ep) for c in range(2)]
    pairs_b = [(2 * i + c, 2 * (i ^ (2, 1)[c]) + c) for i in range(n_ep) for c in range(2)]
    pairs_z = [(i, (i + 4) % n_ep) for i in range(n_ep)]

    def hop_a(x):
        return lax.ppermute(x, axes, pairs_a)

    def hop_b(x):
        return lax.ppermute(x, axes, pairs_b)

    def hop_z(x):
        return lax.ppermute(x, "ep", pairs_z)

    def swap(x):
        return lax.ppermute(x, "etp", [(0, 1), (1, 0)])

    mine = me.reshape(1).astype(jnp.int32)
    near = (me ^ jnp.where(core == 0, 2, 1)).reshape(1).astype(jnp.int32)

    high = lax.reduce_precision(route_weights, 8, 7)
    middle = lax.reduce_precision(route_weights - high, 8, 7)
    low = route_weights - high - middle
    meta = jnp.concatenate([expert_ids.astype(F32), high, middle, low], axis=1).astype(BF)
    meta = jnp.pad(meta, ((0, 0), (0, META - meta.shape[1])))
    block = jnp.concatenate([tokens, meta], axis=1)

    blocks = []
    for k in range(ring):
        if k:
            block = hop_z(block)
        a = hop_a(block)
        b = hop_b(select(near, block, a, top, cap, slots))
        blocks.append((block, a, b))

    w0 = jnp.concatenate([gate_proj[0], up_proj[0]], axis=1)
    w1 = swap(w0)
    d0 = down_proj[0]
    d1 = swap(d0)

    parts = [run_expert(mine, z, a, b, w0, w1, d0, d1, top) for z, a, b in blocks]

    carry = None
    for k in list(range(1, ring)) + [0]:
        z, a, _ = blocks[k]
        pz, pa, pb = parts[k]
        got_b = hop_b(pb)
        got_a = hop_a(put_back(near, pa, a, got_b, [], top, cap))
        more = [got_a] if carry is None else [got_a, hop_z(carry)]
        carry = put_back(near, pz, z, got_b, more, top, 0)
    return carry


def solution(mesh):
    in_specs = (
        P(("groups", "ep", "etp"), None),
        P(("groups", "ep", "etp"), None),
        P(("groups", "ep", "etp"), None),
        P("ep", None, "etp"),
        P("ep", None, "etp"),
        P("ep", "etp", None),
    )
    out_specs = P(("groups", "ep", "etp"), None)
    return jax.shard_map(
        on_device, mesh=mesh, in_specs=in_specs, out_specs=out_specs, check_vma=False
    )
```

time: 270 us -> 162 us (0.60)
  the two profiles are of different devices: /device:TPU:14 before, /device:TPU:0 now
where the time goes in v2:
time: 162 us; the launch traced here: 161 us
  waiting for transfers between devices  69.4 us (43%)
  Pallas kernels  60.4 us (37%)
  starting transfers between devices  23.1 us (14%)
  other arithmetic  7.3 us (5%)
    ppermute x6, waiting for transfers between devices, hop_z(): return lax.ppermute(x, 'ep', pairs_z)  48.3 us
    pallas_call x4, Pallas kernels, run_expert(): pl.pallas_call(functools.partial(expert_kernel, top, nk, ff), out_shape=[...  45.2 us
    ppermute x8, waiting for transfers between devices, hop_b(): return lax.ppermute(x, axes, pairs_b)  16 us
    ppermute x8, starting transfers between devices, hop_a(): return lax.ppermute(x, axes, pairs_a)  9.9 us
    ppermute x8, starting transfers between devices, hop_b(): return lax.ppermute(x, axes, pairs_b)  9.27 us
    pallas_call x8, Pallas kernels, put_back(): pl.pallas_call(functools.partial(put_back_kernel, top, first, slots, len(...  8.62 us
    pallas_call x4, Pallas kernels, select(): pl.pallas_call(functools.partial(select_kernel, top, cap, slots), out_sha...  6.53 us
    concatenate x1, other arithmetic, on_device(): w0 = jnp.concatenate([gate_proj[0], up_proj[0]], axis=1)  6.11 us
  transfers between devices with their start and end apart: 24, of which 8 were waited for; matrix products, arithmetic and copies ran while one was open for 1% of the time, Pallas kernels for 37%

profile of v2, /device:TPU:0, one launch (start us, length us, event | category | flops | bytes accessed | tf_op | source)
XLA Modules:
  0.0 161.5 jit_solution(13031117813860828683)
XLA Ops:
  0.0 6.1 %pad_maximum_fusion.w0_ref = bf16[4096,768]{1,0:T(8,128)(2,1)} fusion(bf16[4096,384]{1,0:T(8,128)(2,1)} %bitcast.10, bf16[4096,384]{1,0:T(8,128)(2,1)} %bitcast.11), kind=kLoop, calls=%fused_computation | loop fusion | flops 12582912 | bytes 12582912 | tf_op jit(solution)/shard_map/concatenate | solution.py:227
  9.0 3.0 %collective-permute-start.6 = (bf16[64,4224]{1,0:T(8,128)(2,1)S(1)}, bf16[64,4224]{1,0:T(8,128)(2,1)}, u32[]{:S(2)}, u32[]{:S(2)}) collective-permute-start(bf16[64,4224]{1,0:T(8,128)(2,1)S(1)} %pad_maximum_fusion.1.z_ref.zm_ref.meta_ref), channel_id=1, source_target_pairs={{0,8},{2,10},{4,12},{6,14},{8,16},{10,18},{12,20},{14,22},{16,24},... | collective-permute-start | bytes 1622024 | tf_op jit(solution)/shard_map/ppermute | solution.py:204
  12.1 14.6 %collective-permute-done.6.z_ref.zm_ref.meta_ref = bf16[64,4224]{1,0:T(8,128)(2,1)} collective-permute-done((bf16[64,4224]{1,0:T(8,128)(2,1)S(1)}, bf16[64,4224]{1,0:T(8,128)(2,1)}, u32[]{:S(2)}, u32[]{:S(2)}) %collective-permute-start.6) | collective-permute-done | bytes 540704 | tf_op jit(solution)/shard_map/ppermute | solution.py:204
  26.6 1.5 collective-permute-start.17
  28.1 14.3 %collective-permute-done.7.z_ref.zm_ref.meta_ref = bf16[64,4224]{1,0:T(8,128)(2,1)} collective-permute-done((bf16[64,4224]{1,0:T(8,128)(2,1)}, bf16[64,4224]{1,0:T(8,128)(2,1)}, u32[]{:S(2)}, u32[]{:S(2)}) %collective-permute-start.7) | collective-permute-done | bytes 540704 | tf_op jit(solution)/shard_map/ppermute | solution.py:204
  42.4 1.2 collective-permute-start.13
  43.6 2.0 %shard_map.73 = bf16[80,4224]{1,0:T(8,128)(2,1)S(1)} custom-call(s32[1]{0:T(128)} %bitcast.expert_ref, bf16[64,4224]{1,0:T(8,128)(2,1)} %collective-permute-done.6.z_ref.zm_ref.meta_ref, bf16[64,4224]{1,0:T(8,128)(2,1)} %collective-permute-done.17.a_ref.am_ref.meta_ref, bf16[64,4224]{1,0:T(8,128)(2,1)} %collective-permute-done.6.z_ref.zm_ref.meta_ref, ...), custom_call_target="tpu_custom_call" | custom-call | flops 86507520 | bytes 1622016 | tf_op jit(solution)/shard_map/pallas_call | solution.py:50
  45.7 1.6 collective-permute-start.18
  47.3 10.0 %collective-permute-done.8.z_ref.zm_ref.meta_ref = bf16[64,4224]{1,0:T(8,128)(2,1)} collective-permute-done((bf16[64,4224]{1,0:T(8,128)(2,1)}, bf16[64,4224]{1,0:T(8,128)(2,1)}, u32[]{:S(2)}, u32[]{:S(2)}) %collective-permute-start.8) | collective-permute-done | bytes 540704 | tf_op jit(solution)/shard_map/ppermute | solution.py:204
  58.2 2.0 %shard_map.70 = bf16[80,4224]{1,0:T(8,128)(2,1)S(1)} custom-call(s32[1]{0:T(128)} %bitcast.expert_ref, bf16[64,4224]{1,0:T(8,128)(2,1)} %collective-permute-done.7.z_ref.zm_ref.meta_ref, bf16[64,4224]{1,0:T(8,128)(2,1)} %collective-permute-done.13.a_ref.am_ref.meta_ref, bf16[64,4224]{1,0:T(8,128)(2,1)} %collective-permute-done.7.z_ref.zm_ref.meta_ref, ...), custom_call_target="tpu_custom_call" | custom-call | flops 86507520 | bytes 1622016 | tf_op jit(solution)/shard_map/pallas_call | solution.py:50
  60.2 1.6 collective-permute-start.14
  62.6 11.3 %shard_map.74 = (bf16[64,4096]{1,0:T(8,128)(2,1)S(1)}, bf16[64,4096]{1,0:T(8,128)(2,1)S(1)}, bf16[80,4096]{1,0:T(8,128)(2,1)S(1)}) custom-call(s32[1]{0:T(128)} %bitcast.1.expert_ref, bf16[64,4224]{1,0:T(8,128)(2,1)} %collective-permute-done.6.z_ref.zm_ref.meta_ref, bf16[64,4224]{1,0:T(8,128)(2,1)} %collective-permute-done.17.a_ref.am_ref.meta_ref, ...), custom_call_target="tpu_custom_call" | custom-call | flops 3925868544 | bytes 22282240 | tf_op jit(solution)/shard_map/pallas_call | solution.py:111
  74.7 1.8 %shard_map.67 = bf16[80,4224]{1,0:T(8,128)(2,1)S(1)} custom-call(s32[1]{0:T(128)} %bitcast.expert_ref, bf16[64,4224]{1,0:T(8,128)(2,1)} %collective-permute-done.8.z_ref.zm_ref.meta_ref, bf16[64,4224]{1,0:T(8,128)(2,1)S(1)} %collective-permute-done.9.a_ref.am_ref.meta_ref, bf16[64,4224]{1,0:T(8,128)(2,1)} %collective-permute-done.8.z_ref.zm_ref.meta_ref, ...), custom_call_target="tpu_custom_call" | custom-call | flops 86507520 | bytes 1622016 | tf_op jit(solution)/shard_map/pallas_call | solution.py:50
  76.5 1.3 collective-permute-start.10
  77.9 11.3 %shard_map.71 = (bf16[64,4096]{1,0:T(8,128)(2,1)S(1)}, bf16[64,4096]{1,0:T(8,128)(2,1)S(1)}, bf16[80,4096]{1,0:T(8,128)(2,1)S(1)}) custom-call(s32[1]{0:T(128)} %bitcast.1.expert_ref, bf16[64,4224]{1,0:T(8,128)(2,1)} %collective-permute-done.7.z_ref.zm_ref.meta_ref, bf16[64,4224]{1,0:T(8,128)(2,1)} %collective-permute-done.13.a_ref.am_ref.meta_ref, ...), custom_call_target="tpu_custom_call" | custom-call | flops 3925868544 | bytes 22282240 | tf_op jit(solution)/shard_map/pallas_call | solution.py:111
  90.8 1.4 collective-permute-start.1
  92.1 1.2 shard_map.75
  93.3 1.3 collective-permute-start.20
  94.6 11.3 %shard_map.68 = (bf16[64,4096]{1,0:T(8,128)(2,1)S(1)}, bf16[64,4096]{1,0:T(8,128)(2,1)S(1)}, bf16[80,4096]{1,0:T(8,128)(2,1)S(1)}) custom-call(s32[1]{0:T(128)} %bitcast.1.expert_ref, bf16[64,4224]{1,0:T(8,128)(2,1)} %collective-permute-done.8.z_ref.zm_ref.meta_ref, bf16[64,4224]{1,0:T(8,128)(2,1)S(1)} %collective-permute-done.9.a_ref.am_ref.meta_ref, ...), custom_call_target="tpu_custom_call" | custom-call | flops 3925868544 | bytes 22282240 | tf_op jit(solution)/shard_map/pallas_call | solution.py:111
  106.5 1.2 shard_map.72
  108.8 1.2 shard_map.76
  110.3 4.2 %collective-permute-done.1.b_ref.bm_ref = bf16[80,4224]{1,0:T(8,128)(2,1)S(1)} collective-permute-done((bf16[80,4224]{1,0:T(8,128)(2,1)S(1)}, bf16[80,4224]{1,0:T(8,128)(2,1)S(1)}, u32[]{:S(2)}, u32[]{:S(2)}) %collective-permute-start.1) | collective-permute-done | bytes 675872 | tf_op jit(solution)/shard_map/ppermute | solution.py:201
  114.5 11.4 %shard_map.65 = (bf16[64,4096]{1,0:T(8,128)(2,1)S(1)}, bf16[64,4096]{1,0:T(8,128)(2,1)S(1)}, bf16[80,4096]{1,0:T(8,128)(2,1)S(1)}) custom-call(s32[1]{0:T(128)} %bitcast.1.expert_ref, bf16[64,4224]{1,0:T(8,128)(2,1)S(1)} %copy-done.2, bf16[64,4224]{1,0:T(8,128)(2,1)S(1)} %collective-permute-done.a_ref.am_ref.meta_ref, ...), custom_call_target="tpu_custom_call" | custom-call | flops 3925868544 | bytes 22282240 | tf_op jit(solution)/shard_map/pallas_call | solution.py:111
  125.9 1.2 collective-permute-start.4
  127.5 1.3 collective-permute-start.12
  128.9 1.3 shard_map.77
  130.2 11.8 %collective-permute-done.4.got_ref = bf16[80,4096]{1,0:T(8,128)(2,1)S(1)} collective-permute-done((bf16[80,4096]{1,0:T(8,128)(2,1)S(1)}, bf16[80,4096]{1,0:T(8,128)(2,1)S(1)}, u32[]{:S(2)}, u32[]{:S(2)}) %collective-permute-start.4) | collective-permute-done | bytes 655392 | tf_op jit(solution)/shard_map/ppermute | solution.py:201
  142.5 1.7 %collective-permute-start.5 = (bf16[64,4096]{1,0:T(8,128)(2,1)S(1)}, bf16[64,4096]{1,0:T(8,128)(2,1)S(1)}, u32[]{:S(2)}, u32[]{:S(2)}) collective-permute-start(bf16[64,4096]{1,0:T(8,128)(2,1)S(1)} %shard_map.66), channel_id=1, source_target_pairs={{0,2},{1,5},{2,0},{3,7},{4,6},{5,1},{6,4},{7,3},{8,10},{9,13},{10,... | collective-permute-start | bytes 1572872 | tf_op jit(solution)/shard_map/ppermute | solution.py:198
  145.4 1.3 shard_map.78
  146.7 5.0 %collective-permute-done.5.refs_0_ = bf16[64,4096]{1,0:T(8,128)(2,1)S(1)} collective-permute-done((bf16[64,4096]{1,0:T(8,128)(2,1)S(1)}, bf16[64,4096]{1,0:T(8,128)(2,1)S(1)}, u32[]{:S(2)}, u32[]{:S(2)}) %collective-permute-start.5) | collective-permute-done | bytes 524320 | tf_op jit(solution)/shard_map/ppermute | solution.py:198
  151.7 8.3 %collective-permute-done.23.refs_1_ = bf16[64,4096]{1,0:T(8,128)(2,1)S(1)} collective-permute-done((bf16[64,4096]{1,0:T(8,128)(2,1)S(1)}, bf16[64,4096]{1,0:T(8,128)(2,1)S(1)}, u32[]{:S(2)}, u32[]{:S(2)}) %collective-permute-start.23) | collective-permute-done | bytes 524320 | tf_op jit(solution)/shard_map/ppermute | solution.py:204
  160.1 1.4 shard_map.79
  (52 shorter events, 11.3 us)
Async XLA Ops:
  0.0 6.6 %copy-start = (bf16[1,384,4096]{2,1,0:T(8,128)(2,1)S(1)}, bf16[1,384,4096]{2,1,0:T(8,128)(2,1)}, u32[]{:S(2)}) copy-start(bf16[1,384,4096]{2,1,0:T(8,128)(2,1)} %param.11) | copy-start | bytes 9437188
  0.0 6.6 %copy-start.3 = (f32[64,8]{0,1:T(8,128)S(1)}, f32[64,8]{0,1:T(8,128)}, u32[]{:S(2)}) copy-start(f32[64,8]{0,1:T(8,128)} %param.8) | copy-start | bytes 6148
  0.0 6.9 %copy-start.4 = (s32[64,8]{0,1:T(8,128)S(1)}, s32[64,8]{0,1:T(8,128)}, u32[]{:S(2)}) copy-start(s32[64,8]{0,1:T(8,128)} %param.7) | copy-start | bytes 6148
  6.1 56.5 %collective-permute-start.2 = (bf16[4096,768]{1,0:T(8,128)(2,1)}, bf16[4096,768]{1,0:T(8,128)(2,1)}, u32[]{:S(2)}, u32[]{:S(2)}) collective-permute-start(bf16[4096,768]{1,0:T(8,128)(2,1)} %pad_maximum_fusion.w0_ref), channel_id=1, source_target_pairs={{0,1},{1,0},{2,3},{3,2},{4,5},{5,4},{6,7},{7,6},{8,9},{9,8},{10,11... | collective-permute-start | bytes 18874376 | tf_op jit(solution)/shard_map/ppermute | solution.py:207
  6.6 56.0 %collective-permute-start.3 = (bf16[384,4096]{1,0:T(8,128)(2,1)S(1)}, bf16[384,4096]{1,0:T(8,128)(2,1)}, u32[]{:S(2)}, u32[]{:S(2)}) collective-permute-start(bf16[384,4096]{1,0:T(8,128)(2,1)S(1)} %bitcast.5), channel_id=1, source_target_pairs={{0,1},{1,0},{2,3},{3,2},{4,5},{5,4},{6,7},{7,6},{8,9},{9,8},{10,11... | collective-permute-start | bytes 9437192 | tf_op jit(solution)/shard_map/ppermute | solution.py:207
  8.2 0.8 copy-start.1
  9.0 17.6 %collective-permute-start.6 = (bf16[64,4224]{1,0:T(8,128)(2,1)S(1)}, bf16[64,4224]{1,0:T(8,128)(2,1)}, u32[]{:S(2)}, u32[]{:S(2)}) collective-permute-start(bf16[64,4224]{1,0:T(8,128)(2,1)S(1)} %pad_maximum_fusion.1.z_ref.zm_ref.meta_ref), channel_id=1, source_target_pairs={{0,8},{2,10},{4,12},{6,14},{8,16},{10,18},{12,20},{14,22},{16,24},... | collective-permute-start | bytes 1622024 | tf_op jit(solution)/shard_map/ppermute | solution.py:204
  26.6 15.8 %collective-permute-start.7 = (bf16[64,4224]{1,0:T(8,128)(2,1)}, bf16[64,4224]{1,0:T(8,128)(2,1)}, u32[]{:S(2)}, u32[]{:S(2)}) collective-permute-start(bf16[64,4224]{1,0:T(8,128)(2,1)} %collective-permute-done.6.z_ref.zm_ref.meta_ref), channel_id=1, source_target_pairs={{0,8},{2,10},{4,12},{6,14},{8,16},{10,18},{12,20},{14,22},{16,24},... | collective-permute-start | bytes 1622024 | tf_op jit(solution)/shard_map/ppermute | solution.py:204
  26.6 17.0 %collective-permute-start.17 = (bf16[64,4224]{1,0:T(8,128)(2,1)}, bf16[64,4224]{1,0:T(8,128)(2,1)}, u32[]{:S(2)}, u32[]{:S(2)}) collective-permute-start(bf16[64,4224]{1,0:T(8,128)(2,1)} %collective-permute-done.6.z_ref.zm_ref.meta_ref), channel_id=1, source_target_pairs={{0,2},{1,5},{2,0},{3,7},{4,6},{5,1},{6,4},{7,3},{8,10},{9,13},{10,... | collective-permute-start | bytes 1622024 | tf_op jit(solution)/shard_map/ppermute | solution.py:198
  42.4 14.8 %collective-permute-start.8 = (bf16[64,4224]{1,0:T(8,128)(2,1)}, bf16[64,4224]{1,0:T(8,128)(2,1)}, u32[]{:S(2)}, u32[]{:S(2)}) collective-permute-start(bf16[64,4224]{1,0:T(8,128)(2,1)} %collective-permute-done.7.z_ref.zm_ref.meta_ref), channel_id=1, source_target_pairs={{0,8},{2,10},{4,12},{6,14},{8,16},{10,18},{12,20},{14,22},{16,24},... | collective-permute-start | bytes 1622024 | tf_op jit(solution)/shard_map/ppermute | solution.py:204
  42.4 15.8 %collective-permute-start.13 = (bf16[64,4224]{1,0:T(8,128)(2,1)}, bf16[64,4224]{1,0:T(8,128)(2,1)}, u32[]{:S(2)}, u32[]{:S(2)}) collective-permute-start(bf16[64,4224]{1,0:T(8,128)(2,1)} %collective-permute-done.7.z_ref.zm_ref.meta_ref), channel_id=1, source_target_pairs={{0,2},{1,5},{2,0},{3,7},{4,6},{5,1},{6,4},{7,3},{8,10},{9,13},{10,... | collective-permute-start | bytes 1622024 | tf_op jit(solution)/shard_map/ppermute | solution.py:198
  43.6 18.2 %copy-start.2 = (bf16[64,4224]{1,0:T(8,128)(2,1)S(1)}, bf16[64,4224]{1,0:T(8,128)(2,1)}, u32[]{:S(2)}) copy-start(bf16[64,4224]{1,0:T(8,128)(2,1)} %copy-done.1) | copy-start | bytes 1622020
  45.7 16.1 %collective-permute-start.18 = (bf16[80,4224]{1,0:T(8,128)(2,1)S(1)}, bf16[80,4224]{1,0:T(8,128)(2,1)S(1)}, u32[]{:S(2)}, u32[]{:S(2)}) collective-permute-start(bf16[80,4224]{1,0:T(8,128)(2,1)S(1)} %shard_map.73), channel_id=1, source_target_pairs={{0,4},{1,3},{2,6},{3,1},{4,0},{5,7},{6,2},{7,5},{8,12},{9,11},{10,... | collective-permute-start | bytes 2027528 | tf_op jit(solution)/shard_map/ppermute | solution.py:201
  57.2 17.5 %collective-permute-start.9 = (bf16[64,4224]{1,0:T(8,128)(2,1)}, bf16[64,4224]{1,0:T(8,128)(2,1)S(1)}, u32[]{:S(2)}, u32[]{:S(2)}) collective-permute-start(bf16[64,4224]{1,0:T(8,128)(2,1)} %collective-permute-done.8.z_ref.zm_ref.meta_ref), channel_id=1, source_target_pairs={{0,2},{1,5},{2,0},{3,7},{4,6},{5,1},{6,4},{7,3},{8,10},{9,13},{10,... | collective-permute-start | bytes 1622024 | tf_op jit(solution)/shard_map/ppermute | solution.py:198
  60.2 17.7 %collective-permute-start.14 = (bf16[80,4224]{1,0:T(8,128)(2,1)S(1)}, bf16[80,4224]{1,0:T(8,128)(2,1)S(1)}, u32[]{:S(2)}, u32[]{:S(2)}) collective-permute-start(bf16[80,4224]{1,0:T(8,128)(2,1)S(1)} %shard_map.70), channel_id=1, source_target_pairs={{0,4},{1,3},{2,6},{3,1},{4,0},{5,7},{6,2},{7,5},{8,12},{9,11},{10,... | collective-permute-start | bytes 2027528 | tf_op jit(solution)/shard_map/ppermute | solution.py:201
  61.8 28.2 %collective-permute-start = (bf16[64,4224]{1,0:T(8,128)(2,1)S(1)}, bf16[64,4224]{1,0:T(8,128)(2,1)S(1)}, u32[]{:S(2)}, u32[]{:S(2)}) collective-permute-start(bf16[64,4224]{1,0:T(8,128)(2,1)S(1)} %copy-done.2), channel_id=1, source_target_pairs={{0,2},{1,5},{2,0},{3,7},{4,6},{5,1},{6,4},{7,3},{8,10},{9,13},{10,... | collective-permute-start | bytes 1622024 | tf_op jit(solution)/shard_map/ppermute | solution.py:198
  73.9 18.2 %collective-permute-start.19 = (bf16[80,4096]{1,0:T(8,128)(2,1)S(1)}, bf16[80,4096]{1,0:T(8,128)(2,1)S(1)}, u32[]{:S(2)}, u32[]{:S(2)}) collective-permute-start(bf16[80,4096]{1,0:T(8,128)(2,1)S(1)} %get-tuple-element.27), channel_id=1, source_target_pairs={{0,4},{1,3},{2,6},{3,1},{4,0},{5,7},{6,2},{7,5},{8,12},{9,11},{10,... | collective-permute-start | bytes 1966088 | tf_op jit(solution)/shard_map/ppermute | solution.py:201
  76.5 18.1 %collective-permute-start.10 = (bf16[80,4224]{1,0:T(8,128)(2,1)S(1)}, bf16[80,4224]{1,0:T(8,128)(2,1)S(1)}, u32[]{:S(2)}, u32[]{:S(2)}) collective-permute-start(bf16[80,4224]{1,0:T(8,128)(2,1)S(1)} %shard_map.67), channel_id=1, source_target_pairs={{0,4},{1,3},{2,6},{3,1},{4,0},{5,7},{6,2},{7,5},{8,12},{9,11},{10,... | collective-permute-start | bytes 2027528 | tf_op jit(solution)/shard_map/ppermute | solution.py:201
  89.2 17.3 %collective-permute-start.15 = (bf16[80,4096]{1,0:T(8,128)(2,1)S(1)}, bf16[80,4096]{1,0:T(8,128)(2,1)S(1)}, u32[]{:S(2)}, u32[]{:S(2)}) collective-permute-start(bf16[80,4096]{1,0:T(8,128)(2,1)S(1)} %get-tuple-element.24), channel_id=1, source_target_pairs={{0,4},{1,3},{2,6},{3,1},{4,0},{5,7},{6,2},{7,5},{8,12},{9,11},{10,... | collective-permute-start | bytes 1966088 | tf_op jit(solution)/shard_map/ppermute | solution.py:201
  90.8 23.7 %collective-permute-start.1 = (bf16[80,4224]{1,0:T(8,128)(2,1)S(1)}, bf16[80,4224]{1,0:T(8,128)(2,1)S(1)}, u32[]{:S(2)}, u32[]{:S(2)}) collective-permute-start(bf16[80,4224]{1,0:T(8,128)(2,1)S(1)} %shard_map.64), channel_id=1, source_target_pairs={{0,4},{1,3},{2,6},{3,1},{4,0},{5,7},{6,2},{7,5},{8,12},{9,11},{10,... | collective-permute-start | bytes 2027528 | tf_op jit(solution)/shard_map/ppermute | solution.py:201
  93.3 15.4 %collective-permute-start.20 = (bf16[64,4096]{1,0:T(8,128)(2,1)S(1)}, bf16[64,4096]{1,0:T(8,128)(2,1)S(1)}, u32[]{:S(2)}, u32[]{:S(2)}) collective-permute-start(bf16[64,4096]{1,0:T(8,128)(2,1)S(1)} %shard_map.75), channel_id=1, source_target_pairs={{0,2},{1,5},{2,0},{3,7},{4,6},{5,1},{6,4},{7,3},{8,10},{9,13},{10,... | collective-permute-start | bytes 1572872 | tf_op jit(solution)/shard_map/ppermute | solution.py:198
  105.9 21.2 %collective-permute-start.11 = (bf16[80,4096]{1,0:T(8,128)(2,1)S(1)}, bf16[80,4096]{1,0:T(8,128)(2,1)S(1)}, u32[]{:S(2)}, u32[]{:S(2)}) collective-permute-start(bf16[80,4096]{1,0:T(8,128)(2,1)S(1)} %get-tuple-element.21), channel_id=1, source_target_pairs={{0,4},{1,3},{2,6},{3,1},{4,0},{5,7},{6,2},{7,5},{8,12},{9,11},{10,... | collective-permute-start | bytes 1966088 | tf_op jit(solution)/shard_map/ppermute | solution.py:201
  107.7 21.2 %collective-permute-start.16 = (bf16[64,4096]{1,0:T(8,128)(2,1)S(1)}, bf16[64,4096]{1,0:T(8,128)(2,1)S(1)}, u32[]{:S(2)}, u32[]{:S(2)}) collective-permute-start(bf16[64,4096]{1,0:T(8,128)(2,1)S(1)} %shard_map.72), channel_id=1, source_target_pairs={{0,2},{1,5},{2,0},{3,7},{4,6},{5,1},{6,4},{7,3},{8,10},{9,13},{10,... | collective-permute-start | bytes 1572872 | tf_op jit(solution)/shard_map/ppermute | solution.py:198
  110.0 18.8 %collective-permute-start.21 = (bf16[64,4096]{1,0:T(8,128)(2,1)S(1)}, bf16[64,4096]{1,0:T(8,128)(2,1)S(1)}, u32[]{:S(2)}, u32[]{:S(2)}) collective-permute-start(bf16[64,4096]{1,0:T(8,128)(2,1)S(1)} %shard_map.76), channel_id=1, source_target_pairs={{0,8},{2,10},{4,12},{6,14},{8,16},{10,18},{12,20},{14,22},{16,24},... | collective-permute-start | bytes 1572872 | tf_op jit(solution)/shard_map/ppermute | solution.py:204
  125.9 16.2 %collective-permute-start.4 = (bf16[80,4096]{1,0:T(8,128)(2,1)S(1)}, bf16[80,4096]{1,0:T(8,128)(2,1)S(1)}, u32[]{:S(2)}, u32[]{:S(2)}) collective-permute-start(bf16[80,4096]{1,0:T(8,128)(2,1)S(1)} %get-tuple-element.18), channel_id=1, source_target_pairs={{0,4},{1,3},{2,6},{3,1},{4,0},{5,7},{6,2},{7,5},{8,12},{9,11},{10,... | collective-permute-start | bytes 1966088 | tf_op jit(solution)/shard_map/ppermute | solution.py:201
  127.5 16.7 %collective-permute-start.12 = (bf16[64,4096]{1,0:T(8,128)(2,1)S(1)}, bf16[64,4096]{1,0:T(8,128)(2,1)S(1)}, u32[]{:S(2)}, u32[]{:S(2)}) collective-permute-start(bf16[64,4096]{1,0:T(8,128)(2,1)S(1)} %shard_map.69), channel_id=1, source_target_pairs={{0,2},{1,5},{2,0},{3,7},{4,6},{5,1},{6,4},{7,3},{8,10},{9,13},{10,... | collective-permute-start | bytes 1572872 | tf_op jit(solution)/shard_map/ppermute | solution.py:198
  130.2 15.2 %collective-permute-start.22 = (bf16[64,4096]{1,0:T(8,128)(2,1)S(1)}, bf16[64,4096]{1,0:T(8,128)(2,1)S(1)}, u32[]{:S(2)}, u32[]{:S(2)}) collective-permute-start(bf16[64,4096]{1,0:T(8,128)(2,1)S(1)} %shard_map.77), channel_id=1, source_target_pairs={{0,8},{2,10},{4,12},{6,14},{8,16},{10,18},{12,20},{14,22},{16,24},... | collective-permute-start | bytes 1572872 | tf_op jit(solution)/shard_map/ppermute | solution.py:204
  142.5 9.2 %collective-permute-start.5 = (bf16[64,4096]{1,0:T(8,128)(2,1)S(1)}, bf16[64,4096]{1,0:T(8,128)(2,1)S(1)}, u32[]{:S(2)}, u32[]{:S(2)}) collective-permute-start(bf16[64,4096]{1,0:T(8,128)(2,1)S(1)} %shard_map.66), channel_id=1, source_target_pairs={{0,2},{1,5},{2,0},{3,7},{4,6},{5,1},{6,4},{7,3},{8,10},{9,13},{10,... | collective-permute-start | bytes 1572872 | tf_op jit(solution)/shard_map/ppermute | solution.py:198
  146.7 13.4 %collective-permute-start.23 = (bf16[64,4096]{1,0:T(8,128)(2,1)S(1)}, bf16[64,4096]{1,0:T(8,128)(2,1)S(1)}, u32[]{:S(2)}, u32[]{:S(2)}) collective-permute-start(bf16[64,4096]{1,0:T(8,128)(2,1)S(1)} %shard_map.78), channel_id=1, source_target_pairs={{0,8},{2,10},{4,12},{6,14},{8,16},{10,18},{12,20},{14,22},{16,24},... | collective-permute-start | bytes 1572872 | tf_op jit(solution)/shard_map/ppermute | solution.py:204

commit v3 on v0

v3 whole, which is shorter than its diff:
```python
import functools

import jax
import jax.numpy as jnp
from jax import lax
from jax.experimental import pallas as pl
from jax.experimental.pallas import tpu as pltpu
from jax.sharding import PartitionSpec as P

BF = jnp.bfloat16
F32 = jnp.float32
META = 128


def named_by(meta, expert, top):
    ids = meta[:, :top].astype(F32)
    return (ids == expert.astype(F32)).astype(F32)


def weight_for(meta, expert, top):
    m = meta.astype(F32)
    parts = m[:, top : 2 * top] + m[:, 2 * top : 3 * top] + m[:, 3 * top : 4 * top]
    return jnp.sum(named_by(meta, expert, top) * parts, axis=1, keepdims=True)


def one_hot(meta, expert, top, slots):
    rows = meta.shape[0]
    named = jnp.sum(named_by(meta, expert, top), axis=1, keepdims=True)
    below = lax.broadcasted_iota(jnp.int32, (rows, rows), 0) > lax.broadcasted_iota(jnp.int32, (rows, rows), 1)
    wide = jnp.broadcast_to(named, (rows, slots)).astype(BF)
    rank = jnp.dot(below.astype(F32).astype(BF), wide, preferred_element_type=F32)
    slot = lax.broadcasted_iota(jnp.int32, (rows, slots), 1).astype(F32)
    hit = jnp.logical_and(rank == slot, named > 0.5)
    return hit.astype(F32).astype(BF)


def whole_specs(n):
    return [pl.BlockSpec(memory_space=pltpu.SMEM)] + [pl.BlockSpec(memory_space=pltpu.VMEM)] * n


def select_kernel(top, slots, experts_ref, z_ref, *out_refs):
    width = z_ref.shape[1] - META
    for i, out_ref in enumerate(out_refs):
        pick = one_hot(z_ref[:, width:], experts_ref[1 + i], top, slots)
        rows = lax.dot_general(pick, z_ref[...], (((0,), (0,)), ((), ())), preferred_element_type=F32)
        out_ref[...] = rows.astype(BF)


def select(experts, z, top, slots):
    rows, wide = z.shape
    return pl.pallas_call(
        functools.partial(select_kernel, top, slots),
        out_shape=[jax.ShapeDtypeStruct((slots, wide), BF)] * 3,
        in_specs=whole_specs(1),
        out_specs=[pl.BlockSpec(memory_space=pltpu.VMEM)] * 3,
        compiler_params=pltpu.CompilerParams(vmem_limit_bytes=12 << 20),
        cost_estimate=pl.CostEstimate(flops=6 * slots * rows * wide, bytes_accessed=6 * rows * wide, transcendentals=0),
    )(experts, z)


def prepare_kernel(ids_ref, weights_ref, tokens_ref, out_ref):
    weights = weights_ref[...]
    high = weights.astype(BF).astype(F32)
    middle = (weights - high).astype(BF).astype(F32)
    low = weights - high - middle
    rows, width = tokens_ref.shape
    rest = jnp.zeros((rows, META - 4 * weights.shape[1]), F32)
    meta = jnp.concatenate([ids_ref[...].astype(F32), high, middle, low, rest], axis=1)
    out_ref[:, :width] = tokens_ref[...]
    out_ref[:, width:] = meta.astype(BF)


def prepare(ids, weights, tokens):
    rows, width = tokens.shape
    return pl.pallas_call(
        prepare_kernel,
        out_shape=jax.ShapeDtypeStruct((rows, width + META), BF),
        in_specs=[pl.BlockSpec(memory_space=pltpu.VMEM)] * 3,
        out_specs=pl.BlockSpec(memory_space=pltpu.VMEM),
        compiler_params=pltpu.CompilerParams(vmem_limit_bytes=12 << 20),
        cost_estimate=pl.CostEstimate(flops=rows, bytes_accessed=4 * rows * width, transcendentals=0),
    )(ids, weights, tokens)


def stage_kernel(gate_ref, up_ref, down_ref, joined_ref, held_ref, sems):
    ff = down_ref.shape[0]
    copies = [
        pltpu.make_async_copy(gate_ref, joined_ref.at[:, pl.ds(0, ff)], sems.at[0]),
        pltpu.make_async_copy(up_ref, joined_ref.at[:, pl.ds(ff, ff)], sems.at[1]),
        pltpu.make_async_copy(down_ref, held_ref, sems.at[2]),
    ]
    for copy in copies:
        copy.start()
    for copy in copies:
        copy.wait()


def stage(gate, up, down):
    width, ff = gate.shape
    return pl.pallas_call(
        stage_kernel,
        out_shape=[pltpu.VMEM((width, 2 * ff), BF), pltpu.VMEM(down.shape, BF)],
        in_specs=[pl.BlockSpec(memory_space=pl.ANY)] * 3,
        out_specs=[pl.BlockSpec(memory_space=pltpu.VMEM)] * 2,
        scratch_shapes=[pltpu.SemaphoreType.DMA((3,))],
        compiler_params=pltpu.CompilerParams(vmem_limit_bytes=12 << 20),
        cost_estimate=pl.CostEstimate(flops=width, bytes_accessed=12 * width * ff, transcendentals=0),
    )(gate, up, down)


def expert_kernel(top, pitch, experts_ref, *refs):
    blocks, (w0_ref, d0_ref, w1_ref, d1_ref), outs, (x, hid) = refs[:4], refs[4:8], refs[8:12], refs[12:]
    expert = experts_ref[0]
    rows = blocks[0].shape[0]
    width = w0_ref.shape[0]
    ff = d0_ref.shape[0]
    spans = [(0, rows)] + [(rows + i * pitch, blocks[1].shape[0]) for i in range(3)]
    if pitch > blocks[1].shape[0]:
        x[rows:] = jnp.zeros_like(x[rows:])
    for block, (first, count) in zip(blocks, spans):
        x[first : first + count] = block[:, :width]
    for c, w_ref in enumerate((w0_ref, w1_ref)):
        both = jnp.dot(x[...], w_ref[...], preferred_element_type=F32)
        gate = both[:, :ff]
        hid[:, c * ff : (c + 1) * ff] = (gate / (1.0 + jnp.exp(-gate)) * both[:, ff:]).astype(BF)
    scales = [weight_for(block[:, width:], expert, top) for block in blocks]
    tile = 1024
    for n in range(width // tile):
        s = slice(n * tile, (n + 1) * tile)
        out = jnp.dot(hid[:, :ff], d0_ref[:, s], preferred_element_type=F32)
        out = out + jnp.dot(hid[:, ff:], d1_ref[:, s], preferred_element_type=F32)
        for ref, scale, (first, count) in zip(outs, scales, spans):
            ref[:, s] = (out[first : first + count] * scale).astype(BF)


def run_expert(experts, blocks, weights, top):
    rows, wide = blocks[0].shape
    slots = blocks[1].shape[0]
    width = weights[0].shape[0]
    ff = weights[1].shape[0]
    pitch = -(-slots // 16) * 16
    total = rows + 3 * pitch
    return pl.pallas_call(
        functools.partial(expert_kernel, top, pitch),
        out_shape=[jax.ShapeDtypeStruct((block.shape[0], width), BF) for block in blocks],
        in_specs=whole_specs(8),
        out_specs=[pl.BlockSpec(memory_space=pltpu.VMEM)] * 4,
        scratch_shapes=[pltpu.VMEM((total, width), BF), pltpu.VMEM((total, 2 * ff), BF)],
        compiler_params=pltpu.CompilerParams(vmem_limit_bytes=14 << 20),
        cost_estimate=pl.CostEstimate(
            flops=12 * total * width * ff, bytes_accessed=4 * total * width, transcendentals=2 * total * ff
        ),
    )(experts, *blocks, *weights)


def put_back_kernel(top, slots, n_more, experts_ref, own_ref, block_ref, *refs):
    got, more, out_ref = refs[:3], refs[3 : 3 + n_more], refs[3 + n_more]
    width = own_ref.shape[1]
    total = own_ref[...].astype(F32)
    for i, ref in enumerate(got):
        place = one_hot(block_ref[:, width:], experts_ref[1 + i], top, slots)
        total = total + jnp.dot(place, ref[...], preferred_element_type=F32)
    for ref in more:
        total = total + ref[...].astype(F32)
    out_ref[...] = total.astype(BF)


def put_back(experts, own, block, got, more, top):
    rows, width = own.shape
    slots = got[0].shape[0]
    return pl.pallas_call(
        functools.partial(put_back_kernel, top, slots, len(more)),
        out_shape=jax.ShapeDtypeStruct((rows, width), BF),
        in_specs=whole_specs(5 + len(more)),
        out_specs=pl.BlockSpec(memory_space=pltpu.VMEM),
        compiler_params=pltpu.CompilerParams(vmem_limit_bytes=12 << 20),
        cost_estimate=pl.CostEstimate(
            flops=6 * slots * rows * width, bytes_accessed=(8 + 2 * len(more)) * rows * width, transcendentals=0
        ),
    )(experts, own, block, *got, *more)


def on_device(tokens, expert_ids, route_weights, gate_proj, up_proj, down_proj):
    rows, width = tokens.shape
    top = expert_ids.shape[1]
    n_ep = lax.axis_size("ep")
    ring = n_ep // 4
    cap = max(2, min(rows, rows * top * 5 // (4 * n_ep)))
    slots = -(-cap // 8) * 8
    me = lax.axis_index("ep").astype(jnp.int32)

    def swap(x):
        return lax.ppermute(x, "etp", [(0, 1), (1, 0)])

    def hop_z(x):
        return lax.ppermute(x, "ep", [(i, (i + 4) % n_ep) for i in range(n_ep)])

    def spread(arrays):
        return [
            lax.ppermute(x, "ep", [(i, i ^ flip) for i in range(n_ep)]) for flip, x in zip((1, 2, 3), arrays)
        ]

    def after(x, *others):
        return lax.optimization_barrier((x, *others))[0]

    experts = jnp.stack([me, me ^ 1, me ^ 2, me ^ 3])
    block = prepare(expert_ids, route_weights, tokens)
    half = (gate_proj[0], up_proj[0], down_proj[0])
    other = [swap(x) for x in half]

    levels, given, results, weights = [block], [], [], []

    def compute(k):
        if not weights:
            weights.extend([*stage(*after(half, levels[1])), *stage(*other)])
        mine = after(given[k], results[-1][0]) if results else given[k]
        results.append(run_expert(experts, [levels[k], *mine], weights, top))

    for k in range(ring):
        z = levels[k]
        if k:
            z = levels[k] = after(z, given[k - 1])
        if k > 1:
            compute(k - 2)
        if k + 1 < ring:
            levels.append(hop_z(z))
        given.append(spread(select(experts, z, top, slots)))

    carry = None
    returned = None
    for k in [*range(1, ring), 0]:
        while len(results) < min(ring, k + 2):
            compute(len(results))
        pz, *out = results[k]
        returned = spread(out)
        carry = put_back(experts, pz, levels[k], returned, [] if carry is None else [hop_z(carry)], top)
    return carry
def solution(mesh):
    in_specs = (
        P(("groups", "ep", "etp"), None),
        P(("groups", "ep", "etp"), None),
        P(("groups", "ep", "etp"), None),
        P("ep", None, "etp"),
        P("ep", None, "etp"),
        P("ep", "etp", None),
    )
    out_specs = P(("groups", "ep", "etp"), None)
    return jax.shard_map(
        on_device, mesh=mesh, in_specs=in_specs, out_specs=out_specs, check_vma=False
    )
```

time: 396 us -> 158 us (0.40)
  blocking collectives: 121 us -> 0 us
  waiting for transfers between devices: 174 us -> 69.3 us
  Pallas kernels: 0 us -> 39.8 us
  starting transfers between devices: 7.13 us -> 38.3 us
  matrix products: 29 us -> 0 us
  local copies, waits for them, and re-layouts: 34.5 us -> 8.25 us
  other arithmetic: 15.6 us -> 0.08 us
  between operations: 13.4 us -> 0.15 us
    all_to_all x1 -> x0, blocking collectives: 121 us -> none  [on_device(): lax.all_to_all(outgoing, 'ep', split_axis=0, concat_axis=0, tiled=True)]
    all_to_all x1 -> x0, waiting for transfers between devices: 119 us -> none  [on_device(): lax.all_to_all(back, 'ep', split_axis=0, concat_axis=0, tiled=True)]
    ppermute x0 -> x33, waiting for transfers between devices: none -> 69.3 us  [the longest x24 64.4 us: spread(): lax.ppermute(x, 'ep', [(i, i ^ flip) for i in range(n_ep)])]
    pallas_call x0 -> x15, Pallas kernels: none -> 39.8 us  [the longest x4 21.4 us: run_expert(): pl.pallas_call(functools.partial(expert_kernel, top, pitch), out_shape=[j...]
    ppermute x0 -> x33, starting transfers between devices: none -> 38.3 us  [the longest x24 23.6 us: spread(): lax.ppermute(x, 'ep', [(i, i ^ flip) for i in range(n_ep)])]
    reduce_scatter x1 -> x0, waiting for transfers between devices: 32.1 us -> none  [on_device(): lax.psum_scatter(jnp.dot(hidden, w_down, preferred_element_type=jnp.float...]
    dot_general x2 -> x0, matrix products: 29 us -> none  [the longest x1 18.8 us: on_device(): jnp.dot(hidden, w_down, preferred_element_type=jnp.float32)]
    all_gather x1 -> x0, waiting for transfers between devices: 23.2 us -> none  [on_device(): piece = lax.all_gather(rows, 'etp', axis=0, tiled=True)]
  transfers between devices with their start and end apart: 3 -> 33, of which waited for: 3 -> 14; matrix products, arithmetic and copies ran while one was open for 0% -> 1% of each run, Pallas kernels for 0% -> 22%
where the time goes in v3:
time: 158 us; the launch traced here: 156 us
  waiting for transfers between devices  69.3 us (44%)
  Pallas kernels  39.8 us (25%)
  starting transfers between devices  38.3 us (24%)
  local copies, waits for them, and re-layouts  8.25 us (5%)
    ppermute x24, waiting for transfers between devices, spread(): lax.ppermute(x, 'ep', [(i, i ^ flip) for i in range(n_ep)])  64.4 us
    ppermute x24, starting transfers between devices, spread(): lax.ppermute(x, 'ep', [(i, i ^ flip) for i in range(n_ep)])  23.6 us
    pallas_call x4, Pallas kernels, run_expert(): pl.pallas_call(functools.partial(expert_kernel, top, pitch), out_shape=[j...  21.4 us
    ppermute x6, starting transfers between devices, hop_z(): return lax.ppermute(x, 'ep', [(i, (i + 4) % n_ep) for i in range(n_ep)])  14.1 us
    unnamed x10, local copies, waits for them, and re-layouts  8.25 us
    pallas_call x4, Pallas kernels, put_back(): pl.pallas_call(functools.partial(put_back_kernel, top, slots, len(more)),...  7.1 us
    pallas_call x4, Pallas kernels, select(): pl.pallas_call(functools.partial(select_kernel, top, slots), out_shape=[j...  6.58 us
    ppermute x6, waiting for transfers between devices, hop_z(): return lax.ppermute(x, 'ep', [(i, (i + 4) % n_ep) for i in range(n_ep)])  4.85 us
  transfers between devices with their start and end apart: 33, of which 14 were waited for; matrix products, arithmetic and copies ran while one was open for 1% of the time, Pallas kernels for 22%

profile of v3, /device:TPU:14, one launch (start us, length us, event | category | flops | bytes accessed | tf_op | source)
XLA Modules:
  0.0 155.8 jit_solution(4475717540714224498)
XLA Ops:
  6.0 9.3 %collective-permute-done.refs_1_ = bf16[40,4224]{1,0:T(8,128)(2,1)S(1)} collective-permute-done((bf16[40,4224]{1,0:T(8,128)(2,1)S(1)}, bf16[40,4224]{1,0:T(8,128)(2,1)S(1)}, u32[]{:S(2)}, u32[]{:S(2)}) %collective-permute-start) | collective-permute-done | bytes 337952 | tf_op jit(solution)/shard_map/ppermute | solution.py:200
  17.4 9.7 %collective-permute-done.2.refs_3_ = bf16[40,4224]{1,0:T(8,128)(2,1)S(1)} collective-permute-done((bf16[40,4224]{1,0:T(8,128)(2,1)S(1)}, bf16[40,4224]{1,0:T(8,128)(2,1)S(1)}, u32[]{:S(2)}, u32[]{:S(2)}) %collective-permute-start.2) | collective-permute-done | bytes 337952 | tf_op jit(solution)/shard_map/ppermute | solution.py:200
  27.1 2.1 %collective-permute-done.3.z_ref.refs_0_.block_ref = bf16[64,4224]{1,0:T(8,128)(2,1)S(1)} collective-permute-done((bf16[64,4224]{1,0:T(8,128)(2,1)S(1)}, bf16[64,4224]{1,0:T(8,128)(2,1)S(1)}, u32[]{:S(2)}, u32[]{:S(2)}) %collective-permute-start.3) | collective-permute-done | bytes 540704 | tf_op jit(solution)/shard_map/ppermute | solution.py:196
  29.3 1.6 %shard_map.69 = (bf16[40,4224]{1,0:T(8,128)(2,1)S(1)}, bf16[40,4224]{1,0:T(8,128)(2,1)S(1)}, bf16[40,4224]{1,0:T(8,128)(2,1)S(1)}) custom-call(s32[4]{0:T(128)S(1)} %pad_add_fusion.experts_ref, bf16[64,4224]{1,0:T(8,128)(2,1)S(1)} %collective-permute-done.3.z_ref.refs_0_.block_ref), custom_call_target="tpu_custom_call" | custom-call | flops 64880640 | bytes 1622016 | tf_op jit(solution)/shard_map/pallas_call | solution.py:51
  32.0 7.7 %collective-permute-done.11.refs_1_ = bf16[40,4224]{1,0:T(8,128)(2,1)S(1)} collective-permute-done((bf16[40,4224]{1,0:T(8,128)(2,1)S(1)}, bf16[40,4224]{1,0:T(8,128)(2,1)S(1)}, u32[]{:S(2)}, u32[]{:S(2)}) %collective-permute-start.11) | collective-permute-done | bytes 337952 | tf_op jit(solution)/shard_map/ppermute | solution.py:200
  41.7 1.9 %copy-done = bf16[1,4096,384]{2,1,0:T(8,128)(2,1)S(1)} copy-done((bf16[1,4096,384]{2,1,0:T(8,128)(2,1)S(1)}, bf16[1,4096,384]{2,1,0:T(8,128)(2,1)}, u32[]{:S(2)}) %copy-start) | copy-done | bytes 3145752
  43.6 1.9 %copy-done.1 = bf16[1,4096,384]{2,1,0:T(8,128)(2,1)S(1)} copy-done((bf16[1,4096,384]{2,1,0:T(8,128)(2,1)S(1)}, bf16[1,4096,384]{2,1,0:T(8,128)(2,1)}, u32[]{:S(2)}) %copy-start.1) | copy-done | bytes 3145752
  45.5 1.9 %copy-done.2 = bf16[1,384,4096]{2,1,0:T(8,128)(2,1)S(1)} copy-done((bf16[1,384,4096]{2,1,0:T(8,128)(2,1)S(1)}, bf16[1,384,4096]{2,1,0:T(8,128)(2,1)}, u32[]{:S(2)}) %copy-start.2) | copy-done | bytes 3145752
  49.6 2.7 %collective-permute-done.10.z_ref.refs_0_.block_ref = bf16[64,4224]{1,0:T(8,128)(2,1)S(1)} collective-permute-done((bf16[64,4224]{1,0:T(8,128)(2,1)S(1)}, bf16[64,4224]{1,0:T(8,128)(2,1)S(1)}, u32[]{:S(2)}, u32[]{:S(2)}) %collective-permute-start.10) | collective-permute-done | bytes 540704 | tf_op jit(solution)/shard_map/ppermute | solution.py:196
  56.1 2.8 %collective-permute-start.17 = (bf16[40,4224]{1,0:T(8,128)(2,1)S(1)}, bf16[40,4224]{1,0:T(8,128)(2,1)S(1)}, u32[]{:S(2)}, u32[]{:S(2)}) collective-permute-start(bf16[40,4224]{1,0:T(8,128)(2,1)S(1)} %get-tuple-element.73), channel_id=1, source_target_pairs={{0,6},{2,4},{4,2},{6,0},{8,14},{10,12},{12,10},{14,8},{16,22},{18,... | collective-permute-start | bytes 1013768 | tf_op jit(solution)/shard_map/ppermute | solution.py:200
  58.9 3.8 %shard_map.67 = (bf16[4096,768]{1,0:T(8,128)(2,1)S(1)}, bf16[384,4096]{1,0:T(8,128)(2,1)S(1)}) custom-call(bf16[4096,384]{1,0:T(8,128)(2,1)} %collective-permute-done.4.gate_ref, bf16[4096,384]{1,0:T(8,128)(2,1)} %collective-permute-done.5.up_ref, bf16[384,4096]{1,0:T(8,128)(2,1)} %collective-permute-done.6.down_ref), custom_call_target="tpu_custom_call" | custom-call | flops 4096 | bytes 18874368 | tf_op jit(solution)/shard_map/pallas_call | solution.py:100
  62.7 5.3 %shard_map.68 = (bf16[64,4096]{1,0:T(8,128)(2,1)S(1)}, bf16[40,4096]{1,0:T(8,128)(2,1)S(1)}, bf16[40,4096]{1,0:T(8,128)(2,1)S(1)}, bf16[40,4096]{1,0:T(8,128)(2,1)S(1)}) custom-call(s32[4]{0:T(128)S(1)} %pad_add_fusion.experts_ref, bf16[64,4224]{1,0:T(8,128)(2,1)S(1)} %shard_map.64.z_ref.refs_0_.block_ref, ...), custom_call_target="tpu_custom_call" | custom-call | flops 3925868544 | bytes 3407872 | tf_op jit(solution)/shard_map/pallas_call | solution.py:143
  68.0 5.3 %shard_map.72 = (bf16[64,4096]{1,0:T(8,128)(2,1)S(1)}, bf16[40,4096]{1,0:T(8,128)(2,1)S(1)}, bf16[40,4096]{1,0:T(8,128)(2,1)S(1)}, bf16[40,4096]{1,0:T(8,128)(2,1)S(1)}) custom-call(s32[4]{0:T(128)S(1)} %pad_add_fusion.experts_ref, bf16[64,4224]{1,0:T(8,128)(2,1)S(1)} %collective-permute-done.3.z_ref.refs_0_.block_ref, ...), custom_call_target="tpu_custom_call" | custom-call | flops 3925868544 | bytes 3407872 | tf_op jit(solution)/shard_map/pallas_call | solution.py:143
  74.1 2.8 %collective-permute-start.29 = (bf16[40,4096]{1,0:T(8,128)(2,1)S(1)}, bf16[40,4096]{1,0:T(8,128)(2,1)S(1)}, u32[]{:S(2)}, u32[]{:S(2)}) collective-permute-start(bf16[40,4096]{1,0:T(8,128)(2,1)S(1)} %get-tuple-element.98), channel_id=1, source_target_pairs={{0,6},{2,4},{4,2},{6,0},{8,14},{10,12},{12,10},{14,8},{16,22},{18,... | collective-permute-start | bytes 983048 | tf_op jit(solution)/shard_map/ppermute | solution.py:200
  76.9 1.7 %shard_map.71 = (bf16[40,4224]{1,0:T(8,128)(2,1)S(1)}, bf16[40,4224]{1,0:T(8,128)(2,1)S(1)}, bf16[40,4224]{1,0:T(8,128)(2,1)S(1)}) custom-call(s32[4]{0:T(128)S(1)} %pad_add_fusion.experts_ref, bf16[64,4224]{1,0:T(8,128)(2,1)S(1)} %collective-permute-done.14.z_ref.refs_0_.block_ref), custom_call_target="tpu_custom_call" | custom-call | flops 64880640 | bytes 1622016 | tf_op jit(solution)/shard_map/pallas_call | solution.py:51
  79.3 4.8 %collective-permute-done.27.refs_0_ = bf16[40,4096]{1,0:T(8,128)(2,1)S(1)} collective-permute-done((bf16[40,4096]{1,0:T(8,128)(2,1)S(1)}, bf16[40,4096]{1,0:T(8,128)(2,1)S(1)}, u32[]{:S(2)}, u32[]{:S(2)}) %collective-permute-start.27) | collective-permute-done | bytes 327712 | tf_op jit(solution)/shard_map/ppermute | solution.py:200
  84.2 7.2 %collective-permute-done.28.refs_1_ = bf16[40,4096]{1,0:T(8,128)(2,1)S(1)} collective-permute-done((bf16[40,4096]{1,0:T(8,128)(2,1)S(1)}, bf16[40,4096]{1,0:T(8,128)(2,1)S(1)}, u32[]{:S(2)}, u32[]{:S(2)}) %collective-permute-start.28) | collective-permute-done | bytes 327712 | tf_op jit(solution)/shard_map/ppermute | solution.py:200
  93.0 1.9 %collective-permute-start.30 = (bf16[64,4096]{1,0:T(8,128)(2,1)S(1)}, bf16[64,4096]{1,0:T(8,128)(2,1)S(1)}, u32[]{:S(2)}, u32[]{:S(2)}) collective-permute-start(bf16[64,4096]{1,0:T(8,128)(2,1)S(1)} %shard_map.75), channel_id=1, source_target_pairs={{0,8},{2,10},{4,12},{6,14},{8,16},{10,18},{12,20},{14,22},{16,24},... | collective-permute-start | bytes 1572872 | tf_op jit(solution)/shard_map/ppermute | solution.py:196
  94.8 5.4 %shard_map.73 = (bf16[64,4096]{1,0:T(8,128)(2,1)S(1)}, bf16[40,4096]{1,0:T(8,128)(2,1)S(1)}, bf16[40,4096]{1,0:T(8,128)(2,1)S(1)}, bf16[40,4096]{1,0:T(8,128)(2,1)S(1)}) custom-call(s32[4]{0:T(128)S(1)} %pad_add_fusion.experts_ref, bf16[64,4224]{1,0:T(8,128)(2,1)S(1)} %collective-permute-done.10.z_ref.refs_0_.block_ref, ...), custom_call_target="tpu_custom_call" | custom-call | flops 3925868544 | bytes 3407872 | tf_op jit(solution)/shard_map/pallas_call | solution.py:143
  102.3 3.5 %collective-permute-start.26 = (bf16[40,4096]{1,0:T(8,128)(2,1)S(1)}, bf16[40,4096]{1,0:T(8,128)(2,1)S(1)}, u32[]{:S(2)}, u32[]{:S(2)}) collective-permute-start(bf16[40,4096]{1,0:T(8,128)(2,1)S(1)} %get-tuple-element.95), channel_id=1, source_target_pairs={{0,6},{2,4},{4,2},{6,0},{8,14},{10,12},{12,10},{14,8},{16,22},{18,... | collective-permute-start | bytes 983048 | tf_op jit(solution)/shard_map/ppermute | solution.py:200
  105.7 4.9 %collective-permute-done.24.refs_0_ = bf16[40,4096]{1,0:T(8,128)(2,1)S(1)} collective-permute-done((bf16[40,4096]{1,0:T(8,128)(2,1)S(1)}, bf16[40,4096]{1,0:T(8,128)(2,1)S(1)}, u32[]{:S(2)}, u32[]{:S(2)}) %collective-permute-start.24) | collective-permute-done | bytes 327712 | tf_op jit(solution)/shard_map/ppermute | solution.py:200
  110.7 3.7 %collective-permute-done.25.refs_1_ = bf16[40,4096]{1,0:T(8,128)(2,1)S(1)} collective-permute-done((bf16[40,4096]{1,0:T(8,128)(2,1)S(1)}, bf16[40,4096]{1,0:T(8,128)(2,1)S(1)}, u32[]{:S(2)}, u32[]{:S(2)}) %collective-permute-start.25) | collective-permute-done | bytes 327712 | tf_op jit(solution)/shard_map/ppermute | solution.py:200
  115.9 1.8 %collective-permute-start.31 = (bf16[64,4096]{1,0:T(8,128)(2,1)S(1)}, bf16[64,4096]{1,0:T(8,128)(2,1)S(1)}, u32[]{:S(2)}, u32[]{:S(2)}) collective-permute-start(bf16[64,4096]{1,0:T(8,128)(2,1)S(1)} %shard_map.76), channel_id=1, source_target_pairs={{0,8},{2,10},{4,12},{6,14},{8,16},{10,18},{12,20},{14,22},{16,24},... | collective-permute-start | bytes 1572872 | tf_op jit(solution)/shard_map/ppermute | solution.py:196
  117.8 5.3 %shard_map.74 = (bf16[64,4096]{1,0:T(8,128)(2,1)S(1)}, bf16[40,4096]{1,0:T(8,128)(2,1)S(1)}, bf16[40,4096]{1,0:T(8,128)(2,1)S(1)}, bf16[40,4096]{1,0:T(8,128)(2,1)S(1)}) custom-call(s32[4]{0:T(128)S(1)} %pad_add_fusion.experts_ref, bf16[64,4224]{1,0:T(8,128)(2,1)S(1)} %collective-permute-done.14.z_ref.refs_0_.block_ref, ...), custom_call_target="tpu_custom_call" | custom-call | flops 3925868544 | bytes 3407872 | tf_op jit(solution)/shard_map/pallas_call | solution.py:143
  125.0 1.7 %collective-permute-start.23 = (bf16[40,4096]{1,0:T(8,128)(2,1)S(1)}, bf16[40,4096]{1,0:T(8,128)(2,1)S(1)}, u32[]{:S(2)}, u32[]{:S(2)}) collective-permute-start(bf16[40,4096]{1,0:T(8,128)(2,1)S(1)} %get-tuple-element.92), channel_id=1, source_target_pairs={{0,6},{2,4},{4,2},{6,0},{8,14},{10,12},{12,10},{14,8},{16,22},{18,... | collective-permute-start | bytes 983048 | tf_op jit(solution)/shard_map/ppermute | solution.py:200
  126.7 3.6 %collective-permute-done.21.refs_0_ = bf16[40,4096]{1,0:T(8,128)(2,1)S(1)} collective-permute-done((bf16[40,4096]{1,0:T(8,128)(2,1)S(1)}, bf16[40,4096]{1,0:T(8,128)(2,1)S(1)}, u32[]{:S(2)}, u32[]{:S(2)}) %collective-permute-start.21) | collective-permute-done | bytes 327712 | tf_op jit(solution)/shard_map/ppermute | solution.py:200
  130.2 4.8 %collective-permute-done.22.refs_1_ = bf16[40,4096]{1,0:T(8,128)(2,1)S(1)} collective-permute-done((bf16[40,4096]{1,0:T(8,128)(2,1)S(1)}, bf16[40,4096]{1,0:T(8,128)(2,1)S(1)}, u32[]{:S(2)}, u32[]{:S(2)}) %collective-permute-start.22) | collective-permute-done | bytes 327712 | tf_op jit(solution)/shard_map/ppermute | solution.py:200
  136.6 5.9 %collective-permute-start.32 = (bf16[64,4096]{1,0:T(8,128)(2,1)S(1)}, bf16[64,4096]{1,0:T(8,128)(2,1)S(1)}, u32[]{:S(2)}, u32[]{:S(2)}) collective-permute-start(bf16[64,4096]{1,0:T(8,128)(2,1)S(1)} %shard_map.77), channel_id=1, source_target_pairs={{0,8},{2,10},{4,12},{6,14},{8,16},{10,18},{12,20},{14,22},{16,24},... | collective-permute-start | bytes 1572872 | tf_op jit(solution)/shard_map/ppermute | solution.py:196
  142.5 2.3 %collective-permute-start.8 = (bf16[40,4096]{1,0:T(8,128)(2,1)S(1)}, bf16[40,4096]{1,0:T(8,128)(2,1)S(1)}, u32[]{:S(2)}, u32[]{:S(2)}) collective-permute-start(bf16[40,4096]{1,0:T(8,128)(2,1)S(1)} %get-tuple-element.65), channel_id=1, source_target_pairs={{0,4},{2,6},{4,0},{6,2},{8,12},{10,14},{12,8},{14,10},{16,20},{18,... | collective-permute-start | bytes 983048 | tf_op jit(solution)/shard_map/ppermute | solution.py:200
  146.0 3.6 %collective-permute-done.7.refs_0_ = bf16[40,4096]{1,0:T(8,128)(2,1)S(1)} collective-permute-done((bf16[40,4096]{1,0:T(8,128)(2,1)S(1)}, bf16[40,4096]{1,0:T(8,128)(2,1)S(1)}, u32[]{:S(2)}, u32[]{:S(2)}) %collective-permute-start.7) | collective-permute-done | bytes 327712 | tf_op jit(solution)/shard_map/ppermute | solution.py:200
  149.6 3.8 %collective-permute-done.8.refs_1_ = bf16[40,4096]{1,0:T(8,128)(2,1)S(1)} collective-permute-done((bf16[40,4096]{1,0:T(8,128)(2,1)S(1)}, bf16[40,4096]{1,0:T(8,128)(2,1)S(1)}, u32[]{:S(2)}, u32[]{:S(2)}) %collective-permute-start.8) | collective-permute-done | bytes 327712 | tf_op jit(solution)/shard_map/ppermute | solution.py:200
  153.4 2.4 %shard_map.78 = bf16[64,4096]{1,0:T(8,128)(2,1)} custom-call(s32[4]{0:T(128)S(1)} %pad_add_fusion.experts_ref, bf16[64,4096]{1,0:T(8,128)(2,1)S(1)} %get-tuple-element.63.own_ref, bf16[64,4224]{1,0:T(8,128)(2,1)S(1)} %shard_map.64.z_ref.refs_0_.block_ref, bf16[40,4096]{1,0:T(8,128)(2,1)S(1)} %collective-permute-done.7.refs_0_, ...), custom_call_target="tpu_custom_call" | custom-call | flops 62914560 | bytes 2621440 | tf_op jit(solution)/shard_map/pallas_call | solution.py:171
  (60 shorter events, 28.6 us)
Async XLA Ops:
  0.0 55.9 %collective-permute-start.4 = (bf16[4096,384]{1,0:T(8,128)(2,1)}, bf16[4096,384]{1,0:T(8,128)(2,1)}, u32[]{:S(2)}, u32[]{:S(2)}) collective-permute-start(bf16[4096,384]{1,0:T(8,128)(2,1)} %bitcast.7), channel_id=1, source_target_pairs={{0,1},{1,0},{2,3},{3,2},{4,5},{5,4},{6,7},{7,6},{8,9},{9,8},{10,11... | collective-permute-start | bytes 9437192 | tf_op jit(solution)/shard_map/ppermute | solution.py:193
  0.0 56.1 %collective-permute-start.5 = (bf16[4096,384]{1,0:T(8,128)(2,1)}, bf16[4096,384]{1,0:T(8,128)(2,1)}, u32[]{:S(2)}, u32[]{:S(2)}) collective-permute-start(bf16[4096,384]{1,0:T(8,128)(2,1)} %bitcast.9), channel_id=1, source_target_pairs={{0,1},{1,0},{2,3},{3,2},{4,5},{5,4},{6,7},{7,6},{8,9},{9,8},{10,11... | collective-permute-start | bytes 9437192 | tf_op jit(solution)/shard_map/ppermute | solution.py:193
  0.5 58.4 %collective-permute-start.6 = (bf16[384,4096]{1,0:T(8,128)(2,1)}, bf16[384,4096]{1,0:T(8,128)(2,1)}, u32[]{:S(2)}, u32[]{:S(2)}) collective-permute-start(bf16[384,4096]{1,0:T(8,128)(2,1)} %bitcast.11), channel_id=1, source_target_pairs={{0,1},{1,0},{2,3},{3,2},{4,5},{5,4},{6,7},{7,6},{8,9},{9,8},{10,11... | collective-permute-start | bytes 9437192 | tf_op jit(solution)/shard_map/ppermute | solution.py:193
  4.9 10.4 %collective-permute-start = (bf16[40,4224]{1,0:T(8,128)(2,1)S(1)}, bf16[40,4224]{1,0:T(8,128)(2,1)S(1)}, u32[]{:S(2)}, u32[]{:S(2)}) collective-permute-start(bf16[40,4224]{1,0:T(8,128)(2,1)S(1)} %get-tuple-element.52), channel_id=1, source_target_pairs={{0,2},{2,0},{4,6},{6,4},{8,10},{10,8},{12,14},{14,12},{16,18},{18,... | collective-permute-start | bytes 1013768 | tf_op jit(solution)/shard_map/ppermute | solution.py:200
  5.5 11.4 %collective-permute-start.1 = (bf16[40,4224]{1,0:T(8,128)(2,1)S(1)}, bf16[40,4224]{1,0:T(8,128)(2,1)S(1)}, u32[]{:S(2)}, u32[]{:S(2)}) collective-permute-start(bf16[40,4224]{1,0:T(8,128)(2,1)S(1)} %get-tuple-element.53), channel_id=1, source_target_pairs={{0,4},{2,6},{4,0},{6,2},{8,12},{10,14},{12,8},{14,10},{16,20},{18,... | collective-permute-start | bytes 1013768 | tf_op jit(solution)/shard_map/ppermute | solution.py:200
  15.3 13.9 %collective-permute-start.3 = (bf16[64,4224]{1,0:T(8,128)(2,1)S(1)}, bf16[64,4224]{1,0:T(8,128)(2,1)S(1)}, u32[]{:S(2)}, u32[]{:S(2)}) collective-permute-start(bf16[64,4224]{1,0:T(8,128)(2,1)S(1)} %shard_map.64.z_ref.refs_0_.block_ref), channel_id=1, source_target_pairs={{0,8},{2,10},{4,12},{6,14},{8,16},{10,18},{12,20},{14,22},{16,24},... | collective-permute-start | bytes 1622024 | tf_op jit(solution)/shard_map/ppermute | solution.py:196
  16.9 10.2 %collective-permute-start.2 = (bf16[40,4224]{1,0:T(8,128)(2,1)S(1)}, bf16[40,4224]{1,0:T(8,128)(2,1)S(1)}, u32[]{:S(2)}, u32[]{:S(2)}) collective-permute-start(bf16[40,4224]{1,0:T(8,128)(2,1)S(1)} %get-tuple-element.54), channel_id=1, source_target_pairs={{0,6},{2,4},{4,2},{6,0},{8,14},{10,12},{12,10},{14,8},{16,22},{18,... | collective-permute-start | bytes 1013768 | tf_op jit(solution)/shard_map/ppermute | solution.py:200
  30.9 8.8 %collective-permute-start.11 = (bf16[40,4224]{1,0:T(8,128)(2,1)S(1)}, bf16[40,4224]{1,0:T(8,128)(2,1)S(1)}, u32[]{:S(2)}, u32[]{:S(2)}) collective-permute-start(bf16[40,4224]{1,0:T(8,128)(2,1)S(1)} %get-tuple-element.67), channel_id=1, source_target_pairs={{0,2},{2,0},{4,6},{6,4},{8,10},{10,8},{12,14},{14,12},{16,18},{18,... | collective-permute-start | bytes 1013768 | tf_op jit(solution)/shard_map/ppermute | solution.py:200
  31.5 9.8 %collective-permute-start.12 = (bf16[40,4224]{1,0:T(8,128)(2,1)S(1)}, bf16[40,4224]{1,0:T(8,128)(2,1)S(1)}, u32[]{:S(2)}, u32[]{:S(2)}) collective-permute-start(bf16[40,4224]{1,0:T(8,128)(2,1)S(1)} %get-tuple-element.68), channel_id=1, source_target_pairs={{0,4},{2,6},{4,0},{6,2},{8,12},{10,14},{12,8},{14,10},{16,20},{18,... | collective-permute-start | bytes 1013768 | tf_op jit(solution)/shard_map/ppermute | solution.py:200
  39.7 12.7 %collective-permute-start.10 = (bf16[64,4224]{1,0:T(8,128)(2,1)S(1)}, bf16[64,4224]{1,0:T(8,128)(2,1)S(1)}, u32[]{:S(2)}, u32[]{:S(2)}) collective-permute-start(bf16[64,4224]{1,0:T(8,128)(2,1)S(1)} %collective-permute-done.3.z_ref.refs_0_.block_ref), channel_id=1, source_target_pairs={{0,8},{2,10},{4,12},{6,14},{8,16},{10,18},{12,20},{14,22},{16,24},... | collective-permute-start | bytes 1622024 | tf_op jit(solution)/shard_map/ppermute | solution.py:196
  41.3 8.4 %collective-permute-start.13 = (bf16[40,4224]{1,0:T(8,128)(2,1)S(1)}, bf16[40,4224]{1,0:T(8,128)(2,1)S(1)}, u32[]{:S(2)}, u32[]{:S(2)}) collective-permute-start(bf16[40,4224]{1,0:T(8,128)(2,1)S(1)} %get-tuple-element.69), channel_id=1, source_target_pairs={{0,6},{2,4},{4,2},{6,0},{8,14},{10,12},{12,10},{14,8},{16,22},{18,... | collective-permute-start | bytes 1013768 | tf_op jit(solution)/shard_map/ppermute | solution.py:200
  52.3 24.6 %collective-permute-start.14 = (bf16[64,4224]{1,0:T(8,128)(2,1)S(1)}, bf16[64,4224]{1,0:T(8,128)(2,1)S(1)}, u32[]{:S(2)}, u32[]{:S(2)}) collective-permute-start(bf16[64,4224]{1,0:T(8,128)(2,1)S(1)} %collective-permute-done.10.z_ref.refs_0_.block_ref), channel_id=1, source_target_pairs={{0,8},{2,10},{4,12},{6,14},{8,16},{10,18},{12,20},{14,22},{16,24},... | collective-permute-start | bytes 1622024 | tf_op jit(solution)/shard_map/ppermute | solution.py:196
  55.3 18.6 %collective-permute-start.15 = (bf16[40,4224]{1,0:T(8,128)(2,1)S(1)}, bf16[40,4224]{1,0:T(8,128)(2,1)S(1)}, u32[]{:S(2)}, u32[]{:S(2)}) collective-permute-start(bf16[40,4224]{1,0:T(8,128)(2,1)S(1)} %get-tuple-element.71), channel_id=1, source_target_pairs={{0,2},{2,0},{4,6},{6,4},{8,10},{10,8},{12,14},{14,12},{16,18},{18,... | collective-permute-start | bytes 1013768 | tf_op jit(solution)/shard_map/ppermute | solution.py:200
  55.9 18.2 %collective-permute-start.16 = (bf16[40,4224]{1,0:T(8,128)(2,1)S(1)}, bf16[40,4224]{1,0:T(8,128)(2,1)S(1)}, u32[]{:S(2)}, u32[]{:S(2)}) collective-permute-start(bf16[40,4224]{1,0:T(8,128)(2,1)S(1)} %get-tuple-element.72), channel_id=1, source_target_pairs={{0,4},{2,6},{4,0},{6,2},{8,12},{10,14},{12,8},{14,10},{16,20},{18,... | collective-permute-start | bytes 1013768 | tf_op jit(solution)/shard_map/ppermute | solution.py:200
  56.1 20.9 %collective-permute-start.17 = (bf16[40,4224]{1,0:T(8,128)(2,1)S(1)}, bf16[40,4224]{1,0:T(8,128)(2,1)S(1)}, u32[]{:S(2)}, u32[]{:S(2)}) collective-permute-start(bf16[40,4224]{1,0:T(8,128)(2,1)S(1)} %get-tuple-element.73), channel_id=1, source_target_pairs={{0,6},{2,4},{4,2},{6,0},{8,14},{10,12},{12,10},{14,8},{16,22},{18,... | collective-permute-start | bytes 1013768 | tf_op jit(solution)/shard_map/ppermute | solution.py:200
  73.4 10.7 %collective-permute-start.27 = (bf16[40,4096]{1,0:T(8,128)(2,1)S(1)}, bf16[40,4096]{1,0:T(8,128)(2,1)S(1)}, u32[]{:S(2)}, u32[]{:S(2)}) collective-permute-start(bf16[40,4096]{1,0:T(8,128)(2,1)S(1)} %get-tuple-element.96), channel_id=1, source_target_pairs={{0,2},{2,0},{4,6},{6,4},{8,10},{10,8},{12,14},{14,12},{16,18},{18,... | collective-permute-start | bytes 983048 | tf_op jit(solution)/shard_map/ppermute | solution.py:200
  73.9 17.5 %collective-permute-start.28 = (bf16[40,4096]{1,0:T(8,128)(2,1)S(1)}, bf16[40,4096]{1,0:T(8,128)(2,1)S(1)}, u32[]{:S(2)}, u32[]{:S(2)}) collective-permute-start(bf16[40,4096]{1,0:T(8,128)(2,1)S(1)} %get-tuple-element.97), channel_id=1, source_target_pairs={{0,4},{2,6},{4,0},{6,2},{8,12},{10,14},{12,8},{14,10},{16,20},{18,... | collective-permute-start | bytes 983048 | tf_op jit(solution)/shard_map/ppermute | solution.py:200
  74.1 17.3 %collective-permute-start.29 = (bf16[40,4096]{1,0:T(8,128)(2,1)S(1)}, bf16[40,4096]{1,0:T(8,128)(2,1)S(1)}, u32[]{:S(2)}, u32[]{:S(2)}) collective-permute-start(bf16[40,4096]{1,0:T(8,128)(2,1)S(1)} %get-tuple-element.98), channel_id=1, source_target_pairs={{0,6},{2,4},{4,2},{6,0},{8,14},{10,12},{12,10},{14,8},{16,22},{18,... | collective-permute-start | bytes 983048 | tf_op jit(solution)/shard_map/ppermute | solution.py:200
  78.6 22.9 %collective-permute-start.18 = (bf16[40,4224]{1,0:T(8,128)(2,1)S(1)}, bf16[40,4224]{1,0:T(8,128)(2,1)S(1)}, u32[]{:S(2)}, u32[]{:S(2)}) collective-permute-start(bf16[40,4224]{1,0:T(8,128)(2,1)S(1)} %get-tuple-element.75), channel_id=1, source_target_pairs={{0,2},{2,0},{4,6},{6,4},{8,10},{10,8},{12,14},{14,12},{16,18},{18,... | collective-permute-start | bytes 1013768 | tf_op jit(solution)/shard_map/ppermute | solution.py:200
  79.1 23.1 %collective-permute-start.19 = (bf16[40,4224]{1,0:T(8,128)(2,1)S(1)}, bf16[40,4224]{1,0:T(8,128)(2,1)S(1)}, u32[]{:S(2)}, u32[]{:S(2)}) collective-permute-start(bf16[40,4224]{1,0:T(8,128)(2,1)S(1)} %get-tuple-element.76), channel_id=1, source_target_pairs={{0,4},{2,6},{4,0},{6,2},{8,12},{10,14},{12,8},{14,10},{16,20},{18,... | collective-permute-start | bytes 1013768 | tf_op jit(solution)/shard_map/ppermute | solution.py:200
  84.1 21.7 %collective-permute-start.20 = (bf16[40,4224]{1,0:T(8,128)(2,1)S(1)}, bf16[40,4224]{1,0:T(8,128)(2,1)S(1)}, u32[]{:S(2)}, u32[]{:S(2)}) collective-permute-start(bf16[40,4224]{1,0:T(8,128)(2,1)S(1)} %get-tuple-element.77), channel_id=1, source_target_pairs={{0,6},{2,4},{4,2},{6,0},{8,14},{10,12},{12,10},{14,8},{16,22},{18,... | collective-permute-start | bytes 1013768 | tf_op jit(solution)/shard_map/ppermute | solution.py:200
  93.0 21.4 %collective-permute-start.30 = (bf16[64,4096]{1,0:T(8,128)(2,1)S(1)}, bf16[64,4096]{1,0:T(8,128)(2,1)S(1)}, u32[]{:S(2)}, u32[]{:S(2)}) collective-permute-start(bf16[64,4096]{1,0:T(8,128)(2,1)S(1)} %shard_map.75), channel_id=1, source_target_pairs={{0,8},{2,10},{4,12},{6,14},{8,16},{10,18},{12,20},{14,22},{16,24},... | collective-permute-start | bytes 1572872 | tf_op jit(solution)/shard_map/ppermute | solution.py:196
  100.2 10.5 %collective-permute-start.24 = (bf16[40,4096]{1,0:T(8,128)(2,1)S(1)}, bf16[40,4096]{1,0:T(8,128)(2,1)S(1)}, u32[]{:S(2)}, u32[]{:S(2)}) collective-permute-start(bf16[40,4096]{1,0:T(8,128)(2,1)S(1)} %get-tuple-element.93), channel_id=1, source_target_pairs={{0,2},{2,0},{4,6},{6,4},{8,10},{10,8},{12,14},{14,12},{16,18},{18,... | collective-permute-start | bytes 983048 | tf_op jit(solution)/shard_map/ppermute | solution.py:200
  101.5 12.8 %collective-permute-start.25 = (bf16[40,4096]{1,0:T(8,128)(2,1)S(1)}, bf16[40,4096]{1,0:T(8,128)(2,1)S(1)}, u32[]{:S(2)}, u32[]{:S(2)}) collective-permute-start(bf16[40,4096]{1,0:T(8,128)(2,1)S(1)} %get-tuple-element.94), channel_id=1, source_target_pairs={{0,4},{2,6},{4,0},{6,2},{8,12},{10,14},{12,8},{14,10},{16,20},{18,... | collective-permute-start | bytes 983048 | tf_op jit(solution)/shard_map/ppermute | solution.py:200
  102.3 12.1 %collective-permute-start.26 = (bf16[40,4096]{1,0:T(8,128)(2,1)S(1)}, bf16[40,4096]{1,0:T(8,128)(2,1)S(1)}, u32[]{:S(2)}, u32[]{:S(2)}) collective-permute-start(bf16[40,4096]{1,0:T(8,128)(2,1)S(1)} %get-tuple-element.95), channel_id=1, source_target_pairs={{0,6},{2,4},{4,2},{6,0},{8,14},{10,12},{12,10},{14,8},{16,22},{18,... | collective-permute-start | bytes 983048 | tf_op jit(solution)/shard_map/ppermute | solution.py:200
  115.9 19.1 %collective-permute-start.31 = (bf16[64,4096]{1,0:T(8,128)(2,1)S(1)}, bf16[64,4096]{1,0:T(8,128)(2,1)S(1)}, u32[]{:S(2)}, u32[]{:S(2)}) collective-permute-start(bf16[64,4096]{1,0:T(8,128)(2,1)S(1)} %shard_map.76), channel_id=1, source_target_pairs={{0,8},{2,10},{4,12},{6,14},{8,16},{10,18},{12,20},{14,22},{16,24},... | collective-permute-start | bytes 1572872 | tf_op jit(solution)/shard_map/ppermute | solution.py:196
  123.1 7.1 %collective-permute-start.21 = (bf16[40,4096]{1,0:T(8,128)(2,1)S(1)}, bf16[40,4096]{1,0:T(8,128)(2,1)S(1)}, u32[]{:S(2)}, u32[]{:S(2)}) collective-permute-start(bf16[40,4096]{1,0:T(8,128)(2,1)S(1)} %get-tuple-element.90), channel_id=1, source_target_pairs={{0,2},{2,0},{4,6},{6,4},{8,10},{10,8},{12,14},{14,12},{16,18},{18,... | collective-permute-start | bytes 983048 | tf_op jit(solution)/shard_map/ppermute | solution.py:200
  124.4 10.6 %collective-permute-start.22 = (bf16[40,4096]{1,0:T(8,128)(2,1)S(1)}, bf16[40,4096]{1,0:T(8,128)(2,1)S(1)}, u32[]{:S(2)}, u32[]{:S(2)}) collective-permute-start(bf16[40,4096]{1,0:T(8,128)(2,1)S(1)} %get-tuple-element.91), channel_id=1, source_target_pairs={{0,4},{2,6},{4,0},{6,2},{8,12},{10,14},{12,8},{14,10},{16,20},{18,... | collective-permute-start | bytes 983048 | tf_op jit(solution)/shard_map/ppermute | solution.py:200
  125.0 10.0 %collective-permute-start.23 = (bf16[40,4096]{1,0:T(8,128)(2,1)S(1)}, bf16[40,4096]{1,0:T(8,128)(2,1)S(1)}, u32[]{:S(2)}, u32[]{:S(2)}) collective-permute-start(bf16[40,4096]{1,0:T(8,128)(2,1)S(1)} %get-tuple-element.92), channel_id=1, source_target_pairs={{0,6},{2,4},{4,2},{6,0},{8,14},{10,12},{12,10},{14,8},{16,22},{18,... | collective-permute-start | bytes 983048 | tf_op jit(solution)/shard_map/ppermute | solution.py:200
  136.6 16.8 %collective-permute-start.32 = (bf16[64,4096]{1,0:T(8,128)(2,1)S(1)}, bf16[64,4096]{1,0:T(8,128)(2,1)S(1)}, u32[]{:S(2)}, u32[]{:S(2)}) collective-permute-start(bf16[64,4096]{1,0:T(8,128)(2,1)S(1)} %shard_map.77), channel_id=1, source_target_pairs={{0,8},{2,10},{4,12},{6,14},{8,16},{10,18},{12,20},{14,22},{16,24},... | collective-permute-start | bytes 1572872 | tf_op jit(solution)/shard_map/ppermute | solution.py:196
  142.5 10.8 %collective-permute-start.8 = (bf16[40,4096]{1,0:T(8,128)(2,1)S(1)}, bf16[40,4096]{1,0:T(8,128)(2,1)S(1)}, u32[]{:S(2)}, u32[]{:S(2)}) collective-permute-start(bf16[40,4096]{1,0:T(8,128)(2,1)S(1)} %get-tuple-element.65), channel_id=1, source_target_pairs={{0,4},{2,6},{4,0},{6,2},{8,12},{10,14},{12,8},{14,10},{16,20},{18,... | collective-permute-start | bytes 983048 | tf_op jit(solution)/shard_map/ppermute | solution.py:200
  144.8 8.6 %collective-permute-start.9 = (bf16[40,4096]{1,0:T(8,128)(2,1)S(1)}, bf16[40,4096]{1,0:T(8,128)(2,1)S(1)}, u32[]{:S(2)}, u32[]{:S(2)}) collective-permute-start(bf16[40,4096]{1,0:T(8,128)(2,1)S(1)} %get-tuple-element.66), channel_id=1, source_target_pairs={{0,6},{2,4},{4,2},{6,0},{8,14},{10,12},{12,10},{14,8},{16,22},{18,... | collective-permute-start | bytes 983048 | tf_op jit(solution)/shard_map/ppermute | solution.py:200
  (5 other events, 13.8 us)

commit v4 on v3

--- a/solution.py
+++ b/solution.py
@@ -206,12 +206,13 @@
     experts = jnp.stack([me, me ^ 1, me ^ 2, me ^ 3])
     block = prepare(expert_ids, route_weights, tokens)
     half = (gate_proj[0], up_proj[0], down_proj[0])
-    other = [swap(x) for x in half]
+    other = []
 
     levels, given, results, weights = [block], [], [], []
 
     def compute(k):
         if not weights:
+            other.extend(swap(x) for x in after(half, levels[1]))
             weights.extend([*stage(*after(half, levels[1])), *stage(*other)])
         mine = after(given[k], results[-1][0]) if results else given[k]
         results.append(run_expert(experts, [levels[k], *mine], weights, top))

time: 158 us -> 154 us (0.975)
  Pallas kernels: 39.8 us -> 36.5 us
  waiting for transfers between devices: 69.3 us -> 71.5 us
  starting transfers between devices: 38.3 us -> 36.7 us
    ppermute x6, starting transfers between devices: 14.1 us -> 9.08 us  [hop_z(): return lax.ppermute(x, 'ep', [(i, (i + 4) % n_ep) for i in range(n_ep)])]
    ppermute x24, waiting for transfers between devices: 64.4 us -> 69.3 us  [spread(): lax.ppermute(x, 'ep', [(i, i ^ flip) for i in range(n_ep)])]
    ppermute x24, starting transfers between devices: 23.6 us -> 27.1 us  [spread(): lax.ppermute(x, 'ep', [(i, i ^ flip) for i in range(n_ep)])]
    pallas_call x2, Pallas kernels: 4.65 us -> 1.74 us  [stage(): pl.pallas_call(stage_kernel, out_shape=[pltpu.VMEM((width, 2 * ff), BF),...]
    ppermute x6, waiting for transfers between devices: 4.85 us -> 2.18 us  [hop_z(): return lax.ppermute(x, 'ep', [(i, (i + 4) % n_ep) for i in range(n_ep)])]
  transfers between devices with their start and end apart: 33 -> 33, of which waited for: 14 -> 15; matrix products, arithmetic and copies ran while one was open for 1% -> 0% of each run, Pallas kernels for 22% -> 20%
where the time goes in v4:
time: 154 us; the launch traced here: 153 us
  waiting for transfers between devices  71.5 us (46%)
  starting transfers between devices  36.7 us (24%)
  Pallas kernels  36.5 us (24%)
  local copies, waits for them, and re-layouts  8.25 us (5%)
    ppermute x24, waiting for transfers between devices, spread(): lax.ppermute(x, 'ep', [(i, i ^ flip) for i in range(n_ep)])  69.3 us
    ppermute x24, starting transfers between devices, spread(): lax.ppermute(x, 'ep', [(i, i ^ flip) for i in range(n_ep)])  27.1 us
    pallas_call x4, Pallas kernels, run_expert(): pl.pallas_call(functools.partial(expert_kernel, top, pitch), out_shape=[j...  21 us
    ppermute x6, starting transfers between devices, hop_z(): return lax.ppermute(x, 'ep', [(i, (i + 4) % n_ep) for i in range(n_ep)])  9.08 us
    unnamed x10, local copies, waits for them, and re-layouts  8.25 us
    pallas_call x4, Pallas kernels, put_back(): pl.pallas_call(functools.partial(put_back_kernel, top, slots, len(more)),...  7.1 us
    pallas_call x4, Pallas kernels, select(): pl.pallas_call(functools.partial(select_kernel, top, slots), out_shape=[j...  6.59 us
  transfers between devices with their start and end apart: 33, of which 15 were waited for; matrix products, arithmetic and copies ran while one was open for 0% of the time, Pallas kernels for 20%

profile of v4, /device:TPU:14, one launch (start us, length us, event | category | flops | bytes accessed | tf_op | source)
XLA Modules:
  0.0 153.2 jit_solution(16677341575943326130)
XLA Ops:
  2.7 1.6 %collective-permute-start.3 = (bf16[64,4224]{1,0:T(8,128)(2,1)S(1)}, bf16[64,4224]{1,0:T(8,128)(2,1)S(1)}, u32[]{:S(2)}, u32[]{:S(2)}) collective-permute-start(bf16[64,4224]{1,0:T(8,128)(2,1)S(1)} %shard_map.64.z_ref.refs_0_.block_ref), channel_id=1, source_target_pairs={{0,8},{2,10},{4,12},{6,14},{8,16},{10,18},{12,20},{14,22},{16,24},... | collective-permute-start | bytes 1622024 | tf_op jit(solution)/shard_map/ppermute | solution.py:196
  4.4 1.7 %shard_map.65 = (bf16[40,4224]{1,0:T(8,128)(2,1)S(1)}, bf16[40,4224]{1,0:T(8,128)(2,1)S(1)}, bf16[40,4224]{1,0:T(8,128)(2,1)S(1)}) custom-call(s32[4]{0:T(128)S(1)} %pad_add_fusion.experts_ref, bf16[64,4224]{1,0:T(8,128)(2,1)S(1)} %shard_map.64.z_ref.refs_0_.block_ref), custom_call_target="tpu_custom_call" | custom-call | flops 64880640 | bytes 1622016 | tf_op jit(solution)/shard_map/pallas_call | solution.py:51
  7.1 2.4 %collective-permute-start.2 = (bf16[40,4224]{1,0:T(8,128)(2,1)S(1)}, bf16[40,4224]{1,0:T(8,128)(2,1)S(1)}, u32[]{:S(2)}, u32[]{:S(2)}) collective-permute-start(bf16[40,4224]{1,0:T(8,128)(2,1)S(1)} %get-tuple-element.54), channel_id=1, source_target_pairs={{0,6},{2,4},{4,2},{6,0},{8,14},{10,12},{12,10},{14,8},{16,22},{18,... | collective-permute-start | bytes 1013768 | tf_op jit(solution)/shard_map/ppermute | solution.py:200
  9.6 7.4 %collective-permute-done.refs_1_ = bf16[40,4224]{1,0:T(8,128)(2,1)S(1)} collective-permute-done((bf16[40,4224]{1,0:T(8,128)(2,1)S(1)}, bf16[40,4224]{1,0:T(8,128)(2,1)S(1)}, u32[]{:S(2)}, u32[]{:S(2)}) %collective-permute-start) | collective-permute-done | bytes 337952 | tf_op jit(solution)/shard_map/ppermute | solution.py:200
  17.0 6.0 %collective-permute-done.1.refs_2_ = bf16[40,4224]{1,0:T(8,128)(2,1)S(1)} collective-permute-done((bf16[40,4224]{1,0:T(8,128)(2,1)S(1)}, bf16[40,4224]{1,0:T(8,128)(2,1)S(1)}, u32[]{:S(2)}, u32[]{:S(2)}) %collective-permute-start.1) | collective-permute-done | bytes 337952 | tf_op jit(solution)/shard_map/ppermute | solution.py:200
  23.6 1.6 %shard_map.69 = (bf16[40,4224]{1,0:T(8,128)(2,1)S(1)}, bf16[40,4224]{1,0:T(8,128)(2,1)S(1)}, bf16[40,4224]{1,0:T(8,128)(2,1)S(1)}) custom-call(s32[4]{0:T(128)S(1)} %pad_add_fusion.experts_ref, bf16[64,4224]{1,0:T(8,128)(2,1)S(1)} %collective-permute-done.3.z_ref.refs_0_.block_ref), custom_call_target="tpu_custom_call" | custom-call | flops 64880640 | bytes 1622016 | tf_op jit(solution)/shard_map/pallas_call | solution.py:51
  27.3 8.3 %collective-permute-done.11.refs_1_ = bf16[40,4224]{1,0:T(8,128)(2,1)S(1)} collective-permute-done((bf16[40,4224]{1,0:T(8,128)(2,1)S(1)}, bf16[40,4224]{1,0:T(8,128)(2,1)S(1)}, u32[]{:S(2)}, u32[]{:S(2)}) %collective-permute-start.11) | collective-permute-done | bytes 337952 | tf_op jit(solution)/shard_map/ppermute | solution.py:200
  38.6 1.9 %copy-done = bf16[1,4096,384]{2,1,0:T(8,128)(2,1)S(1)} copy-done((bf16[1,4096,384]{2,1,0:T(8,128)(2,1)S(1)}, bf16[1,4096,384]{2,1,0:T(8,128)(2,1)}, u32[]{:S(2)}) %copy-start) | copy-done | bytes 3145752
  40.5 1.9 %copy-done.1 = bf16[1,4096,384]{2,1,0:T(8,128)(2,1)S(1)} copy-done((bf16[1,4096,384]{2,1,0:T(8,128)(2,1)S(1)}, bf16[1,4096,384]{2,1,0:T(8,128)(2,1)}, u32[]{:S(2)}) %copy-start.1) | copy-done | bytes 3145752
  42.4 1.9 %copy-done.2 = bf16[1,384,4096]{2,1,0:T(8,128)(2,1)S(1)} copy-done((bf16[1,384,4096]{2,1,0:T(8,128)(2,1)S(1)}, bf16[1,384,4096]{2,1,0:T(8,128)(2,1)}, u32[]{:S(2)}) %copy-start.2) | copy-done | bytes 3145752
  45.1 2.1 %collective-permute-done.13.refs_3_ = bf16[40,4224]{1,0:T(8,128)(2,1)S(1)} collective-permute-done((bf16[40,4224]{1,0:T(8,128)(2,1)S(1)}, bf16[40,4224]{1,0:T(8,128)(2,1)S(1)}, u32[]{:S(2)}, u32[]{:S(2)}) %collective-permute-start.13) | collective-permute-done | bytes 337952 | tf_op jit(solution)/shard_map/ppermute | solution.py:200
  47.2 2.2 %collective-permute-done.10.z_ref.refs_0_.block_ref = bf16[64,4224]{1,0:T(8,128)(2,1)S(1)} collective-permute-done((bf16[64,4224]{1,0:T(8,128)(2,1)S(1)}, bf16[64,4224]{1,0:T(8,128)(2,1)S(1)}, u32[]{:S(2)}, u32[]{:S(2)}) %collective-permute-start.10) | collective-permute-done | bytes 540704 | tf_op jit(solution)/shard_map/ppermute | solution.py:196
  51.0 1.7 %shard_map.70 = (bf16[40,4224]{1,0:T(8,128)(2,1)S(1)}, bf16[40,4224]{1,0:T(8,128)(2,1)S(1)}, bf16[40,4224]{1,0:T(8,128)(2,1)S(1)}) custom-call(s32[4]{0:T(128)S(1)} %pad_add_fusion.experts_ref, bf16[64,4224]{1,0:T(8,128)(2,1)S(1)} %collective-permute-done.10.z_ref.refs_0_.block_ref), custom_call_target="tpu_custom_call" | custom-call | flops 64880640 | bytes 1622016 | tf_op jit(solution)/shard_map/pallas_call | solution.py:51
  57.1 5.2 %shard_map.68 = (bf16[64,4096]{1,0:T(8,128)(2,1)S(1)}, bf16[40,4096]{1,0:T(8,128)(2,1)S(1)}, bf16[40,4096]{1,0:T(8,128)(2,1)S(1)}, bf16[40,4096]{1,0:T(8,128)(2,1)S(1)}) custom-call(s32[4]{0:T(128)S(1)} %pad_add_fusion.experts_ref, bf16[64,4224]{1,0:T(8,128)(2,1)S(1)} %shard_map.64.z_ref.refs_0_.block_ref, ...), custom_call_target="tpu_custom_call" | custom-call | flops 3925868544 | bytes 3407872 | tf_op jit(solution)/shard_map/pallas_call | solution.py:143
  62.3 5.3 %shard_map.72 = (bf16[64,4096]{1,0:T(8,128)(2,1)S(1)}, bf16[40,4096]{1,0:T(8,128)(2,1)S(1)}, bf16[40,4096]{1,0:T(8,128)(2,1)S(1)}, bf16[40,4096]{1,0:T(8,128)(2,1)S(1)}) custom-call(s32[4]{0:T(128)S(1)} %pad_add_fusion.experts_ref, bf16[64,4224]{1,0:T(8,128)(2,1)S(1)} %collective-permute-done.3.z_ref.refs_0_.block_ref, ...), custom_call_target="tpu_custom_call" | custom-call | flops 3925868544 | bytes 3407872 | tf_op jit(solution)/shard_map/pallas_call | solution.py:143
  71.2 1.6 %shard_map.71 = (bf16[40,4224]{1,0:T(8,128)(2,1)S(1)}, bf16[40,4224]{1,0:T(8,128)(2,1)S(1)}, bf16[40,4224]{1,0:T(8,128)(2,1)S(1)}) custom-call(s32[4]{0:T(128)S(1)} %pad_add_fusion.experts_ref, bf16[64,4224]{1,0:T(8,128)(2,1)S(1)} %collective-permute-done.14.z_ref.refs_0_.block_ref), custom_call_target="tpu_custom_call" | custom-call | flops 64880640 | bytes 1622016 | tf_op jit(solution)/shard_map/pallas_call | solution.py:51
  74.9 3.4 %collective-permute-done.27.refs_0_ = bf16[40,4096]{1,0:T(8,128)(2,1)S(1)} collective-permute-done((bf16[40,4096]{1,0:T(8,128)(2,1)S(1)}, bf16[40,4096]{1,0:T(8,128)(2,1)S(1)}, u32[]{:S(2)}, u32[]{:S(2)}) %collective-permute-start.27) | collective-permute-done | bytes 327712 | tf_op jit(solution)/shard_map/ppermute | solution.py:200
  79.7 7.0 %collective-permute-done.28.refs_1_ = bf16[40,4096]{1,0:T(8,128)(2,1)S(1)} collective-permute-done((bf16[40,4096]{1,0:T(8,128)(2,1)S(1)}, bf16[40,4096]{1,0:T(8,128)(2,1)S(1)}, u32[]{:S(2)}, u32[]{:S(2)}) %collective-permute-start.28) | collective-permute-done | bytes 327712 | tf_op jit(solution)/shard_map/ppermute | solution.py:200
  88.9 5.2 %shard_map.73 = (bf16[64,4096]{1,0:T(8,128)(2,1)S(1)}, bf16[40,4096]{1,0:T(8,128)(2,1)S(1)}, bf16[40,4096]{1,0:T(8,128)(2,1)S(1)}, bf16[40,4096]{1,0:T(8,128)(2,1)S(1)}) custom-call(s32[4]{0:T(128)S(1)} %pad_add_fusion.experts_ref, bf16[64,4224]{1,0:T(8,128)(2,1)S(1)} %collective-permute-done.10.z_ref.refs_0_.block_ref, ...), custom_call_target="tpu_custom_call" | custom-call | flops 3925868544 | bytes 3407872 | tf_op jit(solution)/shard_map/pallas_call | solution.py:143
  95.9 2.8 %collective-permute-done.19.refs_2_ = bf16[40,4224]{1,0:T(8,128)(2,1)S(1)} collective-permute-done((bf16[40,4224]{1,0:T(8,128)(2,1)S(1)}, bf16[40,4224]{1,0:T(8,128)(2,1)S(1)}, u32[]{:S(2)}, u32[]{:S(2)}) %collective-permute-start.19) | collective-permute-done | bytes 337952 | tf_op jit(solution)/shard_map/ppermute | solution.py:200
  100.6 6.4 %collective-permute-done.24.refs_0_ = bf16[40,4096]{1,0:T(8,128)(2,1)S(1)} collective-permute-done((bf16[40,4096]{1,0:T(8,128)(2,1)S(1)}, bf16[40,4096]{1,0:T(8,128)(2,1)S(1)}, u32[]{:S(2)}, u32[]{:S(2)}) %collective-permute-start.24) | collective-permute-done | bytes 327712 | tf_op jit(solution)/shard_map/ppermute | solution.py:200
  106.9 5.1 %collective-permute-done.25.refs_1_ = bf16[40,4096]{1,0:T(8,128)(2,1)S(1)} collective-permute-done((bf16[40,4096]{1,0:T(8,128)(2,1)S(1)}, bf16[40,4096]{1,0:T(8,128)(2,1)S(1)}, u32[]{:S(2)}, u32[]{:S(2)}) %collective-permute-start.25) | collective-permute-done | bytes 327712 | tf_op jit(solution)/shard_map/ppermute | solution.py:200
  112.0 1.6 %shard_map.76 = bf16[64,4096]{1,0:T(8,128)(2,1)S(1)} custom-call(s32[4]{0:T(128)S(1)} %pad_add_fusion.experts_ref, bf16[64,4096]{1,0:T(8,128)(2,1)S(1)} %get-tuple-element.85.own_ref, bf16[64,4224]{1,0:T(8,128)(2,1)S(1)} %collective-permute-done.10.z_ref.refs_0_.block_ref, bf16[40,4096]{1,0:T(8,128)(2,1)S(1)} %collective-permute-done.24.refs_0_, ...), custom_call_target="tpu_custom_call" | custom-call | flops 62914560 | bytes 2621440 | tf_op jit(solution)/shard_map/pallas_call | solution.py:171
  114.0 5.3 %shard_map.74 = (bf16[64,4096]{1,0:T(8,128)(2,1)S(1)}, bf16[40,4096]{1,0:T(8,128)(2,1)S(1)}, bf16[40,4096]{1,0:T(8,128)(2,1)S(1)}, bf16[40,4096]{1,0:T(8,128)(2,1)S(1)}) custom-call(s32[4]{0:T(128)S(1)} %pad_add_fusion.experts_ref, bf16[64,4224]{1,0:T(8,128)(2,1)S(1)} %collective-permute-done.14.z_ref.refs_0_.block_ref, ...), custom_call_target="tpu_custom_call" | custom-call | flops 3925868544 | bytes 3407872 | tf_op jit(solution)/shard_map/pallas_call | solution.py:143
  121.2 1.6 %collective-permute-start.23 = (bf16[40,4096]{1,0:T(8,128)(2,1)S(1)}, bf16[40,4096]{1,0:T(8,128)(2,1)S(1)}, u32[]{:S(2)}, u32[]{:S(2)}) collective-permute-start(bf16[40,4096]{1,0:T(8,128)(2,1)S(1)} %get-tuple-element.92), channel_id=1, source_target_pairs={{0,6},{2,4},{4,2},{6,0},{8,14},{10,12},{12,10},{14,8},{16,22},{18,... | collective-permute-start | bytes 983048 | tf_op jit(solution)/shard_map/ppermute | solution.py:200
  122.8 6.2 %collective-permute-done.21.refs_0_ = bf16[40,4096]{1,0:T(8,128)(2,1)S(1)} collective-permute-done((bf16[40,4096]{1,0:T(8,128)(2,1)S(1)}, bf16[40,4096]{1,0:T(8,128)(2,1)S(1)}, u32[]{:S(2)}, u32[]{:S(2)}) %collective-permute-start.21) | collective-permute-done | bytes 327712 | tf_op jit(solution)/shard_map/ppermute | solution.py:200
  129.1 3.9 %collective-permute-done.22.refs_1_ = bf16[40,4096]{1,0:T(8,128)(2,1)S(1)} collective-permute-done((bf16[40,4096]{1,0:T(8,128)(2,1)S(1)}, bf16[40,4096]{1,0:T(8,128)(2,1)S(1)}, u32[]{:S(2)}, u32[]{:S(2)}) %collective-permute-start.22) | collective-permute-done | bytes 327712 | tf_op jit(solution)/shard_map/ppermute | solution.py:200
  133.0 1.6 %shard_map.77 = bf16[64,4096]{1,0:T(8,128)(2,1)S(1)} custom-call(s32[4]{0:T(128)S(1)} %pad_add_fusion.experts_ref, bf16[64,4096]{1,0:T(8,128)(2,1)S(1)} %get-tuple-element.89.own_ref, bf16[64,4224]{1,0:T(8,128)(2,1)S(1)} %collective-permute-done.14.z_ref.refs_0_.block_ref, bf16[40,4096]{1,0:T(8,128)(2,1)S(1)} %collective-permute-done.21.refs_0_, ...), custom_call_target="tpu_custom_call" | custom-call | flops 62914560 | bytes 2621440 | tf_op jit(solution)/shard_map/pallas_call | solution.py:171
  134.6 3.3 %collective-permute-start.32 = (bf16[64,4096]{1,0:T(8,128)(2,1)S(1)}, bf16[64,4096]{1,0:T(8,128)(2,1)S(1)}, u32[]{:S(2)}, u32[]{:S(2)}) collective-permute-start(bf16[64,4096]{1,0:T(8,128)(2,1)S(1)} %shard_map.77), channel_id=1, source_target_pairs={{0,8},{2,10},{4,12},{6,14},{8,16},{10,18},{12,20},{14,22},{16,24},... | collective-permute-start | bytes 1572872 | tf_op jit(solution)/shard_map/ppermute | solution.py:196
  141.4 4.6 %collective-permute-done.7.refs_0_ = bf16[40,4096]{1,0:T(8,128)(2,1)S(1)} collective-permute-done((bf16[40,4096]{1,0:T(8,128)(2,1)S(1)}, bf16[40,4096]{1,0:T(8,128)(2,1)S(1)}, u32[]{:S(2)}, u32[]{:S(2)}) %collective-permute-start.7) | collective-permute-done | bytes 327712 | tf_op jit(solution)/shard_map/ppermute | solution.py:200
  146.0 4.8 %collective-permute-done.8.refs_1_ = bf16[40,4096]{1,0:T(8,128)(2,1)S(1)} collective-permute-done((bf16[40,4096]{1,0:T(8,128)(2,1)S(1)}, bf16[40,4096]{1,0:T(8,128)(2,1)S(1)}, u32[]{:S(2)}, u32[]{:S(2)}) %collective-permute-start.8) | collective-permute-done | bytes 327712 | tf_op jit(solution)/shard_map/ppermute | solution.py:200
  150.8 2.4 %shard_map.78 = bf16[64,4096]{1,0:T(8,128)(2,1)} custom-call(s32[4]{0:T(128)S(1)} %pad_add_fusion.experts_ref, bf16[64,4096]{1,0:T(8,128)(2,1)S(1)} %get-tuple-element.63.own_ref, bf16[64,4224]{1,0:T(8,128)(2,1)S(1)} %shard_map.64.z_ref.refs_0_.block_ref, bf16[40,4096]{1,0:T(8,128)(2,1)S(1)} %collective-permute-done.7.refs_0_, ...), custom_call_target="tpu_custom_call" | custom-call | flops 62914560 | bytes 2621440 | tf_op jit(solution)/shard_map/pallas_call | solution.py:171
  (60 shorter events, 35.1 us)
Async XLA Ops:
  2.7 20.3 %collective-permute-start.3 = (bf16[64,4224]{1,0:T(8,128)(2,1)S(1)}, bf16[64,4224]{1,0:T(8,128)(2,1)S(1)}, u32[]{:S(2)}, u32[]{:S(2)}) collective-permute-start(bf16[64,4224]{1,0:T(8,128)(2,1)S(1)} %shard_map.64.z_ref.refs_0_.block_ref), channel_id=1, source_target_pairs={{0,8},{2,10},{4,12},{6,14},{8,16},{10,18},{12,20},{14,22},{16,24},... | collective-permute-start | bytes 1622024 | tf_op jit(solution)/shard_map/ppermute | solution.py:196
  6.0 10.9 %collective-permute-start = (bf16[40,4224]{1,0:T(8,128)(2,1)S(1)}, bf16[40,4224]{1,0:T(8,128)(2,1)S(1)}, u32[]{:S(2)}, u32[]{:S(2)}) collective-permute-start(bf16[40,4224]{1,0:T(8,128)(2,1)S(1)} %get-tuple-element.52), channel_id=1, source_target_pairs={{0,2},{2,0},{4,6},{6,4},{8,10},{10,8},{12,14},{14,12},{16,18},{18,... | collective-permute-start | bytes 1013768 | tf_op jit(solution)/shard_map/ppermute | solution.py:200
  6.6 16.4 %collective-permute-start.1 = (bf16[40,4224]{1,0:T(8,128)(2,1)S(1)}, bf16[40,4224]{1,0:T(8,128)(2,1)S(1)}, u32[]{:S(2)}, u32[]{:S(2)}) collective-permute-start(bf16[40,4224]{1,0:T(8,128)(2,1)S(1)} %get-tuple-element.53), channel_id=1, source_target_pairs={{0,4},{2,6},{4,0},{6,2},{8,12},{10,14},{12,8},{14,10},{16,20},{18,... | collective-permute-start | bytes 1013768 | tf_op jit(solution)/shard_map/ppermute | solution.py:200
  7.1 15.8 %collective-permute-start.2 = (bf16[40,4224]{1,0:T(8,128)(2,1)S(1)}, bf16[40,4224]{1,0:T(8,128)(2,1)S(1)}, u32[]{:S(2)}, u32[]{:S(2)}) collective-permute-start(bf16[40,4224]{1,0:T(8,128)(2,1)S(1)} %get-tuple-element.54), channel_id=1, source_target_pairs={{0,6},{2,4},{4,2},{6,0},{8,14},{10,12},{12,10},{14,8},{16,22},{18,... | collective-permute-start | bytes 1013768 | tf_op jit(solution)/shard_map/ppermute | solution.py:200
  23.0 31.2 %collective-permute-start.4 = (bf16[4096,384]{1,0:T(8,128)(2,1)}, bf16[4096,384]{1,0:T(8,128)(2,1)S(1)}, u32[]{:S(2)}, u32[]{:S(2)}) collective-permute-start(bf16[4096,384]{1,0:T(8,128)(2,1)} %bitcast.7), channel_id=1, source_target_pairs={{0,1},{1,0},{2,3},{3,2},{4,5},{5,4},{6,7},{7,6},{8,9},{9,8},{10,11... | collective-permute-start | bytes 9437192 | tf_op jit(solution)/shard_map/ppermute | solution.py:193
  23.0 31.7 %collective-permute-start.5 = (bf16[4096,384]{1,0:T(8,128)(2,1)}, bf16[4096,384]{1,0:T(8,128)(2,1)S(1)}, u32[]{:S(2)}, u32[]{:S(2)}) collective-permute-start(bf16[4096,384]{1,0:T(8,128)(2,1)} %bitcast.9), channel_id=1, source_target_pairs={{0,1},{1,0},{2,3},{3,2},{4,5},{5,4},{6,7},{7,6},{8,9},{9,8},{10,11... | collective-permute-start | bytes 9437192 | tf_op jit(solution)/shard_map/ppermute | solution.py:193
  23.5 32.7 %collective-permute-start.6 = (bf16[384,4096]{1,0:T(8,128)(2,1)}, bf16[384,4096]{1,0:T(8,128)(2,1)S(1)}, u32[]{:S(2)}, u32[]{:S(2)}) collective-permute-start(bf16[384,4096]{1,0:T(8,128)(2,1)} %bitcast.11), channel_id=1, source_target_pairs={{0,1},{1,0},{2,3},{3,2},{4,5},{5,4},{6,7},{7,6},{8,9},{9,8},{10,11... | collective-permute-start | bytes 9437192 | tf_op jit(solution)/shard_map/ppermute | solution.py:193
  25.2 10.3 %collective-permute-start.11 = (bf16[40,4224]{1,0:T(8,128)(2,1)S(1)}, bf16[40,4224]{1,0:T(8,128)(2,1)S(1)}, u32[]{:S(2)}, u32[]{:S(2)}) collective-permute-start(bf16[40,4224]{1,0:T(8,128)(2,1)S(1)} %get-tuple-element.67), channel_id=1, source_target_pairs={{0,2},{2,0},{4,6},{6,4},{8,10},{10,8},{12,14},{14,12},{16,18},{18,... | collective-permute-start | bytes 1013768 | tf_op jit(solution)/shard_map/ppermute | solution.py:200
  26.8 10.4 %collective-permute-start.12 = (bf16[40,4224]{1,0:T(8,128)(2,1)S(1)}, bf16[40,4224]{1,0:T(8,128)(2,1)S(1)}, u32[]{:S(2)}, u32[]{:S(2)}) collective-permute-start(bf16[40,4224]{1,0:T(8,128)(2,1)S(1)} %get-tuple-element.68), channel_id=1, source_target_pairs={{0,4},{2,6},{4,0},{6,2},{8,12},{10,14},{12,8},{14,10},{16,20},{18,... | collective-permute-start | bytes 1013768 | tf_op jit(solution)/shard_map/ppermute | solution.py:200
  35.6 13.8 %collective-permute-start.10 = (bf16[64,4224]{1,0:T(8,128)(2,1)S(1)}, bf16[64,4224]{1,0:T(8,128)(2,1)S(1)}, u32[]{:S(2)}, u32[]{:S(2)}) collective-permute-start(bf16[64,4224]{1,0:T(8,128)(2,1)S(1)} %collective-permute-done.3.z_ref.refs_0_.block_ref), channel_id=1, source_target_pairs={{0,8},{2,10},{4,12},{6,14},{8,16},{10,18},{12,20},{14,22},{16,24},... | collective-permute-start | bytes 1622024 | tf_op jit(solution)/shard_map/ppermute | solution.py:196
  37.1 10.1 %collective-permute-start.13 = (bf16[40,4224]{1,0:T(8,128)(2,1)S(1)}, bf16[40,4224]{1,0:T(8,128)(2,1)S(1)}, u32[]{:S(2)}, u32[]{:S(2)}) collective-permute-start(bf16[40,4224]{1,0:T(8,128)(2,1)S(1)} %get-tuple-element.69), channel_id=1, source_target_pairs={{0,6},{2,4},{4,2},{6,0},{8,14},{10,12},{12,10},{14,8},{16,22},{18,... | collective-permute-start | bytes 1013768 | tf_op jit(solution)/shard_map/ppermute | solution.py:200
  49.4 21.7 %collective-permute-start.14 = (bf16[64,4224]{1,0:T(8,128)(2,1)S(1)}, bf16[64,4224]{1,0:T(8,128)(2,1)S(1)}, u32[]{:S(2)}, u32[]{:S(2)}) collective-permute-start(bf16[64,4224]{1,0:T(8,128)(2,1)S(1)} %collective-permute-done.10.z_ref.refs_0_.block_ref), channel_id=1, source_target_pairs={{0,8},{2,10},{4,12},{6,14},{8,16},{10,18},{12,20},{14,22},{16,24},... | collective-permute-start | bytes 1622024 | tf_op jit(solution)/shard_map/ppermute | solution.py:196
  52.6 16.5 %collective-permute-start.15 = (bf16[40,4224]{1,0:T(8,128)(2,1)S(1)}, bf16[40,4224]{1,0:T(8,128)(2,1)S(1)}, u32[]{:S(2)}, u32[]{:S(2)}) collective-permute-start(bf16[40,4224]{1,0:T(8,128)(2,1)S(1)} %get-tuple-element.71), channel_id=1, source_target_pairs={{0,2},{2,0},{4,6},{6,4},{8,10},{10,8},{12,14},{14,12},{16,18},{18,... | collective-permute-start | bytes 1013768 | tf_op jit(solution)/shard_map/ppermute | solution.py:200
  54.2 15.5 %collective-permute-start.16 = (bf16[40,4224]{1,0:T(8,128)(2,1)S(1)}, bf16[40,4224]{1,0:T(8,128)(2,1)S(1)}, u32[]{:S(2)}, u32[]{:S(2)}) collective-permute-start(bf16[40,4224]{1,0:T(8,128)(2,1)S(1)} %get-tuple-element.72), channel_id=1, source_target_pairs={{0,4},{2,6},{4,0},{6,2},{8,12},{10,14},{12,8},{14,10},{16,20},{18,... | collective-permute-start | bytes 1013768 | tf_op jit(solution)/shard_map/ppermute | solution.py:200
  54.7 16.5 %collective-permute-start.17 = (bf16[40,4224]{1,0:T(8,128)(2,1)S(1)}, bf16[40,4224]{1,0:T(8,128)(2,1)S(1)}, u32[]{:S(2)}, u32[]{:S(2)}) collective-permute-start(bf16[40,4224]{1,0:T(8,128)(2,1)S(1)} %get-tuple-element.73), channel_id=1, source_target_pairs={{0,6},{2,4},{4,2},{6,0},{8,14},{10,12},{12,10},{14,8},{16,22},{18,... | collective-permute-start | bytes 1013768 | tf_op jit(solution)/shard_map/ppermute | solution.py:200
  67.6 10.7 %collective-permute-start.27 = (bf16[40,4096]{1,0:T(8,128)(2,1)S(1)}, bf16[40,4096]{1,0:T(8,128)(2,1)S(1)}, u32[]{:S(2)}, u32[]{:S(2)}) collective-permute-start(bf16[40,4096]{1,0:T(8,128)(2,1)S(1)} %get-tuple-element.96), channel_id=1, source_target_pairs={{0,2},{2,0},{4,6},{6,4},{8,10},{10,8},{12,14},{14,12},{16,18},{18,... | collective-permute-start | bytes 983048 | tf_op jit(solution)/shard_map/ppermute | solution.py:200
  69.1 17.5 %collective-permute-start.28 = (bf16[40,4096]{1,0:T(8,128)(2,1)S(1)}, bf16[40,4096]{1,0:T(8,128)(2,1)S(1)}, u32[]{:S(2)}, u32[]{:S(2)}) collective-permute-start(bf16[40,4096]{1,0:T(8,128)(2,1)S(1)} %get-tuple-element.97), channel_id=1, source_target_pairs={{0,4},{2,6},{4,0},{6,2},{8,12},{10,14},{12,8},{14,10},{16,20},{18,... | collective-permute-start | bytes 983048 | tf_op jit(solution)/shard_map/ppermute | solution.py:200
  69.6 17.0 %collective-permute-start.29 = (bf16[40,4096]{1,0:T(8,128)(2,1)S(1)}, bf16[40,4096]{1,0:T(8,128)(2,1)S(1)}, u32[]{:S(2)}, u32[]{:S(2)}) collective-permute-start(bf16[40,4096]{1,0:T(8,128)(2,1)S(1)} %get-tuple-element.98), channel_id=1, source_target_pairs={{0,6},{2,4},{4,2},{6,0},{8,14},{10,12},{12,10},{14,8},{16,22},{18,... | collective-permute-start | bytes 983048 | tf_op jit(solution)/shard_map/ppermute | solution.py:200
  72.8 21.9 %collective-permute-start.18 = (bf16[40,4224]{1,0:T(8,128)(2,1)S(1)}, bf16[40,4224]{1,0:T(8,128)(2,1)S(1)}, u32[]{:S(2)}, u32[]{:S(2)}) collective-permute-start(bf16[40,4224]{1,0:T(8,128)(2,1)S(1)} %get-tuple-element.75), channel_id=1, source_target_pairs={{0,2},{2,0},{4,6},{6,4},{8,10},{10,8},{12,14},{14,12},{16,18},{18,... | collective-permute-start | bytes 1013768 | tf_op jit(solution)/shard_map/ppermute | solution.py:200
  74.4 24.3 %collective-permute-start.19 = (bf16[40,4224]{1,0:T(8,128)(2,1)S(1)}, bf16[40,4224]{1,0:T(8,128)(2,1)S(1)}, u32[]{:S(2)}, u32[]{:S(2)}) collective-permute-start(bf16[40,4224]{1,0:T(8,128)(2,1)S(1)} %get-tuple-element.76), channel_id=1, source_target_pairs={{0,4},{2,6},{4,0},{6,2},{8,12},{10,14},{12,8},{14,10},{16,20},{18,... | collective-permute-start | bytes 1013768 | tf_op jit(solution)/shard_map/ppermute | solution.py:200
  78.3 22.3 %collective-permute-start.20 = (bf16[40,4224]{1,0:T(8,128)(2,1)S(1)}, bf16[40,4224]{1,0:T(8,128)(2,1)S(1)}, u32[]{:S(2)}, u32[]{:S(2)}) collective-permute-start(bf16[40,4224]{1,0:T(8,128)(2,1)S(1)} %get-tuple-element.77), channel_id=1, source_target_pairs={{0,6},{2,4},{4,2},{6,0},{8,14},{10,12},{12,10},{14,8},{16,22},{18,... | collective-permute-start | bytes 1013768 | tf_op jit(solution)/shard_map/ppermute | solution.py:200
  88.2 23.8 %collective-permute-start.30 = (bf16[64,4096]{1,0:T(8,128)(2,1)S(1)}, bf16[64,4096]{1,0:T(8,128)(2,1)S(1)}, u32[]{:S(2)}, u32[]{:S(2)}) collective-permute-start(bf16[64,4096]{1,0:T(8,128)(2,1)S(1)} %shard_map.75), channel_id=1, source_target_pairs={{0,8},{2,10},{4,12},{6,14},{8,16},{10,18},{12,20},{14,22},{16,24},... | collective-permute-start | bytes 1572872 | tf_op jit(solution)/shard_map/ppermute | solution.py:196
  94.1 12.8 %collective-permute-start.24 = (bf16[40,4096]{1,0:T(8,128)(2,1)S(1)}, bf16[40,4096]{1,0:T(8,128)(2,1)S(1)}, u32[]{:S(2)}, u32[]{:S(2)}) collective-permute-start(bf16[40,4096]{1,0:T(8,128)(2,1)S(1)} %get-tuple-element.93), channel_id=1, source_target_pairs={{0,2},{2,0},{4,6},{6,4},{8,10},{10,8},{12,14},{14,12},{16,18},{18,... | collective-permute-start | bytes 983048 | tf_op jit(solution)/shard_map/ppermute | solution.py:200
  94.7 17.3 %collective-permute-start.25 = (bf16[40,4096]{1,0:T(8,128)(2,1)S(1)}, bf16[40,4096]{1,0:T(8,128)(2,1)S(1)}, u32[]{:S(2)}, u32[]{:S(2)}) collective-permute-start(bf16[40,4096]{1,0:T(8,128)(2,1)S(1)} %get-tuple-element.94), channel_id=1, source_target_pairs={{0,4},{2,6},{4,0},{6,2},{8,12},{10,14},{12,8},{14,10},{16,20},{18,... | collective-permute-start | bytes 983048 | tf_op jit(solution)/shard_map/ppermute | solution.py:200
  98.7 13.3 %collective-permute-start.26 = (bf16[40,4096]{1,0:T(8,128)(2,1)S(1)}, bf16[40,4096]{1,0:T(8,128)(2,1)S(1)}, u32[]{:S(2)}, u32[]{:S(2)}) collective-permute-start(bf16[40,4096]{1,0:T(8,128)(2,1)S(1)} %get-tuple-element.95), channel_id=1, source_target_pairs={{0,6},{2,4},{4,2},{6,0},{8,14},{10,12},{12,10},{14,8},{16,22},{18,... | collective-permute-start | bytes 983048 | tf_op jit(solution)/shard_map/ppermute | solution.py:200
  113.6 19.4 %collective-permute-start.31 = (bf16[64,4096]{1,0:T(8,128)(2,1)S(1)}, bf16[64,4096]{1,0:T(8,128)(2,1)S(1)}, u32[]{:S(2)}, u32[]{:S(2)}) collective-permute-start(bf16[64,4096]{1,0:T(8,128)(2,1)S(1)} %shard_map.76), channel_id=1, source_target_pairs={{0,8},{2,10},{4,12},{6,14},{8,16},{10,18},{12,20},{14,22},{16,24},... | collective-permute-start | bytes 1572872 | tf_op jit(solution)/shard_map/ppermute | solution.py:196
  119.3 9.8 %collective-permute-start.21 = (bf16[40,4096]{1,0:T(8,128)(2,1)S(1)}, bf16[40,4096]{1,0:T(8,128)(2,1)S(1)}, u32[]{:S(2)}, u32[]{:S(2)}) collective-permute-start(bf16[40,4096]{1,0:T(8,128)(2,1)S(1)} %get-tuple-element.90), channel_id=1, source_target_pairs={{0,2},{2,0},{4,6},{6,4},{8,10},{10,8},{12,14},{14,12},{16,18},{18,... | collective-permute-start | bytes 983048 | tf_op jit(solution)/shard_map/ppermute | solution.py:200
  120.1 12.9 %collective-permute-start.22 = (bf16[40,4096]{1,0:T(8,128)(2,1)S(1)}, bf16[40,4096]{1,0:T(8,128)(2,1)S(1)}, u32[]{:S(2)}, u32[]{:S(2)}) collective-permute-start(bf16[40,4096]{1,0:T(8,128)(2,1)S(1)} %get-tuple-element.91), channel_id=1, source_target_pairs={{0,4},{2,6},{4,0},{6,2},{8,12},{10,14},{12,8},{14,10},{16,20},{18,... | collective-permute-start | bytes 983048 | tf_op jit(solution)/shard_map/ppermute | solution.py:200
  121.2 11.8 %collective-permute-start.23 = (bf16[40,4096]{1,0:T(8,128)(2,1)S(1)}, bf16[40,4096]{1,0:T(8,128)(2,1)S(1)}, u32[]{:S(2)}, u32[]{:S(2)}) collective-permute-start(bf16[40,4096]{1,0:T(8,128)(2,1)S(1)} %get-tuple-element.92), channel_id=1, source_target_pairs={{0,6},{2,4},{4,2},{6,0},{8,14},{10,12},{12,10},{14,8},{16,22},{18,... | collective-permute-start | bytes 983048 | tf_op jit(solution)/shard_map/ppermute | solution.py:200
  134.6 16.2 %collective-permute-start.32 = (bf16[64,4096]{1,0:T(8,128)(2,1)S(1)}, bf16[64,4096]{1,0:T(8,128)(2,1)S(1)}, u32[]{:S(2)}, u32[]{:S(2)}) collective-permute-start(bf16[64,4096]{1,0:T(8,128)(2,1)S(1)} %shard_map.77), channel_id=1, source_target_pairs={{0,8},{2,10},{4,12},{6,14},{8,16},{10,18},{12,20},{14,22},{16,24},... | collective-permute-start | bytes 1572872 | tf_op jit(solution)/shard_map/ppermute | solution.py:196
  139.4 11.4 %collective-permute-start.8 = (bf16[40,4096]{1,0:T(8,128)(2,1)S(1)}, bf16[40,4096]{1,0:T(8,128)(2,1)S(1)}, u32[]{:S(2)}, u32[]{:S(2)}) collective-permute-start(bf16[40,4096]{1,0:T(8,128)(2,1)S(1)} %get-tuple-element.65), channel_id=1, source_target_pairs={{0,4},{2,6},{4,0},{6,2},{8,12},{10,14},{12,8},{14,10},{16,20},{18,... | collective-permute-start | bytes 983048 | tf_op jit(solution)/shard_map/ppermute | solution.py:200
  139.9 10.9 %collective-permute-start.9 = (bf16[40,4096]{1,0:T(8,128)(2,1)S(1)}, bf16[40,4096]{1,0:T(8,128)(2,1)S(1)}, u32[]{:S(2)}, u32[]{:S(2)}) collective-permute-start(bf16[40,4096]{1,0:T(8,128)(2,1)S(1)} %get-tuple-element.66), channel_id=1, source_target_pairs={{0,6},{2,4},{4,2},{6,0},{8,14},{10,12},{12,10},{14,8},{16,22},{18,... | collective-permute-start | bytes 983048 | tf_op jit(solution)/shard_map/ppermute | solution.py:200
  (5 other events, 14.8 us)

commit v5 on v4

--- a/solution.py
+++ b/solution.py
@@ -23,14 +23,18 @@
     return jnp.sum(named_by(meta, expert, top) * parts, axis=1, keepdims=True)
 
 
-def one_hot(meta, expert, top, slots):
+def one_hot(meta, experts_ref, top, slots):
     rows = meta.shape[0]
-    named = jnp.sum(named_by(meta, expert, top), axis=1, keepdims=True)
+    ids = meta[:, :top].astype(F32)
+    column = lax.broadcasted_iota(jnp.int32, (rows, 3 * slots), 1)
+    part = (column >= slots).astype(jnp.int32) + (column >= 2 * slots).astype(jnp.int32)
+    expert = jnp.where(part == 0, experts_ref[1], jnp.where(part == 1, experts_ref[2], experts_ref[3])).astype(F32)
+    named = jnp.zeros((rows, 3 * slots), F32)
+    for k in range(top):
+        named = named + (ids[:, k : k + 1] == expert).astype(F32)
     below = lax.broadcasted_iota(jnp.int32, (rows, rows), 0) > lax.broadcasted_iota(jnp.int32, (rows, rows), 1)
-    wide = jnp.broadcast_to(named, (rows, slots)).astype(BF)
-    rank = jnp.dot(below.astype(F32).astype(BF), wide, preferred_element_type=F32)
-    slot = lax.broadcasted_iota(jnp.int32, (rows, slots), 1).astype(F32)
-    hit = jnp.logical_and(rank == slot, named > 0.5)
+    rank = jnp.dot(below.astype(F32).astype(BF), named.astype(BF), preferred_element_type=F32)
+    hit = jnp.logical_and(rank == (column - part * slots).astype(F32), named > 0.5)
     return hit.astype(F32).astype(BF)
 
 
@@ -40,10 +44,10 @@
 
 def select_kernel(top, slots, experts_ref, z_ref, *out_refs):
     width = z_ref.shape[1] - META
+    pick = one_hot(z_ref[:, width:], experts_ref, top, slots)
+    rows = lax.dot_general(pick, z_ref[...], (((0,), (0,)), ((), ())), preferred_element_type=F32)
     for i, out_ref in enumerate(out_refs):
-        pick = one_hot(z_ref[:, width:], experts_ref[1 + i], top, slots)
-        rows = lax.dot_general(pick, z_ref[...], (((0,), (0,)), ((), ())), preferred_element_type=F32)
-        out_ref[...] = rows.astype(BF)
+        out_ref[...] = rows[i * slots : (i + 1) * slots].astype(BF)
 
 
 def select(experts, z, top, slots):
@@ -64,8 +68,8 @@
     middle = (weights - high).astype(BF).astype(F32)
     low = weights - high - middle
     rows, width = tokens_ref.shape
-    rest = jnp.zeros((rows, META - 4 * weights.shape[1]), F32)
-    meta = jnp.concatenate([ids_ref[...].astype(F32), high, middle, low, rest], axis=1)
+    rest = jnp.zeros((META - 4 * weights.shape[0], rows), F32)
+    meta = jnp.concatenate([ids_ref[...].astype(F32), high, middle, low, rest], axis=0).T
     out_ref[:, :width] = tokens_ref[...]
     out_ref[:, width:] = meta.astype(BF)
 
@@ -79,7 +83,7 @@
         out_specs=pl.BlockSpec(memory_space=pltpu.VMEM),
         compiler_params=pltpu.CompilerParams(vmem_limit_bytes=12 << 20),
         cost_estimate=pl.CostEstimate(flops=rows, bytes_accessed=4 * rows * width, transcendentals=0),
-    )(ids, weights, tokens)
+    )(ids.T, weights.T, tokens)
 
 
 def stage_kernel(gate_ref, up_ref, down_ref, joined_ref, held_ref, sems):
@@ -156,10 +160,9 @@
 def put_back_kernel(top, slots, n_more, experts_ref, own_ref, block_ref, *refs):
     got, more, out_ref = refs[:3], refs[3 : 3 + n_more], refs[3 + n_more]
     width = own_ref.shape[1]
-    total = own_ref[...].astype(F32)
-    for i, ref in enumerate(got):
-        place = one_hot(block_ref[:, width:], experts_ref[1 + i], top, slots)
-        total = total + jnp.dot(place, ref[...], preferred_element_type=F32)
+    place = one_hot(block_ref[:, width:], experts_ref, top, slots)
+    rows = jnp.concatenate([ref[...] for ref in got], axis=0)
+    total = own_ref[...].astype(F32) + jnp.dot(place, rows, preferred_element_type=F32)
     for ref in more:
         total = total + ref[...].astype(F32)
     out_ref[...] = total.astype(BF)

time: 154 us -> 152 us (0.987)
  Pallas kernels: 36.5 us -> 33 us
    pallas_call x4, Pallas kernels: 7.1 us -> 5.18 us  [put_back(): pl.pallas_call(functools.partial(put_back_kernel, top, slots, len(more)),...]
    pallas_call x4, Pallas kernels: 6.59 us -> 4.99 us  [select(): pl.pallas_call(functools.partial(select_kernel, top, slots), out_shape=[j...]
    unnamed x10 -> x12, local copies, waits for them, and re-layouts: 8.25 us -> 8.08 us
  transfers between devices with their start and end apart: 33 -> 33, of which waited for: 15 -> 15; matrix products, arithmetic and copies ran while one was open for 0% -> 0% of each run, Pallas kernels for 20% -> 19%
where the time goes in v5:
time: 152 us; the launch traced here: 150 us
  waiting for transfers between devices  72.2 us (48%)
  starting transfers between devices  36.8 us (24%)
  Pallas kernels  33 us (22%)
  local copies, waits for them, and re-layouts  8.08 us (5%)
    ppermute x24, waiting for transfers between devices, spread(): lax.ppermute(x, 'ep', [(i, i ^ flip) for i in range(n_ep)])  70 us
    ppermute x24, starting transfers between devices, spread(): lax.ppermute(x, 'ep', [(i, i ^ flip) for i in range(n_ep)])  27.3 us
    pallas_call x4, Pallas kernels, run_expert(): pl.pallas_call(functools.partial(expert_kernel, top, pitch), out_shape=[j...  21 us
    ppermute x6, starting transfers between devices, hop_z(): return lax.ppermute(x, 'ep', [(i, (i + 4) % n_ep) for i in range(n_ep)])  8.94 us
    unnamed x12, local copies, waits for them, and re-layouts  8.08 us
    pallas_call x4, Pallas kernels, put_back(): pl.pallas_call(functools.partial(put_back_kernel, top, slots, len(more)),...  5.18 us
    pallas_call x4, Pallas kernels, select(): pl.pallas_call(functools.partial(select_kernel, top, slots), out_shape=[j...  4.99 us
  transfers between devices with their start and end apart: 33, of which 15 were waited for; matrix products, arithmetic and copies ran while one was open for 0% of the time, Pallas kernels for 19%

profile of v5, /device:TPU:14, one launch (start us, length us, event | category | flops | bytes accessed | tf_op | source)
XLA Modules:
  0.0 150.3 jit_solution(2514791774666327120)
XLA Ops:
  2.5 1.6 %collective-permute-start.3 = (bf16[64,4224]{1,0:T(8,128)(2,1)S(1)}, bf16[64,4224]{1,0:T(8,128)(2,1)S(1)}, u32[]{:S(2)}, u32[]{:S(2)}) collective-permute-start(bf16[64,4224]{1,0:T(8,128)(2,1)S(1)} %shard_map.64.z_ref.refs_0_.block_ref), channel_id=1, source_target_pairs={{0,8},{2,10},{4,12},{6,14},{8,16},{10,18},{12,20},{14,22},{16,24},... | collective-permute-start | bytes 1622024 | tf_op jit(solution)/shard_map/ppermute | solution.py:199
  6.6 2.4 %collective-permute-start.2 = (bf16[40,4224]{1,0:T(8,128)(2,1)S(1)}, bf16[40,4224]{1,0:T(8,128)(2,1)S(1)}, u32[]{:S(2)}, u32[]{:S(2)}) collective-permute-start(bf16[40,4224]{1,0:T(8,128)(2,1)S(1)} %get-tuple-element.54), channel_id=1, source_target_pairs={{0,6},{2,4},{4,2},{6,0},{8,14},{10,12},{12,10},{14,8},{16,22},{18,... | collective-permute-start | bytes 1013768 | tf_op jit(solution)/shard_map/ppermute | solution.py:203
  9.0 7.4 %collective-permute-done.refs_1_ = bf16[40,4224]{1,0:T(8,128)(2,1)S(1)} collective-permute-done((bf16[40,4224]{1,0:T(8,128)(2,1)S(1)}, bf16[40,4224]{1,0:T(8,128)(2,1)S(1)}, u32[]{:S(2)}, u32[]{:S(2)}) %collective-permute-start) | collective-permute-done | bytes 337952 | tf_op jit(solution)/shard_map/ppermute | solution.py:203
  16.4 6.0 %collective-permute-done.1.refs_2_ = bf16[40,4224]{1,0:T(8,128)(2,1)S(1)} collective-permute-done((bf16[40,4224]{1,0:T(8,128)(2,1)S(1)}, bf16[40,4224]{1,0:T(8,128)(2,1)S(1)}, u32[]{:S(2)}, u32[]{:S(2)}) %collective-permute-start.1) | collective-permute-done | bytes 337952 | tf_op jit(solution)/shard_map/ppermute | solution.py:203
  24.3 1.6 %collective-permute-start.11 = (bf16[40,4224]{1,0:T(8,128)(2,1)S(1)}, bf16[40,4224]{1,0:T(8,128)(2,1)S(1)}, u32[]{:S(2)}, u32[]{:S(2)}) collective-permute-start(bf16[40,4224]{1,0:T(8,128)(2,1)S(1)} %get-tuple-element.67), channel_id=1, source_target_pairs={{0,2},{2,0},{4,6},{6,4},{8,10},{10,8},{12,14},{14,12},{16,18},{18,... | collective-permute-start | bytes 1013768 | tf_op jit(solution)/shard_map/ppermute | solution.py:203
  26.3 8.3 %collective-permute-done.11.refs_1_ = bf16[40,4224]{1,0:T(8,128)(2,1)S(1)} collective-permute-done((bf16[40,4224]{1,0:T(8,128)(2,1)S(1)}, bf16[40,4224]{1,0:T(8,128)(2,1)S(1)}, u32[]{:S(2)}, u32[]{:S(2)}) %collective-permute-start.11) | collective-permute-done | bytes 337952 | tf_op jit(solution)/shard_map/ppermute | solution.py:203
  34.6 1.6 %collective-permute-start.10 = (bf16[64,4224]{1,0:T(8,128)(2,1)S(1)}, bf16[64,4224]{1,0:T(8,128)(2,1)S(1)}, u32[]{:S(2)}, u32[]{:S(2)}) collective-permute-start(bf16[64,4224]{1,0:T(8,128)(2,1)S(1)} %collective-permute-done.3.z_ref.refs_0_.block_ref), channel_id=1, source_target_pairs={{0,8},{2,10},{4,12},{6,14},{8,16},{10,18},{12,20},{14,22},{16,24},... | collective-permute-start | bytes 1622024 | tf_op jit(solution)/shard_map/ppermute | solution.py:199
  37.6 1.9 %copy-done = bf16[1,4096,384]{2,1,0:T(8,128)(2,1)S(1)} copy-done((bf16[1,4096,384]{2,1,0:T(8,128)(2,1)S(1)}, bf16[1,4096,384]{2,1,0:T(8,128)(2,1)}, u32[]{:S(2)}) %copy-start) | copy-done | bytes 3145752
  39.5 1.9 %copy-done.1 = bf16[1,4096,384]{2,1,0:T(8,128)(2,1)S(1)} copy-done((bf16[1,4096,384]{2,1,0:T(8,128)(2,1)S(1)}, bf16[1,4096,384]{2,1,0:T(8,128)(2,1)}, u32[]{:S(2)}) %copy-start.1) | copy-done | bytes 3145752
  41.4 1.9 %copy-done.2 = bf16[1,384,4096]{2,1,0:T(8,128)(2,1)S(1)} copy-done((bf16[1,384,4096]{2,1,0:T(8,128)(2,1)S(1)}, bf16[1,384,4096]{2,1,0:T(8,128)(2,1)}, u32[]{:S(2)}) %copy-start.2) | copy-done | bytes 3145752
  44.2 2.1 %collective-permute-done.13.refs_3_ = bf16[40,4224]{1,0:T(8,128)(2,1)S(1)} collective-permute-done((bf16[40,4224]{1,0:T(8,128)(2,1)S(1)}, bf16[40,4224]{1,0:T(8,128)(2,1)S(1)}, u32[]{:S(2)}, u32[]{:S(2)}) %collective-permute-start.13) | collective-permute-done | bytes 337952 | tf_op jit(solution)/shard_map/ppermute | solution.py:203
  46.3 2.1 %collective-permute-done.10.z_ref.refs_0_.block_ref = bf16[64,4224]{1,0:T(8,128)(2,1)S(1)} collective-permute-done((bf16[64,4224]{1,0:T(8,128)(2,1)S(1)}, bf16[64,4224]{1,0:T(8,128)(2,1)S(1)}, u32[]{:S(2)}, u32[]{:S(2)}) %collective-permute-start.10) | collective-permute-done | bytes 540704 | tf_op jit(solution)/shard_map/ppermute | solution.py:199
  48.4 1.6 %collective-permute-start.14 = (bf16[64,4224]{1,0:T(8,128)(2,1)S(1)}, bf16[64,4224]{1,0:T(8,128)(2,1)S(1)}, u32[]{:S(2)}, u32[]{:S(2)}) collective-permute-start(bf16[64,4224]{1,0:T(8,128)(2,1)S(1)} %collective-permute-done.10.z_ref.refs_0_.block_ref), channel_id=1, source_target_pairs={{0,8},{2,10},{4,12},{6,14},{8,16},{10,18},{12,20},{14,22},{16,24},... | collective-permute-start | bytes 1622024 | tf_op jit(solution)/shard_map/ppermute | solution.py:199
  55.7 5.2 %shard_map.68 = (bf16[64,4096]{1,0:T(8,128)(2,1)S(1)}, bf16[40,4096]{1,0:T(8,128)(2,1)S(1)}, bf16[40,4096]{1,0:T(8,128)(2,1)S(1)}, bf16[40,4096]{1,0:T(8,128)(2,1)S(1)}) custom-call(s32[4]{0:T(128)S(1)} %pad_add_fusion.experts_ref, bf16[64,4224]{1,0:T(8,128)(2,1)S(1)} %shard_map.64.z_ref.refs_0_.block_ref, ...), custom_call_target="tpu_custom_call" | custom-call | flops 3925868544 | bytes 3407872 | tf_op jit(solution)/shard_map/pallas_call | solution.py:147
  61.0 5.3 %shard_map.72 = (bf16[64,4096]{1,0:T(8,128)(2,1)S(1)}, bf16[40,4096]{1,0:T(8,128)(2,1)S(1)}, bf16[40,4096]{1,0:T(8,128)(2,1)S(1)}, bf16[40,4096]{1,0:T(8,128)(2,1)S(1)}) custom-call(s32[4]{0:T(128)S(1)} %pad_add_fusion.experts_ref, bf16[64,4224]{1,0:T(8,128)(2,1)S(1)} %collective-permute-done.3.z_ref.refs_0_.block_ref, ...), custom_call_target="tpu_custom_call" | custom-call | flops 3925868544 | bytes 3407872 | tf_op jit(solution)/shard_map/pallas_call | solution.py:147
  66.2 1.6 %collective-permute-start.27 = (bf16[40,4096]{1,0:T(8,128)(2,1)S(1)}, bf16[40,4096]{1,0:T(8,128)(2,1)S(1)}, u32[]{:S(2)}, u32[]{:S(2)}) collective-permute-start(bf16[40,4096]{1,0:T(8,128)(2,1)S(1)} %get-tuple-element.96), channel_id=1, source_target_pairs={{0,2},{2,0},{4,6},{6,4},{8,10},{10,8},{12,14},{14,12},{16,18},{18,... | collective-permute-start | bytes 983048 | tf_op jit(solution)/shard_map/ppermute | solution.py:203
  71.1 1.6 %collective-permute-start.18 = (bf16[40,4224]{1,0:T(8,128)(2,1)S(1)}, bf16[40,4224]{1,0:T(8,128)(2,1)S(1)}, u32[]{:S(2)}, u32[]{:S(2)}) collective-permute-start(bf16[40,4224]{1,0:T(8,128)(2,1)S(1)} %get-tuple-element.75), channel_id=1, source_target_pairs={{0,2},{2,0},{4,6},{6,4},{8,10},{10,8},{12,14},{14,12},{16,18},{18,... | collective-permute-start | bytes 1013768 | tf_op jit(solution)/shard_map/ppermute | solution.py:203
  73.1 3.8 %collective-permute-done.27.refs_0_ = bf16[40,4096]{1,0:T(8,128)(2,1)S(1)} collective-permute-done((bf16[40,4096]{1,0:T(8,128)(2,1)S(1)}, bf16[40,4096]{1,0:T(8,128)(2,1)S(1)}, u32[]{:S(2)}, u32[]{:S(2)}) %collective-permute-start.27) | collective-permute-done | bytes 327712 | tf_op jit(solution)/shard_map/ppermute | solution.py:203
  78.4 7.1 %collective-permute-done.28.refs_1_ = bf16[40,4096]{1,0:T(8,128)(2,1)S(1)} collective-permute-done((bf16[40,4096]{1,0:T(8,128)(2,1)S(1)}, bf16[40,4096]{1,0:T(8,128)(2,1)S(1)}, u32[]{:S(2)}, u32[]{:S(2)}) %collective-permute-start.28) | collective-permute-done | bytes 327712 | tf_op jit(solution)/shard_map/ppermute | solution.py:203
  87.1 5.2 %shard_map.73 = (bf16[64,4096]{1,0:T(8,128)(2,1)S(1)}, bf16[40,4096]{1,0:T(8,128)(2,1)S(1)}, bf16[40,4096]{1,0:T(8,128)(2,1)S(1)}, bf16[40,4096]{1,0:T(8,128)(2,1)S(1)}) custom-call(s32[4]{0:T(128)S(1)} %pad_add_fusion.experts_ref, bf16[64,4224]{1,0:T(8,128)(2,1)S(1)} %collective-permute-done.10.z_ref.refs_0_.block_ref, ...), custom_call_target="tpu_custom_call" | custom-call | flops 3925868544 | bytes 3407872 | tf_op jit(solution)/shard_map/pallas_call | solution.py:147
  94.2 3.7 %collective-permute-done.19.refs_2_ = bf16[40,4224]{1,0:T(8,128)(2,1)S(1)} collective-permute-done((bf16[40,4224]{1,0:T(8,128)(2,1)S(1)}, bf16[40,4224]{1,0:T(8,128)(2,1)S(1)}, u32[]{:S(2)}, u32[]{:S(2)}) %collective-permute-start.19) | collective-permute-done | bytes 337952 | tf_op jit(solution)/shard_map/ppermute | solution.py:203
  99.3 6.3 %collective-permute-done.24.refs_0_ = bf16[40,4096]{1,0:T(8,128)(2,1)S(1)} collective-permute-done((bf16[40,4096]{1,0:T(8,128)(2,1)S(1)}, bf16[40,4096]{1,0:T(8,128)(2,1)S(1)}, u32[]{:S(2)}, u32[]{:S(2)}) %collective-permute-start.24) | collective-permute-done | bytes 327712 | tf_op jit(solution)/shard_map/ppermute | solution.py:203
  105.6 5.1 %collective-permute-done.25.refs_1_ = bf16[40,4096]{1,0:T(8,128)(2,1)S(1)} collective-permute-done((bf16[40,4096]{1,0:T(8,128)(2,1)S(1)}, bf16[40,4096]{1,0:T(8,128)(2,1)S(1)}, u32[]{:S(2)}, u32[]{:S(2)}) %collective-permute-start.25) | collective-permute-done | bytes 327712 | tf_op jit(solution)/shard_map/ppermute | solution.py:203
  112.1 5.3 %shard_map.74 = (bf16[64,4096]{1,0:T(8,128)(2,1)S(1)}, bf16[40,4096]{1,0:T(8,128)(2,1)S(1)}, bf16[40,4096]{1,0:T(8,128)(2,1)S(1)}, bf16[40,4096]{1,0:T(8,128)(2,1)S(1)}) custom-call(s32[4]{0:T(128)S(1)} %pad_add_fusion.experts_ref, bf16[64,4224]{1,0:T(8,128)(2,1)S(1)} %collective-permute-done.14.z_ref.refs_0_.block_ref, ...), custom_call_target="tpu_custom_call" | custom-call | flops 3925868544 | bytes 3407872 | tf_op jit(solution)/shard_map/pallas_call | solution.py:147
  119.4 1.6 %collective-permute-start.23 = (bf16[40,4096]{1,0:T(8,128)(2,1)S(1)}, bf16[40,4096]{1,0:T(8,128)(2,1)S(1)}, u32[]{:S(2)}, u32[]{:S(2)}) collective-permute-start(bf16[40,4096]{1,0:T(8,128)(2,1)S(1)} %get-tuple-element.92), channel_id=1, source_target_pairs={{0,6},{2,4},{4,2},{6,0},{8,14},{10,12},{12,10},{14,8},{16,22},{18,... | collective-permute-start | bytes 983048 | tf_op jit(solution)/shard_map/ppermute | solution.py:203
  121.0 6.4 %collective-permute-done.21.refs_0_ = bf16[40,4096]{1,0:T(8,128)(2,1)S(1)} collective-permute-done((bf16[40,4096]{1,0:T(8,128)(2,1)S(1)}, bf16[40,4096]{1,0:T(8,128)(2,1)S(1)}, u32[]{:S(2)}, u32[]{:S(2)}) %collective-permute-start.21) | collective-permute-done | bytes 327712 | tf_op jit(solution)/shard_map/ppermute | solution.py:203
  127.3 3.9 %collective-permute-done.22.refs_1_ = bf16[40,4096]{1,0:T(8,128)(2,1)S(1)} collective-permute-done((bf16[40,4096]{1,0:T(8,128)(2,1)S(1)}, bf16[40,4096]{1,0:T(8,128)(2,1)S(1)}, u32[]{:S(2)}, u32[]{:S(2)}) %collective-permute-start.22) | collective-permute-done | bytes 327712 | tf_op jit(solution)/shard_map/ppermute | solution.py:203
  132.3 3.2 %collective-permute-start.32 = (bf16[64,4096]{1,0:T(8,128)(2,1)S(1)}, bf16[64,4096]{1,0:T(8,128)(2,1)S(1)}, u32[]{:S(2)}, u32[]{:S(2)}) collective-permute-start(bf16[64,4096]{1,0:T(8,128)(2,1)S(1)} %shard_map.77), channel_id=1, source_target_pairs={{0,8},{2,10},{4,12},{6,14},{8,16},{10,18},{12,20},{14,22},{16,24},... | collective-permute-start | bytes 1572872 | tf_op jit(solution)/shard_map/ppermute | solution.py:199
  135.5 1.6 %collective-permute-start.7 = (bf16[40,4096]{1,0:T(8,128)(2,1)S(1)}, bf16[40,4096]{1,0:T(8,128)(2,1)S(1)}, u32[]{:S(2)}, u32[]{:S(2)}) collective-permute-start(bf16[40,4096]{1,0:T(8,128)(2,1)S(1)} %get-tuple-element.64), channel_id=1, source_target_pairs={{0,2},{2,0},{4,6},{6,4},{8,10},{10,8},{12,14},{14,12},{16,18},{18,... | collective-permute-start | bytes 983048 | tf_op jit(solution)/shard_map/ppermute | solution.py:203
  139.0 4.7 %collective-permute-done.7.refs_0_ = bf16[40,4096]{1,0:T(8,128)(2,1)S(1)} collective-permute-done((bf16[40,4096]{1,0:T(8,128)(2,1)S(1)}, bf16[40,4096]{1,0:T(8,128)(2,1)S(1)}, u32[]{:S(2)}, u32[]{:S(2)}) %collective-permute-start.7) | collective-permute-done | bytes 327712 | tf_op jit(solution)/shard_map/ppermute | solution.py:203
  143.7 4.7 %collective-permute-done.8.refs_1_ = bf16[40,4096]{1,0:T(8,128)(2,1)S(1)} collective-permute-done((bf16[40,4096]{1,0:T(8,128)(2,1)S(1)}, bf16[40,4096]{1,0:T(8,128)(2,1)S(1)}, u32[]{:S(2)}, u32[]{:S(2)}) %collective-permute-start.8) | collective-permute-done | bytes 327712 | tf_op jit(solution)/shard_map/ppermute | solution.py:203
  148.4 1.9 %shard_map.78 = bf16[64,4096]{1,0:T(8,128)(2,1)} custom-call(s32[4]{0:T(128)S(1)} %pad_add_fusion.experts_ref, bf16[64,4096]{1,0:T(8,128)(2,1)S(1)} %get-tuple-element.63.own_ref, bf16[64,4224]{1,0:T(8,128)(2,1)S(1)} %shard_map.64.z_ref.refs_0_.block_ref, bf16[40,4096]{1,0:T(8,128)(2,1)S(1)} %collective-permute-done.7.refs_0_, ...), custom_call_target="tpu_custom_call" | custom-call | flops 62914560 | bytes 2621440 | tf_op jit(solution)/shard_map/pallas_call | solution.py:174
  (62 shorter events, 31.8 us)
Async XLA Ops:
  2.5 19.9 %collective-permute-start.3 = (bf16[64,4224]{1,0:T(8,128)(2,1)S(1)}, bf16[64,4224]{1,0:T(8,128)(2,1)S(1)}, u32[]{:S(2)}, u32[]{:S(2)}) collective-permute-start(bf16[64,4224]{1,0:T(8,128)(2,1)S(1)} %shard_map.64.z_ref.refs_0_.block_ref), channel_id=1, source_target_pairs={{0,8},{2,10},{4,12},{6,14},{8,16},{10,18},{12,20},{14,22},{16,24},... | collective-permute-start | bytes 1622024 | tf_op jit(solution)/shard_map/ppermute | solution.py:199
  5.5 10.9 %collective-permute-start = (bf16[40,4224]{1,0:T(8,128)(2,1)S(1)}, bf16[40,4224]{1,0:T(8,128)(2,1)S(1)}, u32[]{:S(2)}, u32[]{:S(2)}) collective-permute-start(bf16[40,4224]{1,0:T(8,128)(2,1)S(1)} %get-tuple-element.52), channel_id=1, source_target_pairs={{0,2},{2,0},{4,6},{6,4},{8,10},{10,8},{12,14},{14,12},{16,18},{18,... | collective-permute-start | bytes 1013768 | tf_op jit(solution)/shard_map/ppermute | solution.py:203
  6.1 16.3 %collective-permute-start.1 = (bf16[40,4224]{1,0:T(8,128)(2,1)S(1)}, bf16[40,4224]{1,0:T(8,128)(2,1)S(1)}, u32[]{:S(2)}, u32[]{:S(2)}) collective-permute-start(bf16[40,4224]{1,0:T(8,128)(2,1)S(1)} %get-tuple-element.53), channel_id=1, source_target_pairs={{0,4},{2,6},{4,0},{6,2},{8,12},{10,14},{12,8},{14,10},{16,20},{18,... | collective-permute-start | bytes 1013768 | tf_op jit(solution)/shard_map/ppermute | solution.py:203
  6.6 15.8 %collective-permute-start.2 = (bf16[40,4224]{1,0:T(8,128)(2,1)S(1)}, bf16[40,4224]{1,0:T(8,128)(2,1)S(1)}, u32[]{:S(2)}, u32[]{:S(2)}) collective-permute-start(bf16[40,4224]{1,0:T(8,128)(2,1)S(1)} %get-tuple-element.54), channel_id=1, source_target_pairs={{0,6},{2,4},{4,2},{6,0},{8,14},{10,12},{12,10},{14,8},{16,22},{18,... | collective-permute-start | bytes 1013768 | tf_op jit(solution)/shard_map/ppermute | solution.py:203
  22.4 30.4 %collective-permute-start.4 = (bf16[4096,384]{1,0:T(8,128)(2,1)}, bf16[4096,384]{1,0:T(8,128)(2,1)S(1)}, u32[]{:S(2)}, u32[]{:S(2)}) collective-permute-start(bf16[4096,384]{1,0:T(8,128)(2,1)} %bitcast.9), channel_id=1, source_target_pairs={{0,1},{1,0},{2,3},{3,2},{4,5},{5,4},{6,7},{7,6},{8,9},{9,8},{10,11... | collective-permute-start | bytes 9437192 | tf_op jit(solution)/shard_map/ppermute | solution.py:196
  22.4 30.9 %collective-permute-start.5 = (bf16[4096,384]{1,0:T(8,128)(2,1)}, bf16[4096,384]{1,0:T(8,128)(2,1)S(1)}, u32[]{:S(2)}, u32[]{:S(2)}) collective-permute-start(bf16[4096,384]{1,0:T(8,128)(2,1)} %bitcast.11), channel_id=1, source_target_pairs={{0,1},{1,0},{2,3},{3,2},{4,5},{5,4},{6,7},{7,6},{8,9},{9,8},{10,11... | collective-permute-start | bytes 9437192 | tf_op jit(solution)/shard_map/ppermute | solution.py:196
  22.9 31.9 %collective-permute-start.6 = (bf16[384,4096]{1,0:T(8,128)(2,1)}, bf16[384,4096]{1,0:T(8,128)(2,1)S(1)}, u32[]{:S(2)}, u32[]{:S(2)}) collective-permute-start(bf16[384,4096]{1,0:T(8,128)(2,1)} %bitcast.13), channel_id=1, source_target_pairs={{0,1},{1,0},{2,3},{3,2},{4,5},{5,4},{6,7},{7,6},{8,9},{9,8},{10,11... | collective-permute-start | bytes 9437192 | tf_op jit(solution)/shard_map/ppermute | solution.py:196
  24.3 10.3 %collective-permute-start.11 = (bf16[40,4224]{1,0:T(8,128)(2,1)S(1)}, bf16[40,4224]{1,0:T(8,128)(2,1)S(1)}, u32[]{:S(2)}, u32[]{:S(2)}) collective-permute-start(bf16[40,4224]{1,0:T(8,128)(2,1)S(1)} %get-tuple-element.67), channel_id=1, source_target_pairs={{0,2},{2,0},{4,6},{6,4},{8,10},{10,8},{12,14},{14,12},{16,18},{18,... | collective-permute-start | bytes 1013768 | tf_op jit(solution)/shard_map/ppermute | solution.py:203
  25.8 10.4 %collective-permute-start.12 = (bf16[40,4224]{1,0:T(8,128)(2,1)S(1)}, bf16[40,4224]{1,0:T(8,128)(2,1)S(1)}, u32[]{:S(2)}, u32[]{:S(2)}) collective-permute-start(bf16[40,4224]{1,0:T(8,128)(2,1)S(1)} %get-tuple-element.68), channel_id=1, source_target_pairs={{0,4},{2,6},{4,0},{6,2},{8,12},{10,14},{12,8},{14,10},{16,20},{18,... | collective-permute-start | bytes 1013768 | tf_op jit(solution)/shard_map/ppermute | solution.py:203
  34.6 13.8 %collective-permute-start.10 = (bf16[64,4224]{1,0:T(8,128)(2,1)S(1)}, bf16[64,4224]{1,0:T(8,128)(2,1)S(1)}, u32[]{:S(2)}, u32[]{:S(2)}) collective-permute-start(bf16[64,4224]{1,0:T(8,128)(2,1)S(1)} %collective-permute-done.3.z_ref.refs_0_.block_ref), channel_id=1, source_target_pairs={{0,8},{2,10},{4,12},{6,14},{8,16},{10,18},{12,20},{14,22},{16,24},... | collective-permute-start | bytes 1622024 | tf_op jit(solution)/shard_map/ppermute | solution.py:199
  36.2 10.1 %collective-permute-start.13 = (bf16[40,4224]{1,0:T(8,128)(2,1)S(1)}, bf16[40,4224]{1,0:T(8,128)(2,1)S(1)}, u32[]{:S(2)}, u32[]{:S(2)}) collective-permute-start(bf16[40,4224]{1,0:T(8,128)(2,1)S(1)} %get-tuple-element.69), channel_id=1, source_target_pairs={{0,6},{2,4},{4,2},{6,0},{8,14},{10,12},{12,10},{14,8},{16,22},{18,... | collective-permute-start | bytes 1013768 | tf_op jit(solution)/shard_map/ppermute | solution.py:203
  48.4 21.4 %collective-permute-start.14 = (bf16[64,4224]{1,0:T(8,128)(2,1)S(1)}, bf16[64,4224]{1,0:T(8,128)(2,1)S(1)}, u32[]{:S(2)}, u32[]{:S(2)}) collective-permute-start(bf16[64,4224]{1,0:T(8,128)(2,1)S(1)} %collective-permute-done.10.z_ref.refs_0_.block_ref), channel_id=1, source_target_pairs={{0,8},{2,10},{4,12},{6,14},{8,16},{10,18},{12,20},{14,22},{16,24},... | collective-permute-start | bytes 1622024 | tf_op jit(solution)/shard_map/ppermute | solution.py:199
  51.3 16.5 %collective-permute-start.15 = (bf16[40,4224]{1,0:T(8,128)(2,1)S(1)}, bf16[40,4224]{1,0:T(8,128)(2,1)S(1)}, u32[]{:S(2)}, u32[]{:S(2)}) collective-permute-start(bf16[40,4224]{1,0:T(8,128)(2,1)S(1)} %get-tuple-element.71), channel_id=1, source_target_pairs={{0,2},{2,0},{4,6},{6,4},{8,10},{10,8},{12,14},{14,12},{16,18},{18,... | collective-permute-start | bytes 1013768 | tf_op jit(solution)/shard_map/ppermute | solution.py:203
  52.9 15.5 %collective-permute-start.16 = (bf16[40,4224]{1,0:T(8,128)(2,1)S(1)}, bf16[40,4224]{1,0:T(8,128)(2,1)S(1)}, u32[]{:S(2)}, u32[]{:S(2)}) collective-permute-start(bf16[40,4224]{1,0:T(8,128)(2,1)S(1)} %get-tuple-element.72), channel_id=1, source_target_pairs={{0,4},{2,6},{4,0},{6,2},{8,12},{10,14},{12,8},{14,10},{16,20},{18,... | collective-permute-start | bytes 1013768 | tf_op jit(solution)/shard_map/ppermute | solution.py:203
  53.4 16.4 %collective-permute-start.17 = (bf16[40,4224]{1,0:T(8,128)(2,1)S(1)}, bf16[40,4224]{1,0:T(8,128)(2,1)S(1)}, u32[]{:S(2)}, u32[]{:S(2)}) collective-permute-start(bf16[40,4224]{1,0:T(8,128)(2,1)S(1)} %get-tuple-element.73), channel_id=1, source_target_pairs={{0,6},{2,4},{4,2},{6,0},{8,14},{10,12},{12,10},{14,8},{16,22},{18,... | collective-permute-start | bytes 1013768 | tf_op jit(solution)/shard_map/ppermute | solution.py:203
  66.2 10.7 %collective-permute-start.27 = (bf16[40,4096]{1,0:T(8,128)(2,1)S(1)}, bf16[40,4096]{1,0:T(8,128)(2,1)S(1)}, u32[]{:S(2)}, u32[]{:S(2)}) collective-permute-start(bf16[40,4096]{1,0:T(8,128)(2,1)S(1)} %get-tuple-element.96), channel_id=1, source_target_pairs={{0,2},{2,0},{4,6},{6,4},{8,10},{10,8},{12,14},{14,12},{16,18},{18,... | collective-permute-start | bytes 983048 | tf_op jit(solution)/shard_map/ppermute | solution.py:203
  67.8 17.7 %collective-permute-start.28 = (bf16[40,4096]{1,0:T(8,128)(2,1)S(1)}, bf16[40,4096]{1,0:T(8,128)(2,1)S(1)}, u32[]{:S(2)}, u32[]{:S(2)}) collective-permute-start(bf16[40,4096]{1,0:T(8,128)(2,1)S(1)} %get-tuple-element.97), channel_id=1, source_target_pairs={{0,4},{2,6},{4,0},{6,2},{8,12},{10,14},{12,8},{14,10},{16,20},{18,... | collective-permute-start | bytes 983048 | tf_op jit(solution)/shard_map/ppermute | solution.py:203
  68.3 17.2 %collective-permute-start.29 = (bf16[40,4096]{1,0:T(8,128)(2,1)S(1)}, bf16[40,4096]{1,0:T(8,128)(2,1)S(1)}, u32[]{:S(2)}, u32[]{:S(2)}) collective-permute-start(bf16[40,4096]{1,0:T(8,128)(2,1)S(1)} %get-tuple-element.98), channel_id=1, source_target_pairs={{0,6},{2,4},{4,2},{6,0},{8,14},{10,12},{12,10},{14,8},{16,22},{18,... | collective-permute-start | bytes 983048 | tf_op jit(solution)/shard_map/ppermute | solution.py:203
  71.1 21.9 %collective-permute-start.18 = (bf16[40,4224]{1,0:T(8,128)(2,1)S(1)}, bf16[40,4224]{1,0:T(8,128)(2,1)S(1)}, u32[]{:S(2)}, u32[]{:S(2)}) collective-permute-start(bf16[40,4224]{1,0:T(8,128)(2,1)S(1)} %get-tuple-element.75), channel_id=1, source_target_pairs={{0,2},{2,0},{4,6},{6,4},{8,10},{10,8},{12,14},{14,12},{16,18},{18,... | collective-permute-start | bytes 1013768 | tf_op jit(solution)/shard_map/ppermute | solution.py:203
  72.6 25.3 %collective-permute-start.19 = (bf16[40,4224]{1,0:T(8,128)(2,1)S(1)}, bf16[40,4224]{1,0:T(8,128)(2,1)S(1)}, u32[]{:S(2)}, u32[]{:S(2)}) collective-permute-start(bf16[40,4224]{1,0:T(8,128)(2,1)S(1)} %get-tuple-element.76), channel_id=1, source_target_pairs={{0,4},{2,6},{4,0},{6,2},{8,12},{10,14},{12,8},{14,10},{16,20},{18,... | collective-permute-start | bytes 1013768 | tf_op jit(solution)/shard_map/ppermute | solution.py:203
  77.0 22.3 %collective-permute-start.20 = (bf16[40,4224]{1,0:T(8,128)(2,1)S(1)}, bf16[40,4224]{1,0:T(8,128)(2,1)S(1)}, u32[]{:S(2)}, u32[]{:S(2)}) collective-permute-start(bf16[40,4224]{1,0:T(8,128)(2,1)S(1)} %get-tuple-element.77), channel_id=1, source_target_pairs={{0,6},{2,4},{4,2},{6,0},{8,14},{10,12},{12,10},{14,8},{16,22},{18,... | collective-permute-start | bytes 1013768 | tf_op jit(solution)/shard_map/ppermute | solution.py:203
  86.6 24.1 %collective-permute-start.30 = (bf16[64,4096]{1,0:T(8,128)(2,1)S(1)}, bf16[64,4096]{1,0:T(8,128)(2,1)S(1)}, u32[]{:S(2)}, u32[]{:S(2)}) collective-permute-start(bf16[64,4096]{1,0:T(8,128)(2,1)S(1)} %shard_map.75), channel_id=1, source_target_pairs={{0,8},{2,10},{4,12},{6,14},{8,16},{10,18},{12,20},{14,22},{16,24},... | collective-permute-start | bytes 1572872 | tf_op jit(solution)/shard_map/ppermute | solution.py:199
  92.3 13.2 %collective-permute-start.24 = (bf16[40,4096]{1,0:T(8,128)(2,1)S(1)}, bf16[40,4096]{1,0:T(8,128)(2,1)S(1)}, u32[]{:S(2)}, u32[]{:S(2)}) collective-permute-start(bf16[40,4096]{1,0:T(8,128)(2,1)S(1)} %get-tuple-element.93), channel_id=1, source_target_pairs={{0,2},{2,0},{4,6},{6,4},{8,10},{10,8},{12,14},{14,12},{16,18},{18,... | collective-permute-start | bytes 983048 | tf_op jit(solution)/shard_map/ppermute | solution.py:203
  93.0 17.7 %collective-permute-start.25 = (bf16[40,4096]{1,0:T(8,128)(2,1)S(1)}, bf16[40,4096]{1,0:T(8,128)(2,1)S(1)}, u32[]{:S(2)}, u32[]{:S(2)}) collective-permute-start(bf16[40,4096]{1,0:T(8,128)(2,1)S(1)} %get-tuple-element.94), channel_id=1, source_target_pairs={{0,4},{2,6},{4,0},{6,2},{8,12},{10,14},{12,8},{14,10},{16,20},{18,... | collective-permute-start | bytes 983048 | tf_op jit(solution)/shard_map/ppermute | solution.py:203
  97.9 12.8 %collective-permute-start.26 = (bf16[40,4096]{1,0:T(8,128)(2,1)S(1)}, bf16[40,4096]{1,0:T(8,128)(2,1)S(1)}, u32[]{:S(2)}, u32[]{:S(2)}) collective-permute-start(bf16[40,4096]{1,0:T(8,128)(2,1)S(1)} %get-tuple-element.95), channel_id=1, source_target_pairs={{0,6},{2,4},{4,2},{6,0},{8,14},{10,12},{12,10},{14,8},{16,22},{18,... | collective-permute-start | bytes 983048 | tf_op jit(solution)/shard_map/ppermute | solution.py:203
  111.8 19.4 %collective-permute-start.31 = (bf16[64,4096]{1,0:T(8,128)(2,1)S(1)}, bf16[64,4096]{1,0:T(8,128)(2,1)S(1)}, u32[]{:S(2)}, u32[]{:S(2)}) collective-permute-start(bf16[64,4096]{1,0:T(8,128)(2,1)S(1)} %shard_map.76), channel_id=1, source_target_pairs={{0,8},{2,10},{4,12},{6,14},{8,16},{10,18},{12,20},{14,22},{16,24},... | collective-permute-start | bytes 1572872 | tf_op jit(solution)/shard_map/ppermute | solution.py:199
  117.4 9.9 %collective-permute-start.21 = (bf16[40,4096]{1,0:T(8,128)(2,1)S(1)}, bf16[40,4096]{1,0:T(8,128)(2,1)S(1)}, u32[]{:S(2)}, u32[]{:S(2)}) collective-permute-start(bf16[40,4096]{1,0:T(8,128)(2,1)S(1)} %get-tuple-element.90), channel_id=1, source_target_pairs={{0,2},{2,0},{4,6},{6,4},{8,10},{10,8},{12,14},{14,12},{16,18},{18,... | collective-permute-start | bytes 983048 | tf_op jit(solution)/shard_map/ppermute | solution.py:203
  118.2 13.0 %collective-permute-start.22 = (bf16[40,4096]{1,0:T(8,128)(2,1)S(1)}, bf16[40,4096]{1,0:T(8,128)(2,1)S(1)}, u32[]{:S(2)}, u32[]{:S(2)}) collective-permute-start(bf16[40,4096]{1,0:T(8,128)(2,1)S(1)} %get-tuple-element.91), channel_id=1, source_target_pairs={{0,4},{2,6},{4,0},{6,2},{8,12},{10,14},{12,8},{14,10},{16,20},{18,... | collective-permute-start | bytes 983048 | tf_op jit(solution)/shard_map/ppermute | solution.py:203
  119.4 11.8 %collective-permute-start.23 = (bf16[40,4096]{1,0:T(8,128)(2,1)S(1)}, bf16[40,4096]{1,0:T(8,128)(2,1)S(1)}, u32[]{:S(2)}, u32[]{:S(2)}) collective-permute-start(bf16[40,4096]{1,0:T(8,128)(2,1)S(1)} %get-tuple-element.92), channel_id=1, source_target_pairs={{0,6},{2,4},{4,2},{6,0},{8,14},{10,12},{12,10},{14,8},{16,22},{18,... | collective-permute-start | bytes 983048 | tf_op jit(solution)/shard_map/ppermute | solution.py:203
  132.3 16.1 %collective-permute-start.32 = (bf16[64,4096]{1,0:T(8,128)(2,1)S(1)}, bf16[64,4096]{1,0:T(8,128)(2,1)S(1)}, u32[]{:S(2)}, u32[]{:S(2)}) collective-permute-start(bf16[64,4096]{1,0:T(8,128)(2,1)S(1)} %shard_map.77), channel_id=1, source_target_pairs={{0,8},{2,10},{4,12},{6,14},{8,16},{10,18},{12,20},{14,22},{16,24},... | collective-permute-start | bytes 1572872 | tf_op jit(solution)/shard_map/ppermute | solution.py:199
  137.1 11.2 %collective-permute-start.8 = (bf16[40,4096]{1,0:T(8,128)(2,1)S(1)}, bf16[40,4096]{1,0:T(8,128)(2,1)S(1)}, u32[]{:S(2)}, u32[]{:S(2)}) collective-permute-start(bf16[40,4096]{1,0:T(8,128)(2,1)S(1)} %get-tuple-element.65), channel_id=1, source_target_pairs={{0,4},{2,6},{4,0},{6,2},{8,12},{10,14},{12,8},{14,10},{16,20},{18,... | collective-permute-start | bytes 983048 | tf_op jit(solution)/shard_map/ppermute | solution.py:203
  137.6 10.8 %collective-permute-start.9 = (bf16[40,4096]{1,0:T(8,128)(2,1)S(1)}, bf16[40,4096]{1,0:T(8,128)(2,1)S(1)}, u32[]{:S(2)}, u32[]{:S(2)}) collective-permute-start(bf16[40,4096]{1,0:T(8,128)(2,1)S(1)} %get-tuple-element.66), channel_id=1, source_target_pairs={{0,6},{2,4},{4,2},{6,0},{8,14},{10,12},{12,10},{14,8},{16,22},{18,... | collective-permute-start | bytes 983048 | tf_op jit(solution)/shard_map/ppermute | solution.py:203
  (7 other events, 16.2 us)
